TPU v7x, 256 devices: a whole 4x4x8 slice. The times are simulated.
256 devices in a mesh: blk: 16 (over x, y_hi, core), pair: 16 (over y_lo, z).
Axes of the slice: x: 4, y: 4 (y_hi: 2, y_lo: 2; y = y_hi * 2 + y_lo), z: 8, core: 2. Of those that a mesh axis runs over, the one named last changes fastest.
Arguments:
- users: float32 [131072, 256], P(('blk', 'pair')), may hold values from -1.5 to 1.5
- user_moments: float32 [131072, 256], P(('blk', 'pair')), may hold values from 0.0001 to 0.01
- ads: float32 [131072, 256], P(('blk', 'pair')), may hold values from -1.5 to 1.5
- ad_moments: float32 [131072, 256], P(('blk', 'pair')), may hold values from 0.0001 to 0.01
- pos_user: int32 [16, 16, 4, 512], P('blk'), may hold values from 0 to 511
- pos_ad: int32 [16, 16, 4, 512], P('blk'), may hold values from 0 to 511
- neg_ad: int32 [16, 16, 4, 2, 512], P('blk'), may hold values from 0 to 511
Outputs:
- users_out: float32 [131072, 256], P(('blk', 'pair'))
- user_moments_out: float32 [131072, 256], P(('blk', 'pair'))
- ads_out: float32 [131072, 256], P(('blk', 'pair'))
- ad_moments_out: float32 [131072, 256], P(('blk', 'pair'))
Inputs may be any that keep to these rules, and one draw needn't show every extreme that they name: `pos_user`: a row of the user partition. `pos_ad`: a row of the ad partition met. `neg_ad`: a row of the ad partition met; repeats allowed.
All inputs are finite; a program needn't handle non-finite values.
Results may differ from a plain program's by a relative error of at most 0.00017.
Values sent between devices are 32-bit elements; how exact they have to be, the bound alone decides.
No kernel may reach another device: no remote copies, remote signals or barrier semaphores. Data moves between devices by JAX's collectives and lax.ppermute only.
A program may use at most 64 MiB of HBM per device.

v0:
```python
import functools

import jax
import jax.numpy as jnp
from jax import lax
from jax.experimental import pallas as pl
from jax.experimental.pallas import tpu as pltpu
from jax.sharding import PartitionSpec as P

LEARN_RATE = 0.1
EPS = 1e-08
F32 = jnp.float32
BF16 = jnp.bfloat16
AXES = ("blk", "pair")
VMEM_LIMIT = 28 * 1024 * 1024


def dot(a, b, ca, cb):
    return lax.dot_general(a, b, (((ca,), (cb,)), ((), ())), preferred_element_type=F32)


def split(x):
    hi = x.astype(BF16)
    return hi, (x - hi.astype(F32)).astype(BF16)


def dot3(a, b, ca, cb):
    (ah, al), (bh, bl) = a, b
    return dot(ah, bh, ca, cb) + (dot(ah, bl, ca, cb) + dot(al, bh, ca, cb))


def adagrad(row, mom, grad):
    mom = mom + grad * grad
    return row - LEARN_RATE * grad / (jnp.sqrt(mom) + EPS), mom


def onehot(idx, count):
    rows = lax.broadcasted_iota(jnp.int32, (count, idx.shape[1]), 0)
    return jnp.where(rows == idx, F32(1), F32(0)).astype(BF16)


def prepare(group, pu, pa, ng, users, ads, mh_ref, cu_ref, cn_ref):
    n = ng.shape[1]
    hot_u = onehot(pu, users)
    hot_a = onehot(pa, ads)
    mh_ref[group] = (0.5 * dot(hot_u, hot_a, 1, 1)).astype(BF16)
    ones = jnp.ones((pu.shape[1], 128), BF16)
    cu_ref[group] = dot(hot_u, ones, 1, 0) * F32(0.5 / n**0.5)
    cn_ref[group] = dot(jnp.ones((8, n), BF16), onehot(ng, ads), 1, 1)


def gradient_matrix(u_hl, at_hl, mh, cu, cn):
    s = dot3(u_hl, at_hl, 1, 0)
    t = jnp.tanh(0.5 * s)
    w = jnp.concatenate([cu] * (s.shape[1] // 128), axis=1) * cn
    m = mh.astype(F32)
    return split((w + m) * t + (w - m))


BLOCK = 256


def group_pass(group, u_ref, at_hl, prep, gu_out, g_out=None):
    mh_ref, cu_ref, cn_ref = prep
    cn = cn_ref[group, 0:1, :]
    ga = None
    for r in range(0, u_ref.shape[0], BLOCK):
        rows = pl.ds(r, BLOCK)
        u_hl = split(u_ref[rows, :])
        g_hl = gradient_matrix(u_hl, at_hl, mh_ref[group, rows, :], cu_ref[group, rows, :], cn)
        part = dot3(u_hl, g_hl, 0, 0)
        ga = part if ga is None else ga + part
        if g_out is None:
            gu_out(rows, dot3(g_hl, at_hl, 1, 1))
        else:
            g_out[0][rows, :], g_out[1][rows, :] = g_hl
    return ga


def update_users(u_ref, um_ref, uo_ref, umo_ref):
    def put(rows, grad):
        uo_ref[rows, :], umo_ref[rows, :] = adagrad(u_ref[rows, :], um_ref[rows, :], grad)

    return put


def fetch_indices(pu_hbm, pa_hbm, ng_hbm, pu, pa, ng, sems):
    cycle = lax.axis_index("pair")
    copies = [
        pltpu.make_async_copy(src.at[0, cycle], dst, sems.at[k])
        for k, (src, dst) in enumerate(((pu_hbm, pu), (pa_hbm, pa), (ng_hbm, ng)))
    ]
    for c in copies:
        c.start()
    return copies


def prepare_round(rnd, pu, pa, ng, users, ads, prep):
    groups = ng.shape[1]
    edges = pu.shape[1] // groups
    for g in range(groups):
        cols = pl.ds(g * edges, edges)
        prepare(g, pu[rnd : rnd + 1, cols], pa[rnd : rnd + 1, cols], ng[rnd, g : g + 1, :], users, ads, *prep)


def second_group(u_ref, at1, amt1, ato_ref, amto_ref, prep, gh_ref, gl_ref, ah_ref, al_ref):
    at_hl = split(at1)
    ah_ref[...], al_ref[...] = at_hl
    ga = group_pass(1, u_ref, at_hl, prep, None, (gh_ref, gl_ref))
    ato_ref[...], amto_ref[...] = adagrad(at1, amt1, ga)


def first_round_kernel(
    u_ref, um_ref, a_ref, am_ref, pu_hbm, pa_hbm, ng_hbm,
    uo_ref, umo_ref, ato_ref, amto_ref, gh_ref, gl_ref, ah_ref, al_ref,
    pu, pa, ng, mh, cu, cn, sems,
):
    copies = fetch_indices(pu_hbm, pa_hbm, ng_hbm, pu, pa, ng, sems)
    at = a_ref[...].T
    amt = am_ref[...].T
    for c in copies:
        c.wait()
    prep = (mh, cu, cn)
    prepare_round(0, pu, pa, ng, u_ref.shape[0], a_ref.shape[0], prep)
    ga = group_pass(0, u_ref, split(at), prep, update_users(u_ref, um_ref, uo_ref, umo_ref))
    at1, amt1 = adagrad(at, amt, ga)
    second_group(uo_ref, at1, amt1, ato_ref, amto_ref, prep, gh_ref, gl_ref, ah_ref, al_ref)


def embedding_kernel(u_ref, um_ref, at_ref, mh, cu, cn, uo_ref, umo_ref, ga_ref):
    put = update_users(u_ref, um_ref, uo_ref, umo_ref)
    ga_ref[...] = group_pass(0, u_ref, split(at_ref[...]), (mh, cu, cn), put)


def moment_kernel(
    u_ref, at_ref, amt_ref, ga_ref, mh, cu, cn,
    ato_ref, amto_ref, gh_ref, gl_ref, ah_ref, al_ref,
):
    at1, amt1 = adagrad(at_ref[...], amt_ref[...], ga_ref[...])
    second_group(u_ref, at1, amt1, ato_ref, amto_ref, (mh, cu, cn), gh_ref, gl_ref, ah_ref, al_ref)


def users_body(u_ref, um_ref, gh_ref, gl_ref, ah_ref, al_ref, uo_ref, umo_ref):
    put = update_users(u_ref, um_ref, uo_ref, umo_ref)
    at_hl = ah_ref[...], al_ref[...]
    for r in range(0, u_ref.shape[0], BLOCK):
        rows = pl.ds(r, BLOCK)
        put(rows, dot3((gh_ref[rows, :], gl_ref[rows, :]), at_hl, 1, 1))


def users_kernel(
    rnd, u_ref, um_ref, gh_ref, gl_ref, ah_ref, al_ref, pu_hbm, pa_hbm, ng_hbm,
    uo_ref, umo_ref, mh, cu, cn, pu, pa, ng, sems,
):
    copies = fetch_indices(pu_hbm, pa_hbm, ng_hbm, pu, pa, ng, sems)
    users_body(u_ref, um_ref, gh_ref, gl_ref, ah_ref, al_ref, uo_ref, umo_ref)
    for c in copies:
        c.wait()
    prepare_round(rnd, pu, pa, ng, u_ref.shape[0], ah_ref.shape[1], (mh, cu, cn))


def last_users_kernel(u_ref, um_ref, gh_ref, gl_ref, ah_ref, al_ref, uo_ref, umo_ref):
    users_body(u_ref, um_ref, gh_ref, gl_ref, ah_ref, al_ref, uo_ref, umo_ref)


def call(kernel, ins, outs, scratch=(), hbm=0, macs=0, name=None):
    vmem = pl.BlockSpec(memory_space=pltpu.VMEM)
    places = [vmem] * (len(ins) - hbm) + [pl.BlockSpec(memory_space=pl.ANY)] * hbm
    size = sum(x.size * x.dtype.itemsize for x in [*ins[: len(ins) - hbm], *outs])
    return pl.pallas_call(
        kernel,
        out_shape=outs,
        in_specs=places,
        out_specs=[vmem] * len(outs),
        scratch_shapes=list(scratch),
        compiler_params=pltpu.CompilerParams(vmem_limit_bytes=VMEM_LIMIT),
        cost_estimate=pl.CostEstimate(flops=2 * macs, bytes_accessed=size, transcendentals=0),
        name=name,
    )(*ins)


def move(x, steps, flip):
    blocks, cycles = lax.axis_size("blk"), lax.axis_size("pair")
    route = []
    for b in range(blocks):
        for p in range(cycles):
            to = (b + steps) % blocks, p ^ (cycles // 2 if flip else 0)
            route.append((b * cycles + p, to[0] * cycles + to[1]))
    return lax.ppermute(x, AXES, route)


def local(users, user_moms, ads, ad_moms, pos_user, pos_ad, neg_ad):
    nu, d = users.shape
    na = ads.shape[0]
    rounds, groups, n = neg_ad.shape[2:]
    edges = pos_user.shape[3]
    indices = (pos_user, pos_ad, neg_ad)

    def shape(*dims, dtype=F32):
        return jax.ShapeDtypeStruct(dims, dtype)

    table_u, table_a = shape(nu, d), shape(d, na)
    part_g, part_a = shape(nu, na, dtype=BF16), shape(d, na, dtype=BF16)
    index_scratch = [
        pltpu.VMEM((rounds, edges), jnp.int32),
        pltpu.VMEM((rounds, edges), jnp.int32),
        pltpu.VMEM((rounds, groups, n), jnp.int32),
    ]
    sems = pltpu.SemaphoreType.DMA((3,))
    prep_shapes = [shape(groups, nu, na, dtype=BF16), shape(groups, nu, 128), shape(groups, 8, na)]
    prep_scratch = [pltpu.VMEM(s.shape, s.dtype) for s in prep_shapes]
    product = 3 * nu * na * d

    u, um, at, amt, *g = call(
        first_round_kernel,
        (users, user_moms, ads, ad_moms, *indices),
        [table_u, table_u, table_a, table_a, part_g, part_g, part_a, part_a],
        [*index_scratch, *prep_scratch, sems], hbm=3, macs=5 * product, name="round_first",
    )
    for rnd in range(1, rounds):
        flip = rnd == rounds // 2
        at = move(at, 1, flip)
        amt = move(amt, 1, flip)
        u, um, *prep = call(
            functools.partial(users_kernel, rnd),
            (u, um, *g, *indices),
            [table_u, table_u, *prep_shapes],
            [*index_scratch, sems], hbm=3, macs=product, name="users_prepare",
        )
        u, um, ga = call(
            embedding_kernel, (u, um, at, *prep), [table_u, table_u, table_a], macs=3 * product, name="group_first",
        )
        at, amt, *g = call(
            moment_kernel, (u, at, amt, ga, *prep), [table_a, table_a, part_g, part_g, part_a, part_a],
            macs=2 * product, name="group_second",
        )
    a = move(at, 1 - rounds, True)
    am = move(amt, 1 - rounds, True)
    u, um = call(last_users_kernel, (u, um, *g), [table_u, table_u], macs=product, name="users_last")
    return u, um, a.T, am.T


def solution(mesh):
    rows = P(AXES, None)
    return jax.shard_map(
        local,
        mesh=mesh,
        in_specs=(rows, rows, rows, rows, P("blk", None, None, None), P("blk", None, None, None), P("blk", None, None, None, None)),
        out_specs=(rows, rows, rows, rows),
        check_vma=False,
    )
```

profile of v0, /device:TPU:192, one launch (start us, length us, event | category | flops | bytes accessed | tf_op | source)
XLA Modules:
  0.0 93.9 jit_solution(5838824026880057005)
XLA Ops:
  0.6 0.0 copy-start
  0.6 0.9 %copy-done = s32[1,16,4,2,512]{4,3,2,1,0:T(2,128)S(1)} copy-done((s32[1,16,4,2,512]{4,3,2,1,0:T(2,128)S(1)}, s32[1,16,4,2,512]{4,3,2,1,0:T(2,128)}, u32[]{:S(2)}) %copy-start) | copy-done | bytes 262168
  1.6 0.0 copy-start.2
  1.6 0.9 copy-done.2
  2.5 0.0 copy-start.4
  2.5 0.9 copy-done.4
  3.4 0.0 copy-start.6
  3.4 1.0 %copy-done.6 = f32[512,256]{1,0:T(8,128)S(1)} copy-done((f32[512,256]{1,0:T(8,128)S(1)}, f32[512,256]{1,0:T(8,128)}, u32[]{:S(2)}) %copy-start.6) | copy-done | bytes 524312
  4.4 0.0 copy-start.7
  4.4 1.0 %copy-done.7 = f32[512,256]{1,0:T(8,128)S(1)} copy-done((f32[512,256]{1,0:T(8,128)S(1)}, f32[512,256]{1,0:T(8,128)}, u32[]{:S(2)}) %copy-start.7) | copy-done | bytes 524312
  5.5 0.0 copy-start.8
  5.5 1.0 %copy-done.8 = f32[512,256]{1,0:T(8,128)S(1)} copy-done((f32[512,256]{1,0:T(8,128)S(1)}, f32[512,256]{1,0:T(8,128)}, u32[]{:S(2)}) %copy-start.8) | copy-done | bytes 524312
  6.5 0.0 copy-start.9
  6.5 1.0 %copy-done.9 = f32[512,256]{1,0:T(8,128)S(1)} copy-done((f32[512,256]{1,0:T(8,128)S(1)}, f32[512,256]{1,0:T(8,128)}, u32[]{:S(2)}) %copy-start.9) | copy-done | bytes 524312
  7.6 0.0 copy-start.1
  7.6 0.0 copy-start.5
  7.6 4.5 %round_first.1 = (f32[512,256]{1,0:T(8,128)S(1)}, f32[512,256]{1,0:T(8,128)S(1)}, f32[256,512]{1,0:T(8,128)S(1)}, f32[256,512]{1,0:T(8,128)S(1)}, bf16[512,512]{...) custom-call(f32[512,256]{1,0:T(8,128)S(1)} %copy-done.6, ...), custom_call_target="tpu_custom_call" | custom-call | flops 2013265920 | bytes 5767168 | tf_op jit(solution)/shard_map/round_first/pallas_call | solution.py:170
  12.1 0.1 collective-permute-start
  12.2 3.3 %collective-permute-start.1 = (f32[256,512]{1,0:T(8,128)S(1)}, f32[256,512]{1,0:T(8,128)S(1)}, u32[]{:S(2)}, u32[]{:S(2)}) collective-permute-start(f32[256,512]{1,0:T(8,128)S(1)} %get-tuple-element.70), channel_id=1, source_target_pairs={{0,16},{1,17},{2,18},{3,19},{4,20},{5,21},{6,22},{7,23},{8,24},{9,... | collective-permute-start | bytes 1572872 | tf_op jit(solution)/shard_map/ppermute | solution.py:189
  15.5 0.0 copy-done.1
  15.5 0.0 copy-done.3
  15.5 0.0 copy-done.5
  15.5 1.7 %users_prepare.3 = (f32[512,256]{1,0:T(8,128)S(1)}, f32[512,256]{1,0:T(8,128)S(1)}, bf16[2,512,512]{2,1,0:T(8,128)(2,1)S(1)}, f32[2,512,128]{2,1,0:T(8,128)S(1)}, f32[2,8,512]{2,1,0:T(8,128)S(1)}) custom-call(f32[512,256]{1,0:T(8,128)S(1)} %get-tuple-element.56.u_ref, f32[512,256]{1,0:T(8,128)S(1)} %get-tuple-element.57.um_ref, ...), custom_call_target="tpu_custom_call" | custom-call | flops 402653184 | bytes 5275648 | tf_op jit(solution)/shard_map/users_prepare/pallas_call | solution.py:170
  17.2 7.2 %collective-permute-done.at_ref = f32[256,512]{1,0:T(8,128)S(1)} collective-permute-done((f32[256,512]{1,0:T(8,128)S(1)}, f32[256,512]{1,0:T(8,128)S(1)}, u32[]{:S(2)}, u32[]{:S(2)}) %collective-permute-start) | collective-permute-done | bytes 524320 | tf_op jit(solution)/shard_map/ppermute | solution.py:189
  24.4 2.1 %group_first.3 = (f32[512,256]{1,0:T(8,128)S(1)}, f32[512,256]{1,0:T(8,128)S(1)}, f32[256,512]{1,0:T(8,128)S(1)}) custom-call(f32[512,256]{1,0:T(8,128)S(1)} %get-tuple-element.62.u_ref, f32[512,256]{1,0:T(8,128)S(1)} %get-tuple-element.63.um_ref, f32[256,512]{1,0:T(8,128)S(1)} %collective-permute-done.at_ref, ...), custom_call_target="tpu_custom_call" | custom-call | flops 1207959552 | bytes 4751360 | tf_op jit(solution)/shard_map/group_first/pallas_call | solution.py:170
  26.6 3.5 %collective-permute-done.1.amt_ref = f32[256,512]{1,0:T(8,128)S(1)} collective-permute-done((f32[256,512]{1,0:T(8,128)S(1)}, f32[256,512]{1,0:T(8,128)S(1)}, u32[]{:S(2)}, u32[]{:S(2)}) %collective-permute-start.1) | collective-permute-done | bytes 524320 | tf_op jit(solution)/shard_map/ppermute | solution.py:189
  30.0 1.8 %group_second.3 = (f32[256,512]{1,0:T(8,128)S(1)}, f32[256,512]{1,0:T(8,128)S(1)}, bf16[512,512]{1,0:T(8,128)(2,1)S(1)}, bf16[512,512]{1,0:T(8,128)(2,1)S(1)}, b...) custom-call(f32[512,256]{1,0:T(8,128)S(1)} %get-tuple-element.68.u_ref, ...), custom_call_target="tpu_custom_call" | custom-call | flops 805306368 | bytes 6324224 | tf_op jit(solution)/shard_map/group_second/pallas_call | solution.py:170
  31.8 0.1 collective-permute-start.2
  31.9 0.7 collective-permute-start.3
  32.7 1.7 %users_prepare.4 = (f32[512,256]{1,0:T(8,128)S(1)}, f32[512,256]{1,0:T(8,128)S(1)}, bf16[2,512,512]{2,1,0:T(8,128)(2,1)S(1)}, f32[2,512,128]{2,1,0:T(8,128)S(1)}, f32[2,8,512]{2,1,0:T(8,128)S(1)}) custom-call(f32[512,256]{1,0:T(8,128)S(1)} %get-tuple-element.68.u_ref, f32[512,256]{1,0:T(8,128)S(1)} %get-tuple-element.69.um_ref, ...), custom_call_target="tpu_custom_call" | custom-call | flops 402653184 | bytes 5275648 | tf_op jit(solution)/shard_map/users_prepare/pallas_call | solution.py:170
  34.3 9.5 %collective-permute-done.2.at_ref = f32[256,512]{1,0:T(8,128)S(1)} collective-permute-done((f32[256,512]{1,0:T(8,128)S(1)}, f32[256,512]{1,0:T(8,128)S(1)}, u32[]{:S(2)}, u32[]{:S(2)}) %collective-permute-start.2) | collective-permute-done | bytes 524320 | tf_op jit(solution)/shard_map/ppermute | solution.py:189
  43.8 2.1 %group_first.4 = (f32[512,256]{1,0:T(8,128)S(1)}, f32[512,256]{1,0:T(8,128)S(1)}, f32[256,512]{1,0:T(8,128)S(1)}) custom-call(f32[512,256]{1,0:T(8,128)S(1)} %get-tuple-element.76.u_ref, f32[512,256]{1,0:T(8,128)S(1)} %get-tuple-element.77.um_ref, f32[256,512]{1,0:T(8,128)S(1)} %collective-permute-done.2.at_ref, ...), custom_call_target="tpu_custom_call" | custom-call | flops 1207959552 | bytes 4751360 | tf_op jit(solution)/shard_map/group_first/pallas_call | solution.py:170
  46.0 3.5 %collective-permute-done.3.amt_ref = f32[256,512]{1,0:T(8,128)S(1)} collective-permute-done((f32[256,512]{1,0:T(8,128)S(1)}, f32[256,512]{1,0:T(8,128)S(1)}, u32[]{:S(2)}, u32[]{:S(2)}) %collective-permute-start.3) | collective-permute-done | bytes 524320 | tf_op jit(solution)/shard_map/ppermute | solution.py:189
  49.5 1.8 %group_second.4 = (f32[256,512]{1,0:T(8,128)S(1)}, f32[256,512]{1,0:T(8,128)S(1)}, bf16[512,512]{1,0:T(8,128)(2,1)S(1)}, bf16[512,512]{1,0:T(8,128)(2,1)S(1)}, b...) custom-call(f32[512,256]{1,0:T(8,128)S(1)} %get-tuple-element.82.u_ref, ...), custom_call_target="tpu_custom_call" | custom-call | flops 805306368 | bytes 6324224 | tf_op jit(solution)/shard_map/group_second/pallas_call | solution.py:170
  51.2 0.1 collective-permute-start.4
  51.3 0.1 collective-permute-start.5
  51.4 1.7 %users_prepare.5 = (f32[512,256]{1,0:T(8,128)S(1)}, f32[512,256]{1,0:T(8,128)S(1)}, bf16[2,512,512]{2,1,0:T(8,128)(2,1)S(1)}, f32[2,512,128]{2,1,0:T(8,128)S(1)}, f32[2,8,512]{2,1,0:T(8,128)S(1)}) custom-call(f32[512,256]{1,0:T(8,128)S(1)} %get-tuple-element.82.u_ref, f32[512,256]{1,0:T(8,128)S(1)} %get-tuple-element.83.um_ref, ...), custom_call_target="tpu_custom_call" | custom-call | flops 402653184 | bytes 5275648 | tf_op jit(solution)/shard_map/users_prepare/pallas_call | solution.py:170
  53.1 10.4 %collective-permute-done.4.at_ref = f32[256,512]{1,0:T(8,128)S(1)} collective-permute-done((f32[256,512]{1,0:T(8,128)S(1)}, f32[256,512]{1,0:T(8,128)S(1)}, u32[]{:S(2)}, u32[]{:S(2)}) %collective-permute-start.4) | collective-permute-done | bytes 524320 | tf_op jit(solution)/shard_map/ppermute | solution.py:189
  63.5 2.1 %group_first.5 = (f32[512,256]{1,0:T(8,128)S(1)}, f32[512,256]{1,0:T(8,128)S(1)}, f32[256,512]{1,0:T(8,128)S(1)}) custom-call(f32[512,256]{1,0:T(8,128)S(1)} %get-tuple-element.90.u_ref, f32[512,256]{1,0:T(8,128)S(1)} %get-tuple-element.91.um_ref, f32[256,512]{1,0:T(8,128)S(1)} %collective-permute-done.4.at_ref, ...), custom_call_target="tpu_custom_call" | custom-call | flops 1207959552 | bytes 4751360 | tf_op jit(solution)/shard_map/group_first/pallas_call | solution.py:170
  65.7 3.5 %collective-permute-done.5.amt_ref = f32[256,512]{1,0:T(8,128)S(1)} collective-permute-done((f32[256,512]{1,0:T(8,128)S(1)}, f32[256,512]{1,0:T(8,128)S(1)}, u32[]{:S(2)}, u32[]{:S(2)}) %collective-permute-start.5) | collective-permute-done | bytes 524320 | tf_op jit(solution)/shard_map/ppermute | solution.py:189
  69.2 1.8 %group_second.5 = (f32[256,512]{1,0:T(8,128)S(1)}, f32[256,512]{1,0:T(8,128)S(1)}, bf16[512,512]{1,0:T(8,128)(2,1)S(1)}, bf16[512,512]{1,0:T(8,128)(2,1)S(1)}, b...) custom-call(f32[512,256]{1,0:T(8,128)S(1)} %get-tuple-element.96.u_ref, ...), custom_call_target="tpu_custom_call" | custom-call | flops 805306368 | bytes 6324224 | tf_op jit(solution)/shard_map/group_second/pallas_call | solution.py:170
  70.9 0.1 collective-permute-start.6
  71.0 0.1 collective-permute-start.7
  71.1 1.7 %users_last.1 = (f32[512,256]{1,0:T(8,128)}, f32[512,256]{1,0:T(8,128)}) custom-call(f32[512,256]{1,0:T(8,128)S(1)} %get-tuple-element.96.u_ref, f32[512,256]{1,0:T(8,128)S(1)} %get-tuple-element.97.um_ref, bf16[512,512]{1,0:T(8,128)(2,1)S(1)} %get-tuple-element.100.gh_ref, bf16[512,512]{1,0:T(8,128)(2,1)S(1)} %get-tuple-element.101.gl_ref, ...), custom_call_target="tpu_custom_call" | custom-call | flops 402653184 | bytes 3670016 | tf_op jit(solution)/shard_map/users_last/pallas_call | solution.py:170
  72.9 10.5 %collective-permute-done.6 = f32[256,512]{1,0:T(8,128)S(1)} collective-permute-done((f32[256,512]{1,0:T(8,128)S(1)}, f32[256,512]{1,0:T(8,128)S(1)}, u32[]{:S(2)}, u32[]{:S(2)}) %collective-permute-start.6) | collective-permute-done | bytes 524320 | tf_op jit(solution)/shard_map/ppermute | solution.py:189
  83.4 1.0 %copy.11 = f32[512,256]{1,0:T(8,128)} copy(f32[512,256]{0,1:T(8,128)S(1)} %bitcast.3) | data formatting | bytes 1048576
  84.4 8.5 %collective-permute-done.7 = f32[256,512]{1,0:T(8,128)S(1)} collective-permute-done((f32[256,512]{1,0:T(8,128)S(1)}, f32[256,512]{1,0:T(8,128)S(1)}, u32[]{:S(2)}, u32[]{:S(2)}) %collective-permute-start.7) | collective-permute-done | bytes 524320 | tf_op jit(solution)/shard_map/ppermute | solution.py:189
  92.9 1.0 %copy.12 = f32[512,256]{1,0:T(8,128)} copy(f32[512,256]{0,1:T(8,128)S(1)} %bitcast.2) | data formatting | bytes 1048576
  (1 shorter events, 0.0 us)
Async XLA Ops:
  0.6 1.0 %copy-start = (s32[1,16,4,2,512]{4,3,2,1,0:T(2,128)S(1)}, s32[1,16,4,2,512]{4,3,2,1,0:T(2,128)}, u32[]{:S(2)}) copy-start(s32[1,16,4,2,512]{4,3,2,1,0:T(2,128)} %ng_hbm.7) | copy-start | bytes 786436
  1.6 0.9 copy-start.2
  2.5 0.9 copy-start.4
  3.4 1.0 %copy-start.6 = (f32[512,256]{1,0:T(8,128)S(1)}, f32[512,256]{1,0:T(8,128)}, u32[]{:S(2)}) copy-start(f32[512,256]{1,0:T(8,128)} %u_ref.1) | copy-start | bytes 1572868
  4.4 1.0 %copy-start.7 = (f32[512,256]{1,0:T(8,128)S(1)}, f32[512,256]{1,0:T(8,128)}, u32[]{:S(2)}) copy-start(f32[512,256]{1,0:T(8,128)} %um_ref.1) | copy-start | bytes 1572868
  5.5 1.0 %copy-start.8 = (f32[512,256]{1,0:T(8,128)S(1)}, f32[512,256]{1,0:T(8,128)}, u32[]{:S(2)}) copy-start(f32[512,256]{1,0:T(8,128)} %a_ref.1) | copy-start | bytes 1572868
  6.5 1.0 %copy-start.9 = (f32[512,256]{1,0:T(8,128)S(1)}, f32[512,256]{1,0:T(8,128)}, u32[]{:S(2)}) copy-start(f32[512,256]{1,0:T(8,128)} %am_ref.1) | copy-start | bytes 1572868
  7.6 7.9 %copy-start.1 = (s32[1,16,4,2,512]{4,3,2,1,0:T(2,128)S(1)}, s32[1,16,4,2,512]{4,3,2,1,0:T(2,128)}, u32[]{:S(2)}) copy-start(s32[1,16,4,2,512]{4,3,2,1,0:T(2,128)} %ng_hbm.7) | copy-start | bytes 786436
  7.6 7.9 %copy-start.3 = (s32[1,16,4,512]{3,2,1,0:T(4,128)S(1)}, s32[1,16,4,512]{3,2,1,0:T(4,128)}, u32[]{:S(2)}) copy-start(s32[1,16,4,512]{3,2,1,0:T(4,128)} %pu_hbm.7) | copy-start | bytes 393220
  7.6 7.9 %copy-start.5 = (s32[1,16,4,512]{3,2,1,0:T(4,128)S(1)}, s32[1,16,4,512]{3,2,1,0:T(4,128)}, u32[]{:S(2)}) copy-start(s32[1,16,4,512]{3,2,1,0:T(4,128)} %pa_hbm.7) | copy-start | bytes 393220
  12.1 12.3 %collective-permute-start = (f32[256,512]{1,0:T(8,128)S(1)}, f32[256,512]{1,0:T(8,128)S(1)}, u32[]{:S(2)}, u32[]{:S(2)}) collective-permute-start(f32[256,512]{1,0:T(8,128)S(1)} %get-tuple-element.64), channel_id=1, source_target_pairs={{0,16},{1,17},{2,18},{3,19},{4,20},{5,21},{6,22},{7,23},{8,24},{9,... | collective-permute-start | bytes 1572872 | tf_op jit(solution)/shard_map/ppermute | solution.py:189
  12.2 17.8 %collective-permute-start.1 = (f32[256,512]{1,0:T(8,128)S(1)}, f32[256,512]{1,0:T(8,128)S(1)}, u32[]{:S(2)}, u32[]{:S(2)}) collective-permute-start(f32[256,512]{1,0:T(8,128)S(1)} %get-tuple-element.70), channel_id=1, source_target_pairs={{0,16},{1,17},{2,18},{3,19},{4,20},{5,21},{6,22},{7,23},{8,24},{9,... | collective-permute-start | bytes 1572872 | tf_op jit(solution)/shard_map/ppermute | solution.py:189
  31.8 12.0 %collective-permute-start.2 = (f32[256,512]{1,0:T(8,128)S(1)}, f32[256,512]{1,0:T(8,128)S(1)}, u32[]{:S(2)}, u32[]{:S(2)}) collective-permute-start(f32[256,512]{1,0:T(8,128)S(1)} %get-tuple-element.78), channel_id=1, source_target_pairs={{0,24},{1,25},{2,26},{3,27},{4,28},{5,29},{6,30},{7,31},{8,16},{9,... | collective-permute-start | bytes 1572872 | tf_op jit(solution)/shard_map/ppermute | solution.py:189
  31.9 17.5 %collective-permute-start.3 = (f32[256,512]{1,0:T(8,128)S(1)}, f32[256,512]{1,0:T(8,128)S(1)}, u32[]{:S(2)}, u32[]{:S(2)}) collective-permute-start(f32[256,512]{1,0:T(8,128)S(1)} %get-tuple-element.84), channel_id=1, source_target_pairs={{0,24},{1,25},{2,26},{3,27},{4,28},{5,29},{6,30},{7,31},{8,16},{9,... | collective-permute-start | bytes 1572872 | tf_op jit(solution)/shard_map/ppermute | solution.py:189
  51.2 12.3 %collective-permute-start.4 = (f32[256,512]{1,0:T(8,128)S(1)}, f32[256,512]{1,0:T(8,128)S(1)}, u32[]{:S(2)}, u32[]{:S(2)}) collective-permute-start(f32[256,512]{1,0:T(8,128)S(1)} %get-tuple-element.92), channel_id=1, source_target_pairs={{0,16},{1,17},{2,18},{3,19},{4,20},{5,21},{6,22},{7,23},{8,24},{9,... | collective-permute-start | bytes 1572872 | tf_op jit(solution)/shard_map/ppermute | solution.py:189
  51.3 17.8 %collective-permute-start.5 = (f32[256,512]{1,0:T(8,128)S(1)}, f32[256,512]{1,0:T(8,128)S(1)}, u32[]{:S(2)}, u32[]{:S(2)}) collective-permute-start(f32[256,512]{1,0:T(8,128)S(1)} %get-tuple-element.98), channel_id=1, source_target_pairs={{0,16},{1,17},{2,18},{3,19},{4,20},{5,21},{6,22},{7,23},{8,24},{9,... | collective-permute-start | bytes 1572872 | tf_op jit(solution)/shard_map/ppermute | solution.py:189
  70.9 12.5 %collective-permute-start.6 = (f32[256,512]{1,0:T(8,128)S(1)}, f32[256,512]{1,0:T(8,128)S(1)}, u32[]{:S(2)}, u32[]{:S(2)}) collective-permute-start(f32[256,512]{1,0:T(8,128)S(1)} %get-tuple-element.106), channel_id=1, source_target_pairs={{0,216},{1,217},{2,218},{3,219},{4,220},{5,221},{6,222},{7,223},{8... | collective-permute-start | bytes 1572872 | tf_op jit(solution)/shard_map/ppermute | solution.py:189
  71.0 21.8 %collective-permute-start.7 = (f32[256,512]{1,0:T(8,128)S(1)}, f32[256,512]{1,0:T(8,128)S(1)}, u32[]{:S(2)}, u32[]{:S(2)}) collective-permute-start(f32[256,512]{1,0:T(8,128)S(1)} %get-tuple-element.107), channel_id=1, source_target_pairs={{0,216},{1,217},{2,218},{3,219},{4,220},{5,221},{6,222},{7,223},{8... | collective-permute-start | bytes 1572872 | tf_op jit(solution)/shard_map/ppermute | solution.py:189
where the time goes:
time: 95 us; the launch traced here: 93.9 us
  waiting for transfers between devices  56.6 us (60%)
  Pallas kernels  23.1 us (24%)
  local copies, waits for them, and re-layouts  8.91 us (9%)
  starting transfers between devices  4.54 us (5%)
    ppermute x8, waiting for transfers between devices, move(): return lax.ppermute(x, AXES, route)  56.6 us
    pallas_call x11, Pallas kernels, call(): pl.pallas_call(kernel, out_shape=outs, in_specs=places, out_specs=[vmem]...  23.1 us
    unnamed x22, local copies, waits for them, and re-layouts  8.91 us
    ppermute x8, starting transfers between devices, move(): return lax.ppermute(x, AXES, route)  4.54 us
  transfers between devices with their start and end apart: 8, of which 8 were waited for; matrix products, arithmetic and copies ran while one was open for 1% of the time, Pallas kernels for 14%

commit v1 on v0

--- a/solution.py
+++ b/solution.py
@@ -1,4 +1,5 @@
 import functools
+import math
 
 import jax
 import jax.numpy as jnp
@@ -111,17 +112,27 @@
 
 
 def first_round_kernel(
-    u_ref, um_ref, a_ref, am_ref, pu_hbm, pa_hbm, ng_hbm,
+    pu_hbm, pa_hbm, ng_hbm, u_hbm, a_hbm, um_hbm, am_hbm,
     uo_ref, umo_ref, ato_ref, amto_ref, gh_ref, gl_ref, ah_ref, al_ref,
-    pu, pa, ng, mh, cu, cn, sems,
+    pu, pa, ng, mh, cu, cn, u_ref, um_ref, a_ref, am_ref, sems, table_sems,
 ):
     copies = fetch_indices(pu_hbm, pa_hbm, ng_hbm, pu, pa, ng, sems)
+    tables = [
+        pltpu.make_async_copy(src, dst, table_sems.at[k])
+        for k, (src, dst) in enumerate(
+            ((u_hbm, u_ref), (a_hbm, a_ref), (um_hbm, um_ref), (am_hbm, am_ref))
+        )
+    ]
+    for c in tables:
+        c.start()
+    for c in copies:
+        c.wait()
+    prep = (mh, cu, cn)
+    prepare_round(0, pu, pa, ng, u_ref.shape[0], a_ref.shape[0], prep)
+    for c in tables:
+        c.wait()
     at = a_ref[...].T
     amt = am_ref[...].T
-    for c in copies:
-        c.wait()
-    prep = (mh, cu, cn)
-    prepare_round(0, pu, pa, ng, u_ref.shape[0], a_ref.shape[0], prep)
     ga = group_pass(0, u_ref, split(at), prep, update_users(u_ref, um_ref, uo_ref, umo_ref))
     at1, amt1 = adagrad(at, amt, ga)
     second_group(uo_ref, at1, amt1, ato_ref, amto_ref, prep, gh_ref, gl_ref, ah_ref, al_ref)
@@ -159,24 +170,59 @@
     prepare_round(rnd, pu, pa, ng, u_ref.shape[0], ah_ref.shape[1], (mh, cu, cn))
 
 
-def last_users_kernel(u_ref, um_ref, gh_ref, gl_ref, ah_ref, al_ref, uo_ref, umo_ref):
+def last_users_kernel(u_ref, um_ref, gh_ref, gl_ref, ah_ref, al_ref, uo_hbm, umo_hbm, uo_ref, umo_ref, sems):
     users_body(u_ref, um_ref, gh_ref, gl_ref, ah_ref, al_ref, uo_ref, umo_ref)
-
-
-def call(kernel, ins, outs, scratch=(), hbm=0, macs=0, name=None):
+    copies = [
+        pltpu.make_async_copy(uo_ref, uo_hbm, sems.at[0]),
+        pltpu.make_async_copy(umo_ref, umo_hbm, sems.at[1]),
+    ]
+    for c in copies:
+        c.start()
+    for c in copies:
+        c.wait()
+
+
+def call(kernel, ins, outs, scratch=(), hbm=0, macs=0, name=None, out_place=pltpu.VMEM):
     vmem = pl.BlockSpec(memory_space=pltpu.VMEM)
-    places = [vmem] * (len(ins) - hbm) + [pl.BlockSpec(memory_space=pl.ANY)] * hbm
-    size = sum(x.size * x.dtype.itemsize for x in [*ins[: len(ins) - hbm], *outs])
+    places = [vmem] * (len(ins) - hbm) + [pl.BlockSpec(memory_space=pltpu.HBM)] * hbm
+    size = sum(math.prod(x.shape) * x.dtype.itemsize for x in [*ins[: len(ins) - hbm], *outs])
     return pl.pallas_call(
         kernel,
         out_shape=outs,
         in_specs=places,
-        out_specs=[vmem] * len(outs),
+        out_specs=[pl.BlockSpec(memory_space=out_place)] * len(outs),
         scratch_shapes=list(scratch),
         compiler_params=pltpu.CompilerParams(vmem_limit_bytes=VMEM_LIMIT),
         cost_estimate=pl.CostEstimate(flops=2 * macs, bytes_accessed=size, transcendentals=0),
         name=name,
-    )(*ins)
+    )(*ins[: len(ins) - hbm], *(pltpu.with_memory_space_constraint(x, pltpu.HBM) for x in ins[len(ins) - hbm :]))
+
+
+def finish_kernel(xt_ref, out_hbm, x_ref, sems):
+    count = sems.shape[0]
+    size = x_ref.shape[0] // count
+    copies = []
+    for k in range(count):
+        rows = pl.ds(k * size, size)
+        x_ref[rows, :] = xt_ref[:, rows].T
+        copies.append(pltpu.make_async_copy(x_ref.at[rows, :], out_hbm.at[rows, :], sems.at[k]))
+        copies[-1].start()
+    for c in copies:
+        c.wait()
+
+
+def finish(xt):
+    d, rows = xt.shape
+    return pl.pallas_call(
+        finish_kernel,
+        out_shape=pltpu.HBM((rows, d), xt.dtype),
+        in_specs=[pl.BlockSpec(memory_space=pltpu.VMEM)],
+        out_specs=pl.BlockSpec(memory_space=pltpu.HBM),
+        scratch_shapes=[pltpu.VMEM((rows, d), xt.dtype), pltpu.SemaphoreType.DMA((4,))],
+        compiler_params=pltpu.CompilerParams(vmem_limit_bytes=VMEM_LIMIT),
+        cost_estimate=pl.CostEstimate(flops=0, bytes_accessed=2 * xt.size * 4, transcendentals=0),
+        name="ads_out",
+    )(xt)
 
 
 def move(x, steps, flip):
@@ -213,9 +259,10 @@
 
     u, um, at, amt, *g = call(
         first_round_kernel,
-        (users, user_moms, ads, ad_moms, *indices),
+        (*indices, users, ads, user_moms, ad_moms),
         [table_u, table_u, table_a, table_a, part_g, part_g, part_a, part_a],
-        [*index_scratch, *prep_scratch, sems], hbm=3, macs=5 * product, name="round_first",
+        [*index_scratch, *prep_scratch, *[pltpu.VMEM((nu, d), F32)] * 2, *[pltpu.VMEM((na, d), F32)] * 2, sems, pltpu.SemaphoreType.DMA((4,))],
+        hbm=7, macs=5 * product, name="round_first",
     )
     for rnd in range(1, rounds):
         flip = rnd == rounds // 2
@@ -234,10 +281,13 @@
             moment_kernel, (u, at, amt, ga, *prep), [table_a, table_a, part_g, part_g, part_a, part_a],
             macs=2 * product, name="group_second",
         )
-    a = move(at, 1 - rounds, True)
-    am = move(amt, 1 - rounds, True)
-    u, um = call(last_users_kernel, (u, um, *g), [table_u, table_u], macs=product, name="users_last")
-    return u, um, a.T, am.T
+    a = finish(move(at, 1 - rounds, True))
+    am = finish(move(amt, 1 - rounds, True))
+    u, um = call(
+        last_users_kernel, (u, um, *g), [pltpu.HBM((nu, d), F32)] * 2,
+        [pltpu.VMEM((nu, d), F32)] * 2 + [pltpu.SemaphoreType.DMA((2,))], macs=product, name="users_last", out_place=pltpu.HBM,
+    )
+    return u, um, a, am
 
 
 def solution(mesh):

time: 95 us -> 89.3 us (0.940)
  local copies, waits for them, and re-layouts: 8.91 us -> 0 us
  Pallas kernels: 23.1 us -> 26.8 us
    unnamed x22 -> x0, local copies, waits for them, and re-layouts: 8.91 us -> none
    pallas_call x11 -> x13, Pallas kernels: 23.1 us -> 26.8 us  [the longest x11 25 us: call(): pl.pallas_call(kernel, out_shape=outs, in_specs=places, out_specs=[pl.Blo...]
  transfers between devices with their start and end apart: 8 -> 8, of which waited for: 8 -> 8; matrix products, arithmetic and copies ran while one was open for 1% -> 0% of each run, Pallas kernels for 14% -> 17%
where the time goes in v1:
time: 89.3 us; the launch traced here: 87.9 us
  waiting for transfers between devices  55.7 us (62%)
  Pallas kernels  26.8 us (30%)
  starting transfers between devices  4.53 us (5%)
  between operations  0.94 us (1%)
    ppermute x8, waiting for transfers between devices, move(): return lax.ppermute(x, AXES, route)  55.7 us
    pallas_call x11, Pallas kernels, call(): pl.pallas_call(kernel, out_shape=outs, in_specs=places, out_specs=[pl.Blo...  25 us
    ppermute x8, starting transfers between devices, move(): return lax.ppermute(x, AXES, route)  4.53 us
    pallas_call x2, Pallas kernels, finish(): pl.pallas_call(finish_kernel, out_shape=pltpu.HBM((rows, d), xt.dtype), i...  1.84 us
  transfers between devices with their start and end apart: 8, of which 8 were waited for; matrix products, arithmetic and copies ran while one was open for 0% of the time, Pallas kernels for 17%

profile of v1, /device:TPU:192, one launch (start us, length us, event | category | flops | bytes accessed | tf_op | source)
XLA Modules:
  0.0 87.9 jit_solution(891377531788529695)
XLA Ops:
  0.6 5.4 %round_first.1 = (f32[512,256]{1,0:T(8,128)S(1)}, f32[512,256]{1,0:T(8,128)S(1)}, f32[256,512]{1,0:T(8,128)S(1)}, f32[256,512]{1,0:T(8,128)S(1)}, bf16[512,512]{...) custom-call(s32[1,16,4,512]{3,2,1,0:T(4,128)} %pu_hbm.7, ...), custom_call_target="tpu_custom_call" | custom-call | flops 2013265920 | bytes 3670016 | tf_op jit(solution)/shard_map/round_first/pallas_call | solution.py:189
  6.1 0.1 collective-permute-start
  6.2 3.3 %collective-permute-start.1 = (f32[256,512]{1,0:T(8,128)S(1)}, f32[256,512]{1,0:T(8,128)S(1)}, u32[]{:S(2)}, u32[]{:S(2)}) collective-permute-start(f32[256,512]{1,0:T(8,128)S(1)} %get-tuple-element.70), channel_id=1, source_target_pairs={{0,16},{1,17},{2,18},{3,19},{4,20},{5,21},{6,22},{7,23},{8,24},{9,... | collective-permute-start | bytes 1572872 | tf_op jit(solution)/shard_map/ppermute | solution.py:235
  9.4 2.0 %users_prepare.3 = (f32[512,256]{1,0:T(8,128)S(1)}, f32[512,256]{1,0:T(8,128)S(1)}, bf16[2,512,512]{2,1,0:T(8,128)(2,1)S(1)}, f32[2,512,128]{2,1,0:T(8,128)S(1)}, f32[2,8,512]{2,1,0:T(8,128)S(1)}) custom-call(f32[512,256]{1,0:T(8,128)S(1)} %get-tuple-element.56.u_ref, f32[512,256]{1,0:T(8,128)S(1)} %get-tuple-element.57.um_ref, ...), custom_call_target="tpu_custom_call" | custom-call | flops 402653184 | bytes 5275648 | tf_op jit(solution)/shard_map/users_prepare/pallas_call | solution.py:189
  11.5 6.9 %collective-permute-done.at_ref = f32[256,512]{1,0:T(8,128)S(1)} collective-permute-done((f32[256,512]{1,0:T(8,128)S(1)}, f32[256,512]{1,0:T(8,128)S(1)}, u32[]{:S(2)}, u32[]{:S(2)}) %collective-permute-start) | collective-permute-done | bytes 524320 | tf_op jit(solution)/shard_map/ppermute | solution.py:235
  18.4 2.1 %group_first.3 = (f32[512,256]{1,0:T(8,128)S(1)}, f32[512,256]{1,0:T(8,128)S(1)}, f32[256,512]{1,0:T(8,128)S(1)}) custom-call(f32[512,256]{1,0:T(8,128)S(1)} %get-tuple-element.62.u_ref, f32[512,256]{1,0:T(8,128)S(1)} %get-tuple-element.63.um_ref, f32[256,512]{1,0:T(8,128)S(1)} %collective-permute-done.at_ref, ...), custom_call_target="tpu_custom_call" | custom-call | flops 1207959552 | bytes 4751360 | tf_op jit(solution)/shard_map/group_first/pallas_call | solution.py:189
  20.5 3.5 %collective-permute-done.1.amt_ref = f32[256,512]{1,0:T(8,128)S(1)} collective-permute-done((f32[256,512]{1,0:T(8,128)S(1)}, f32[256,512]{1,0:T(8,128)S(1)}, u32[]{:S(2)}, u32[]{:S(2)}) %collective-permute-start.1) | collective-permute-done | bytes 524320 | tf_op jit(solution)/shard_map/ppermute | solution.py:235
  24.0 1.8 %group_second.3 = (f32[256,512]{1,0:T(8,128)S(1)}, f32[256,512]{1,0:T(8,128)S(1)}, bf16[512,512]{1,0:T(8,128)(2,1)S(1)}, bf16[512,512]{1,0:T(8,128)(2,1)S(1)}, b...) custom-call(f32[512,256]{1,0:T(8,128)S(1)} %get-tuple-element.68.u_ref, ...), custom_call_target="tpu_custom_call" | custom-call | flops 805306368 | bytes 6324224 | tf_op jit(solution)/shard_map/group_second/pallas_call | solution.py:189
  25.8 0.1 collective-permute-start.2
  25.9 0.7 collective-permute-start.3
  26.6 2.0 %users_prepare.4 = (f32[512,256]{1,0:T(8,128)S(1)}, f32[512,256]{1,0:T(8,128)S(1)}, bf16[2,512,512]{2,1,0:T(8,128)(2,1)S(1)}, f32[2,512,128]{2,1,0:T(8,128)S(1)}, f32[2,8,512]{2,1,0:T(8,128)S(1)}) custom-call(f32[512,256]{1,0:T(8,128)S(1)} %get-tuple-element.68.u_ref, f32[512,256]{1,0:T(8,128)S(1)} %get-tuple-element.69.um_ref, ...), custom_call_target="tpu_custom_call" | custom-call | flops 402653184 | bytes 5275648 | tf_op jit(solution)/shard_map/users_prepare/pallas_call | solution.py:189
  28.6 9.2 %collective-permute-done.2.at_ref = f32[256,512]{1,0:T(8,128)S(1)} collective-permute-done((f32[256,512]{1,0:T(8,128)S(1)}, f32[256,512]{1,0:T(8,128)S(1)}, u32[]{:S(2)}, u32[]{:S(2)}) %collective-permute-start.2) | collective-permute-done | bytes 524320 | tf_op jit(solution)/shard_map/ppermute | solution.py:235
  37.8 2.1 %group_first.4 = (f32[512,256]{1,0:T(8,128)S(1)}, f32[512,256]{1,0:T(8,128)S(1)}, f32[256,512]{1,0:T(8,128)S(1)}) custom-call(f32[512,256]{1,0:T(8,128)S(1)} %get-tuple-element.76.u_ref, f32[512,256]{1,0:T(8,128)S(1)} %get-tuple-element.77.um_ref, f32[256,512]{1,0:T(8,128)S(1)} %collective-permute-done.2.at_ref, ...), custom_call_target="tpu_custom_call" | custom-call | flops 1207959552 | bytes 4751360 | tf_op jit(solution)/shard_map/group_first/pallas_call | solution.py:189
  39.9 3.5 %collective-permute-done.3.amt_ref = f32[256,512]{1,0:T(8,128)S(1)} collective-permute-done((f32[256,512]{1,0:T(8,128)S(1)}, f32[256,512]{1,0:T(8,128)S(1)}, u32[]{:S(2)}, u32[]{:S(2)}) %collective-permute-start.3) | collective-permute-done | bytes 524320 | tf_op jit(solution)/shard_map/ppermute | solution.py:235
  43.4 1.8 %group_second.4 = (f32[256,512]{1,0:T(8,128)S(1)}, f32[256,512]{1,0:T(8,128)S(1)}, bf16[512,512]{1,0:T(8,128)(2,1)S(1)}, bf16[512,512]{1,0:T(8,128)(2,1)S(1)}, b...) custom-call(f32[512,256]{1,0:T(8,128)S(1)} %get-tuple-element.82.u_ref, ...), custom_call_target="tpu_custom_call" | custom-call | flops 805306368 | bytes 6324224 | tf_op jit(solution)/shard_map/group_second/pallas_call | solution.py:189
  45.2 0.1 collective-permute-start.4
  45.3 0.1 collective-permute-start.5
  45.4 2.0 %users_prepare.5 = (f32[512,256]{1,0:T(8,128)S(1)}, f32[512,256]{1,0:T(8,128)S(1)}, bf16[2,512,512]{2,1,0:T(8,128)(2,1)S(1)}, f32[2,512,128]{2,1,0:T(8,128)S(1)}, f32[2,8,512]{2,1,0:T(8,128)S(1)}) custom-call(f32[512,256]{1,0:T(8,128)S(1)} %get-tuple-element.82.u_ref, f32[512,256]{1,0:T(8,128)S(1)} %get-tuple-element.83.um_ref, ...), custom_call_target="tpu_custom_call" | custom-call | flops 402653184 | bytes 5275648 | tf_op jit(solution)/shard_map/users_prepare/pallas_call | solution.py:189
  47.4 10.1 %collective-permute-done.4.at_ref = f32[256,512]{1,0:T(8,128)S(1)} collective-permute-done((f32[256,512]{1,0:T(8,128)S(1)}, f32[256,512]{1,0:T(8,128)S(1)}, u32[]{:S(2)}, u32[]{:S(2)}) %collective-permute-start.4) | collective-permute-done | bytes 524320 | tf_op jit(solution)/shard_map/ppermute | solution.py:235
  57.5 2.1 %group_first.5 = (f32[512,256]{1,0:T(8,128)S(1)}, f32[512,256]{1,0:T(8,128)S(1)}, f32[256,512]{1,0:T(8,128)S(1)}) custom-call(f32[512,256]{1,0:T(8,128)S(1)} %get-tuple-element.90.u_ref, f32[512,256]{1,0:T(8,128)S(1)} %get-tuple-element.91.um_ref, f32[256,512]{1,0:T(8,128)S(1)} %collective-permute-done.4.at_ref, ...), custom_call_target="tpu_custom_call" | custom-call | flops 1207959552 | bytes 4751360 | tf_op jit(solution)/shard_map/group_first/pallas_call | solution.py:189
  59.6 3.5 %collective-permute-done.5.amt_ref = f32[256,512]{1,0:T(8,128)S(1)} collective-permute-done((f32[256,512]{1,0:T(8,128)S(1)}, f32[256,512]{1,0:T(8,128)S(1)}, u32[]{:S(2)}, u32[]{:S(2)}) %collective-permute-start.5) | collective-permute-done | bytes 524320 | tf_op jit(solution)/shard_map/ppermute | solution.py:235
  63.1 1.8 %group_second.5 = (f32[256,512]{1,0:T(8,128)S(1)}, f32[256,512]{1,0:T(8,128)S(1)}, bf16[512,512]{1,0:T(8,128)(2,1)S(1)}, bf16[512,512]{1,0:T(8,128)(2,1)S(1)}, b...) custom-call(f32[512,256]{1,0:T(8,128)S(1)} %get-tuple-element.96.u_ref, ...), custom_call_target="tpu_custom_call" | custom-call | flops 805306368 | bytes 6324224 | tf_op jit(solution)/shard_map/group_second/pallas_call | solution.py:189
  64.9 0.1 collective-permute-start.6
  65.0 0.1 collective-permute-start.7
  65.1 1.8 %users_last.1 = (f32[512,256]{1,0:T(8,128)}, f32[512,256]{1,0:T(8,128)}) custom-call(f32[512,256]{1,0:T(8,128)S(1)} %get-tuple-element.96.u_ref, f32[512,256]{1,0:T(8,128)S(1)} %get-tuple-element.97.um_ref, bf16[512,512]{1,0:T(8,128)(2,1)S(1)} %get-tuple-element.100.gh_ref, bf16[512,512]{1,0:T(8,128)(2,1)S(1)} %get-tuple-element.101.gl_ref, ...), custom_call_target="tpu_custom_call" | custom-call | flops 402653184 | bytes 3670016 | tf_op jit(solution)/shard_map/users_last/pallas_call | solution.py:189
  66.8 10.5 %collective-permute-done.6.xt_ref = f32[256,512]{1,0:T(8,128)S(1)} collective-permute-done((f32[256,512]{1,0:T(8,128)S(1)}, f32[256,512]{1,0:T(8,128)S(1)}, u32[]{:S(2)}, u32[]{:S(2)}) %collective-permute-start.6) | collective-permute-done | bytes 524320 | tf_op jit(solution)/shard_map/ppermute | solution.py:235
  77.4 0.9 %ads_out.2 = f32[512,256]{1,0:T(8,128)} custom-call(f32[256,512]{1,0:T(8,128)S(1)} %collective-permute-done.6.xt_ref), custom_call_target="tpu_custom_call" | custom-call | bytes 1048576 | tf_op jit(solution)/shard_map/ads_out/pallas_call | solution.py:216
  78.3 8.6 %collective-permute-done.7.xt_ref = f32[256,512]{1,0:T(8,128)S(1)} collective-permute-done((f32[256,512]{1,0:T(8,128)S(1)}, f32[256,512]{1,0:T(8,128)S(1)}, u32[]{:S(2)}, u32[]{:S(2)}) %collective-permute-start.7) | collective-permute-done | bytes 524320 | tf_op jit(solution)/shard_map/ppermute | solution.py:235
  86.9 0.9 %ads_out.3 = f32[512,256]{1,0:T(8,128)} custom-call(f32[256,512]{1,0:T(8,128)S(1)} %collective-permute-done.7.xt_ref), custom_call_target="tpu_custom_call" | custom-call | bytes 1048576 | tf_op jit(solution)/shard_map/ads_out/pallas_call | solution.py:216
Async XLA Ops:
  6.1 12.3 %collective-permute-start = (f32[256,512]{1,0:T(8,128)S(1)}, f32[256,512]{1,0:T(8,128)S(1)}, u32[]{:S(2)}, u32[]{:S(2)}) collective-permute-start(f32[256,512]{1,0:T(8,128)S(1)} %get-tuple-element.64), channel_id=1, source_target_pairs={{0,16},{1,17},{2,18},{3,19},{4,20},{5,21},{6,22},{7,23},{8,24},{9,... | collective-permute-start | bytes 1572872 | tf_op jit(solution)/shard_map/ppermute | solution.py:235
  6.2 17.8 %collective-permute-start.1 = (f32[256,512]{1,0:T(8,128)S(1)}, f32[256,512]{1,0:T(8,128)S(1)}, u32[]{:S(2)}, u32[]{:S(2)}) collective-permute-start(f32[256,512]{1,0:T(8,128)S(1)} %get-tuple-element.70), channel_id=1, source_target_pairs={{0,16},{1,17},{2,18},{3,19},{4,20},{5,21},{6,22},{7,23},{8,24},{9,... | collective-permute-start | bytes 1572872 | tf_op jit(solution)/shard_map/ppermute | solution.py:235
  25.8 12.0 %collective-permute-start.2 = (f32[256,512]{1,0:T(8,128)S(1)}, f32[256,512]{1,0:T(8,128)S(1)}, u32[]{:S(2)}, u32[]{:S(2)}) collective-permute-start(f32[256,512]{1,0:T(8,128)S(1)} %get-tuple-element.78), channel_id=1, source_target_pairs={{0,24},{1,25},{2,26},{3,27},{4,28},{5,29},{6,30},{7,31},{8,16},{9,... | collective-permute-start | bytes 1572872 | tf_op jit(solution)/shard_map/ppermute | solution.py:235
  25.9 17.5 %collective-permute-start.3 = (f32[256,512]{1,0:T(8,128)S(1)}, f32[256,512]{1,0:T(8,128)S(1)}, u32[]{:S(2)}, u32[]{:S(2)}) collective-permute-start(f32[256,512]{1,0:T(8,128)S(1)} %get-tuple-element.84), channel_id=1, source_target_pairs={{0,24},{1,25},{2,26},{3,27},{4,28},{5,29},{6,30},{7,31},{8,16},{9,... | collective-permute-start | bytes 1572872 | tf_op jit(solution)/shard_map/ppermute | solution.py:235
  45.2 12.3 %collective-permute-start.4 = (f32[256,512]{1,0:T(8,128)S(1)}, f32[256,512]{1,0:T(8,128)S(1)}, u32[]{:S(2)}, u32[]{:S(2)}) collective-permute-start(f32[256,512]{1,0:T(8,128)S(1)} %get-tuple-element.92), channel_id=1, source_target_pairs={{0,16},{1,17},{2,18},{3,19},{4,20},{5,21},{6,22},{7,23},{8,24},{9,... | collective-permute-start | bytes 1572872 | tf_op jit(solution)/shard_map/ppermute | solution.py:235
  45.3 17.8 %collective-permute-start.5 = (f32[256,512]{1,0:T(8,128)S(1)}, f32[256,512]{1,0:T(8,128)S(1)}, u32[]{:S(2)}, u32[]{:S(2)}) collective-permute-start(f32[256,512]{1,0:T(8,128)S(1)} %get-tuple-element.98), channel_id=1, source_target_pairs={{0,16},{1,17},{2,18},{3,19},{4,20},{5,21},{6,22},{7,23},{8,24},{9,... | collective-permute-start | bytes 1572872 | tf_op jit(solution)/shard_map/ppermute | solution.py:235
  64.9 12.5 %collective-permute-start.6 = (f32[256,512]{1,0:T(8,128)S(1)}, f32[256,512]{1,0:T(8,128)S(1)}, u32[]{:S(2)}, u32[]{:S(2)}) collective-permute-start(f32[256,512]{1,0:T(8,128)S(1)} %get-tuple-element.106), channel_id=1, source_target_pairs={{0,216},{1,217},{2,218},{3,219},{4,220},{5,221},{6,222},{7,223},{8... | collective-permute-start | bytes 1572872 | tf_op jit(solution)/shard_map/ppermute | solution.py:235
  65.0 21.9 %collective-permute-start.7 = (f32[256,512]{1,0:T(8,128)S(1)}, f32[256,512]{1,0:T(8,128)S(1)}, u32[]{:S(2)}, u32[]{:S(2)}) collective-permute-start(f32[256,512]{1,0:T(8,128)S(1)} %get-tuple-element.107), channel_id=1, source_target_pairs={{0,216},{1,217},{2,218},{3,219},{4,220},{5,221},{6,222},{7,223},{8... | collective-permute-start | bytes 1572872 | tf_op jit(solution)/shard_map/ppermute | solution.py:235

commit v2 on v1

--- a/solution.py
+++ b/solution.py
@@ -1,5 +1,4 @@
 import functools
-import math
 
 import jax
 import jax.numpy as jnp
@@ -61,13 +60,13 @@
 BLOCK = 256
 
 
-def group_pass(group, u_ref, at_hl, prep, gu_out, g_out=None):
+def group_pass(group, u_read, users, at_hl, prep, gu_out, g_out=None):
     mh_ref, cu_ref, cn_ref = prep
     cn = cn_ref[group, 0:1, :]
     ga = None
-    for r in range(0, u_ref.shape[0], BLOCK):
+    for r in range(0, users, BLOCK):
         rows = pl.ds(r, BLOCK)
-        u_hl = split(u_ref[rows, :])
+        u_hl = split(u_read(rows))
         g_hl = gradient_matrix(u_hl, at_hl, mh_ref[group, rows, :], cu_ref[group, rows, :], cn)
         part = dot3(u_hl, g_hl, 0, 0)
         ga = part if ga is None else ga + part
@@ -78,15 +77,30 @@
     return ga
 
 
-def update_users(u_ref, um_ref, uo_ref, umo_ref):
+def reader(ref):
+    return lambda rows: ref[rows, :]
+
+
+def picker(odd, even_ref, odd_ref):
+    return lambda rows: jnp.where(odd, odd_ref[rows, :], even_ref[rows, :])
+
+
+def update_users(u_read, um_read, uo_ref, umo_ref):
     def put(rows, grad):
-        uo_ref[rows, :], umo_ref[rows, :] = adagrad(u_ref[rows, :], um_ref[rows, :], grad)
+        uo_ref[rows, :], umo_ref[rows, :] = adagrad(u_read(rows), um_read(rows), grad)
 
     return put
 
 
-def fetch_indices(pu_hbm, pa_hbm, ng_hbm, pu, pa, ng, sems):
+def on_odd_core():
+    return lax.rem(lax.axis_index("blk"), 2) == 1
+
+
+def fetch_indices(pu_hbm, pa_hbm, ng_hbm, pu, pa, ng, sems, away=False):
     cycle = lax.axis_index("pair")
+    if away:
+        count = lax.axis_size("pair")
+        cycle = lax.rem(cycle + jnp.where(on_odd_core(), count // 2, 0), count)
     copies = [
         pltpu.make_async_copy(src.at[0, cycle], dst, sems.at[k])
         for k, (src, dst) in enumerate(((pu_hbm, pu), (pa_hbm, pa), (ng_hbm, ng)))
@@ -107,7 +121,7 @@
 def second_group(u_ref, at1, amt1, ato_ref, amto_ref, prep, gh_ref, gl_ref, ah_ref, al_ref):
     at_hl = split(at1)
     ah_ref[...], al_ref[...] = at_hl
-    ga = group_pass(1, u_ref, at_hl, prep, None, (gh_ref, gl_ref))
+    ga = group_pass(1, reader(u_ref), u_ref.shape[0], at_hl, prep, None, (gh_ref, gl_ref))
     ato_ref[...], amto_ref[...] = adagrad(at1, amt1, ga)
 
 
@@ -133,14 +147,17 @@
         c.wait()
     at = a_ref[...].T
     amt = am_ref[...].T
-    ga = group_pass(0, u_ref, split(at), prep, update_users(u_ref, um_ref, uo_ref, umo_ref))
+    put = update_users(reader(u_ref), reader(um_ref), uo_ref, umo_ref)
+    ga = group_pass(0, reader(u_ref), u_ref.shape[0], split(at), prep, put)
     at1, amt1 = adagrad(at, amt, ga)
     second_group(uo_ref, at1, amt1, ato_ref, amto_ref, prep, gh_ref, gl_ref, ah_ref, al_ref)
 
 
-def embedding_kernel(u_ref, um_ref, at_ref, mh, cu, cn, uo_ref, umo_ref, ga_ref):
-    put = update_users(u_ref, um_ref, uo_ref, umo_ref)
-    ga_ref[...] = group_pass(0, u_ref, split(at_ref[...]), (mh, cu, cn), put)
+def embedding_kernel(u_ref, um_ref, at_ref, mh, cu, cn, *refs):
+    uo_ref, umo_ref, ga_ref = refs[-3:]
+    u_read = reader(u_ref)
+    put = update_users(u_read, reader(um_ref), uo_ref, umo_ref)
+    ga_ref[...] = group_pass(0, u_read, u_ref.shape[0], split(at_ref[...]), (mh, cu, cn), put)
 
 
 def moment_kernel(
@@ -151,27 +168,65 @@
     second_group(u_ref, at1, amt1, ato_ref, amto_ref, (mh, cu, cn), gh_ref, gl_ref, ah_ref, al_ref)
 
 
-def users_body(u_ref, um_ref, gh_ref, gl_ref, ah_ref, al_ref, uo_ref, umo_ref):
-    put = update_users(u_ref, um_ref, uo_ref, umo_ref)
+def moment_pair_kernel(u_ref, at_ref, amt_ref, ga_ref, mh, cu, cn, ads_ref, *parts):
+    moment_kernel(u_ref, at_ref, amt_ref, ga_ref, mh, cu, cn, ads_ref.at[0], ads_ref.at[1], *parts)
+
+
+def embedding_pick_kernel(ue_ref, ume_ref, users_ref, ads_ref, ato_ref, mh, cu, cn, un_ref, umn_ref, ga_ref):
+    odd = on_odd_core()
+    u_read = picker(odd, ue_ref, users_ref.at[0])
+    put = update_users(u_read, picker(odd, ume_ref, users_ref.at[1]), un_ref, umn_ref)
+    at = jnp.where(odd, ato_ref[...], ads_ref[0])
+    ga_ref[...] = group_pass(0, u_read, ue_ref.shape[0], split(at), (mh, cu, cn), put)
+
+
+def moment_pick_kernel(
+    u_ref, ads_ref, ato_ref, amto_ref, ga_ref, mh, cu, cn,
+    atn_ref, amtn_ref, gh_ref, gl_ref, ah_ref, al_ref,
+):
+    odd = on_odd_core()
+    at = jnp.where(odd, ato_ref[...], ads_ref[0])
+    amt = jnp.where(odd, amto_ref[...], ads_ref[1])
+    at1, amt1 = adagrad(at, amt, ga_ref[...])
+    second_group(u_ref, at1, amt1, atn_ref, amtn_ref, (mh, cu, cn), gh_ref, gl_ref, ah_ref, al_ref)
+
+
+def gradient_kernel(u_ref, at_ref, mh, cu, cn, gu_ref, ga_ref):
+    def put(rows, grad):
+        gu_ref[rows, :] = grad
+
+    ga_ref[...] = group_pass(0, reader(u_ref), u_ref.shape[0], split(at_ref[...]), (mh, cu, cn), put)
+
+
+def both_moments_kernel(
+    u_ref, um_ref, at_ref, amt_ref, gu_ref, ga_ref, mh, cu, cn,
+    uo_ref, umo_ref, ato_ref, amto_ref, gh_ref, gl_ref, ah_ref, al_ref,
+):
+    uo_ref[...], umo_ref[...] = adagrad(u_ref[...], um_ref[...], gu_ref[...])
+    at1, amt1 = adagrad(at_ref[...], amt_ref[...], ga_ref[...])
+    second_group(uo_ref, at1, amt1, ato_ref, amto_ref, (mh, cu, cn), gh_ref, gl_ref, ah_ref, al_ref)
+
+
+def users_kernel(u_ref, um_ref, gh_ref, gl_ref, ah_ref, al_ref, uo_ref, umo_ref):
+    put = update_users(reader(u_ref), reader(um_ref), uo_ref, umo_ref)
     at_hl = ah_ref[...], al_ref[...]
     for r in range(0, u_ref.shape[0], BLOCK):
         rows = pl.ds(r, BLOCK)
         put(rows, dot3((gh_ref[rows, :], gl_ref[rows, :]), at_hl, 1, 1))
 
 
-def users_kernel(
-    rnd, u_ref, um_ref, gh_ref, gl_ref, ah_ref, al_ref, pu_hbm, pa_hbm, ng_hbm,
-    uo_ref, umo_ref, mh, cu, cn, pu, pa, ng, sems,
-):
-    copies = fetch_indices(pu_hbm, pa_hbm, ng_hbm, pu, pa, ng, sems)
-    users_body(u_ref, um_ref, gh_ref, gl_ref, ah_ref, al_ref, uo_ref, umo_ref)
-    for c in copies:
-        c.wait()
-    prepare_round(rnd, pu, pa, ng, u_ref.shape[0], ah_ref.shape[1], (mh, cu, cn))
+def users_pair_kernel(u_ref, um_ref, gh_ref, gl_ref, ah_ref, al_ref, users_ref):
+    users_kernel(u_ref, um_ref, gh_ref, gl_ref, ah_ref, al_ref, users_ref.at[0], users_ref.at[1])
+
+
+def prepare_kernel(rnd, away, after_ref, pu_hbm, pa_hbm, ng_hbm, mh, cu, cn, pu, pa, ng, sems):
+    for c in (copies := fetch_indices(pu_hbm, pa_hbm, ng_hbm, pu, pa, ng, sems, away)):
+        c.wait()
+    prepare_round(rnd, pu, pa, ng, mh.shape[1], mh.shape[2], (mh, cu, cn))
 
 
 def last_users_kernel(u_ref, um_ref, gh_ref, gl_ref, ah_ref, al_ref, uo_hbm, umo_hbm, uo_ref, umo_ref, sems):
-    users_body(u_ref, um_ref, gh_ref, gl_ref, ah_ref, al_ref, uo_ref, umo_ref)
+    users_kernel(u_ref, um_ref, gh_ref, gl_ref, ah_ref, al_ref, uo_ref, umo_ref)
     copies = [
         pltpu.make_async_copy(uo_ref, uo_hbm, sems.at[0]),
         pltpu.make_async_copy(umo_ref, umo_hbm, sems.at[1]),
@@ -182,20 +237,20 @@
         c.wait()
 
 
-def call(kernel, ins, outs, scratch=(), hbm=0, macs=0, name=None, out_place=pltpu.VMEM):
+def call(kernel, ins, outs, scratch=(), hbm=0, name=None, out_place=pltpu.VMEM):
     vmem = pl.BlockSpec(memory_space=pltpu.VMEM)
-    places = [vmem] * (len(ins) - hbm) + [pl.BlockSpec(memory_space=pltpu.HBM)] * hbm
-    size = sum(math.prod(x.shape) * x.dtype.itemsize for x in [*ins[: len(ins) - hbm], *outs])
+    split_at = len(ins) - hbm
+    far = [pltpu.with_memory_space_constraint(x, pltpu.HBM) for x in ins[split_at:]]
     return pl.pallas_call(
         kernel,
         out_shape=outs,
-        in_specs=places,
+        in_specs=[vmem] * split_at + [pl.BlockSpec(memory_space=pltpu.HBM)] * hbm,
         out_specs=[pl.BlockSpec(memory_space=out_place)] * len(outs),
         scratch_shapes=list(scratch),
         compiler_params=pltpu.CompilerParams(vmem_limit_bytes=VMEM_LIMIT),
-        cost_estimate=pl.CostEstimate(flops=2 * macs, bytes_accessed=size, transcendentals=0),
+        cost_estimate=pl.CostEstimate(flops=1, bytes_accessed=1, transcendentals=0),
         name=name,
-    )(*ins[: len(ins) - hbm], *(pltpu.with_memory_space_constraint(x, pltpu.HBM) for x in ins[len(ins) - hbm :]))
+    )(*ins[:split_at], *far)
 
 
 def finish_kernel(xt_ref, out_hbm, x_ref, sems):
@@ -225,17 +280,18 @@
     )(xt)
 
 
-def move(x, steps, flip):
+def move(arrays, even, odd):
     blocks, cycles = lax.axis_size("blk"), lax.axis_size("pair")
     route = []
     for b in range(blocks):
         for p in range(cycles):
+            steps, flip = odd if b % 2 else even
             to = (b + steps) % blocks, p ^ (cycles // 2 if flip else 0)
             route.append((b * cycles + p, to[0] * cycles + to[1]))
-    return lax.ppermute(x, AXES, route)
-
-
-def local(users, user_moms, ads, ad_moms, pos_user, pos_ad, neg_ad):
+    return tuple(lax.ppermute(x, AXES, route) for x in arrays)
+
+
+def local(users, user_moms, ads, ad_moments, pos_user, pos_ad, neg_ad):
     nu, d = users.shape
     na = ads.shape[0]
     rounds, groups, n = neg_ad.shape[2:]
@@ -246,7 +302,7 @@
         return jax.ShapeDtypeStruct(dims, dtype)
 
     table_u, table_a = shape(nu, d), shape(d, na)
-    part_g, part_a = shape(nu, na, dtype=BF16), shape(d, na, dtype=BF16)
+    parts = [shape(nu, na, dtype=BF16)] * 2 + [shape(d, na, dtype=BF16)] * 2
     index_scratch = [
         pltpu.VMEM((rounds, edges), jnp.int32),
         pltpu.VMEM((rounds, edges), jnp.int32),
@@ -255,39 +311,74 @@
     sems = pltpu.SemaphoreType.DMA((3,))
     prep_shapes = [shape(groups, nu, na, dtype=BF16), shape(groups, nu, 128), shape(groups, 8, na)]
     prep_scratch = [pltpu.VMEM(s.shape, s.dtype) for s in prep_shapes]
-    product = 3 * nu * na * d
+
+    def prepare_for(rnd, away, after):
+        return call(
+            functools.partial(prepare_kernel, rnd, away), (after, *indices), prep_shapes,
+            [*index_scratch, sems], hbm=3, name="counts",
+        )
+
+    def first_group(u, um, at, prep, *after):
+        return call(embedding_kernel, (u, um, at, *prep, *after), [table_u, table_u, table_a], name="group_first")
+
+    def second_group_of(u, at, amt, ga, prep):
+        at, amt, *g = call(moment_kernel, (u, at, amt, ga, *prep), [table_a, table_a, *parts], name="group_second")
+        return (at, amt), g
+
+    def update(u, um, g):
+        return call(users_kernel, (u, um, *g), [table_u, table_u], name="users_update")
 
     u, um, at, amt, *g = call(
         first_round_kernel,
-        (*indices, users, ads, user_moms, ad_moms),
-        [table_u, table_u, table_a, table_a, part_g, part_g, part_a, part_a],
+        (*indices, users, ads, user_moms, ad_moments),
+        [table_u, table_u, table_a, table_a, *parts],
         [*index_scratch, *prep_scratch, *[pltpu.VMEM((nu, d), F32)] * 2, *[pltpu.VMEM((na, d), F32)] * 2, sems, pltpu.SemaphoreType.DMA((4,))],
-        hbm=7, macs=5 * product, name="round_first",
-    )
-    for rnd in range(1, rounds):
-        flip = rnd == rounds // 2
-        at = move(at, 1, flip)
-        amt = move(amt, 1, flip)
-        u, um, *prep = call(
-            functools.partial(users_kernel, rnd),
-            (u, um, *g, *indices),
-            [table_u, table_u, *prep_shapes],
-            [*index_scratch, sems], hbm=3, macs=product, name="users_prepare",
-        )
-        u, um, ga = call(
-            embedding_kernel, (u, um, at, *prep), [table_u, table_u, table_a], macs=3 * product, name="group_first",
-        )
-        at, amt, *g = call(
-            moment_kernel, (u, at, amt, ga, *prep), [table_a, table_a, part_g, part_g, part_a, part_a],
-            macs=2 * product, name="group_second",
-        )
-    a = finish(move(at, 1 - rounds, True))
-    am = finish(move(amt, 1 - rounds, True))
+        hbm=7, name="round_first",
+    )
+    near = move((at, amt), (1, False), (-1, False))
+    far = move((at, amt), (1, False), (1, False))
+    u, um = update(u, um, g)
+    prep = prepare_for(1, False, um)
+
+    u_early, um_early, ga = first_group(u, um, near[0], prep)
+    ads_early, *g = call(
+        moment_pair_kernel, (u_early, *near, ga, *prep), [shape(2, d, na), *parts], name="group_second_pair",
+    )
+    (ads_early,) = move((ads_early,), (1, False), (1, True))
+    (after,) = call(users_pair_kernel, (u_early, um_early, *g), [shape(2, nu, d)], name="users_update_pair")
+    (users_early,) = move((after,), (0, False), (0, True))
+
+    u, um, ga = first_group(u, um, far[0], prep, after)
+    ads_late, g = second_group_of(u, *far, ga, prep)
+    ads_late = move(ads_late, (1, False), (-1, False))
+    u, um = update(u, um, g)
+    prep = prepare_for(2, True, um)
+
+    u, um, ga = call(
+        embedding_pick_kernel, (u, um, users_early, ads_early, ads_late[0], *prep), [table_u, table_u, table_a],
+        name="group_first_pick",
+    )
+    at, amt, *g = call(
+        moment_pick_kernel, (u, ads_early, *ads_late, ga, *prep),
+        [table_a, table_a, *parts], name="group_second_pick",
+    )
+    at, amt = move((at, amt), (1, False), (1, True))
+    u, um = update(u, um, g)
+    after = um
+    u, um = move((u, um), (0, False), (0, True))
+    prep = prepare_for(3, False, after)
+
+    gu, ga = call(gradient_kernel, (u, at, *prep), [table_u, table_a], name="group_first_gradients")
+    u, um, at, amt, *g = call(
+        both_moments_kernel, (u, um, at, amt, gu, ga, *prep), [table_u, table_u, table_a, table_a, *parts],
+        name="group_second_both",
+    )
+    at, amt = move((at, amt), (1 - rounds, True), (1 - rounds, True))
     u, um = call(
         last_users_kernel, (u, um, *g), [pltpu.HBM((nu, d), F32)] * 2,
-        [pltpu.VMEM((nu, d), F32)] * 2 + [pltpu.SemaphoreType.DMA((2,))], macs=product, name="users_last", out_place=pltpu.HBM,
-    )
-    return u, um, a, am
+        [pltpu.VMEM((nu, d), F32)] * 2 + [pltpu.SemaphoreType.DMA((2,))], name="users_last", out_place=pltpu.HBM,
+    )
+    return u, um, finish(at), finish(amt)
 
 
 def solution(mesh):

time: 89.3 us -> 87.4 us (0.979)
  waiting for transfers between devices: 55.7 us -> 41.6 us
  starting transfers between devices: 4.53 us -> 10.6 us
  Pallas kernels: 26.8 us -> 32.7 us
    ppermute x8 -> x14, waiting for transfers between devices: 55.7 us -> 41.6 us  [move(): return tuple((lax.ppermute(x, AXES, route) for x in arrays))]
    ppermute x8 -> x14, starting transfers between devices: 4.53 us -> 10.6 us  [move(): return tuple((lax.ppermute(x, AXES, route) for x in arrays))]
    pallas_call x11 -> x17, Pallas kernels: 25 us -> 30.9 us  [call(): pl.pallas_call(kernel, out_shape=outs, in_specs=[vmem] * split_at + [pl.B...]
  transfers between devices with their start and end apart: 8 -> 14, of which waited for: 8 -> 6; matrix products, arithmetic and copies ran while one was open for 0% -> 0% of each run, Pallas kernels for 17% -> 25%
where the time goes in v2:
time: 87.4 us; the launch traced here: 86 us
  waiting for transfers between devices  41.6 us (48%)
  Pallas kernels  32.7 us (37%)
  starting transfers between devices  10.6 us (12%)
  between operations  1.07 us (1%)
    ppermute x14, waiting for transfers between devices, move(): return tuple((lax.ppermute(x, AXES, route) for x in arrays))  41.6 us
    pallas_call x17, Pallas kernels, call(): pl.pallas_call(kernel, out_shape=outs, in_specs=[vmem] * split_at + [pl.B...  30.9 us
    ppermute x14, starting transfers between devices, move(): return tuple((lax.ppermute(x, AXES, route) for x in arrays))  10.6 us
    pallas_call x2, Pallas kernels, finish(): pl.pallas_call(finish_kernel, out_shape=pltpu.HBM((rows, d), xt.dtype), i...  1.84 us
  transfers between devices with their start and end apart: 14, of which 6 were waited for; matrix products, arithmetic and copies ran while one was open for 0% of the time, Pallas kernels for 25%

profile of v2, /device:TPU:192, one launch (start us, length us, event | category | flops | bytes accessed | tf_op | source)
XLA Modules:
  0.0 86.0 jit_solution(11161193808798581957)
XLA Ops:
  0.6 5.4 %round_first.1 = (f32[512,256]{1,0:T(8,128)S(1)}, f32[512,256]{1,0:T(8,128)S(1)}, f32[256,512]{1,0:T(8,128)S(1)}, f32[256,512]{1,0:T(8,128)S(1)}, bf16[512,512]{...) custom-call(s32[1,16,4,512]{3,2,1,0:T(4,128)} %pu_hbm.7, ...), custom_call_target="tpu_custom_call" | custom-call | flops 1 | bytes 1 | tf_op jit(solution)/shard_map/round_first/pallas_call | solution.py:244
  6.1 0.1 collective-permute-start.1
  6.2 0.5 collective-permute-start.2
  6.7 0.1 collective-permute-start
  6.8 3.2 %collective-permute-start.3 = (f32[256,512]{1,0:T(8,128)S(1)}, f32[256,512]{1,0:T(8,128)S(1)}, u32[]{:S(2)}, u32[]{:S(2)}) collective-permute-start(f32[256,512]{1,0:T(8,128)S(1)} %get-tuple-element.79), channel_id=1, source_target_pairs={{0,16},{1,17},{2,18},{3,19},{4,20},{5,21},{6,22},{7,23},{8,24},{9,... | collective-permute-start | bytes 1572872 | tf_op jit(solution)/shard_map/ppermute | solution.py:291
  10.0 0.8 users_update.3
  10.8 1.6 %counts.3 = (bf16[2,512,512]{2,1,0:T(8,128)(2,1)S(1)}, f32[2,512,128]{2,1,0:T(8,128)S(1)}, f32[2,8,512]{2,1,0:T(8,128)S(1)}) custom-call(f32[512,256]{1,0:T(8,128)S(1)} %get-tuple-element.72.after_ref.um_ref, s32[1,16,4,512]{3,2,1,0:T(4,128)} %pu_hbm.7, s32[1,16,4,512]{3,2,1,0:T(4,128)} %pa_hbm.7, s32[1,16,4,2,512]{4,3,2,1,0:T(2,128)} %ng_hbm.7), custom_call_target="tpu_custom_call" | custom-call | flops 1 | bytes 1 | tf_op jit(solution)/shard_map/counts/pallas_call | solution.py:244
  12.4 0.0 collective-permute-done.1.at_ref
  12.4 2.1 %group_first.2 = (f32[512,256]{1,0:T(8,128)S(1)}, f32[512,256]{1,0:T(8,128)S(1)}, f32[256,512]{1,0:T(8,128)S(1)}) custom-call(f32[512,256]{1,0:T(8,128)S(1)} %get-tuple-element.71.u_ref, f32[512,256]{1,0:T(8,128)S(1)} %get-tuple-element.72.after_ref.um_ref, f32[256,512]{1,0:T(8,128)S(1)} %collective-permute-done.1.at_ref, ...), custom_call_target="tpu_custom_call" | custom-call | flops 1 | bytes 1 | tf_op jit(solution)/shard_map/group_first/pallas_call | solution.py:244
  14.5 0.0 collective-permute-done.2.amt_ref
  14.5 1.8 %group_second_pair.1 = (f32[2,256,512]{2,1,0:T(8,128)S(1)}, bf16[512,512]{1,0:T(8,128)(2,1)S(1)}, bf16[512,512]{1,0:T(8,128)(2,1)S(1)}, bf16[256,512]{1,0:T(8,128)(2,1)S(1)}, bf16[256,512]{1,0:T(8,128)(2,1)S(1)}) custom-call(f32[512,256]{1,0:T(8,128)S(1)} %get-tuple-element.77.u_ref, f32[256,512]{1,0:T(8,128)S(1)} %collective-permute-done.1.at_ref, ...), custom_call_target="tpu_custom_call" | custom-call | flops 1 | bytes 1 | tf_op jit(solution)/shard_map/group_second_pair/pallas_call | solution.py:244
  16.3 0.8 users_update_pair.1.refs_0_
  17.1 0.7 collective-permute-start.4
  17.9 1.9 %collective-permute-start.5 = (f32[2,256,512]{2,1,0:T(8,128)S(1)}, f32[2,256,512]{2,1,0:T(8,128)S(1)}, u32[]{:S(2)}, u32[]{:S(2)}) collective-permute-start(f32[2,256,512]{2,1,0:T(8,128)S(1)} %get-tuple-element.94), channel_id=1, source_target_pairs={{0,16},{1,17},{2,18},{3,19},{4,20},{5,21},{6,22},{7,23},{8,24},{9,... | collective-permute-start | bytes 3145736 | tf_op jit(solution)/shard_map/ppermute | solution.py:291
  19.8 0.0 collective-permute-done.at_ref
  19.8 2.1 %group_first.3 = (f32[512,256]{1,0:T(8,128)S(1)}, f32[512,256]{1,0:T(8,128)S(1)}, f32[256,512]{1,0:T(8,128)S(1)}) custom-call(f32[512,256]{1,0:T(8,128)S(1)} %get-tuple-element.71.u_ref, f32[512,256]{1,0:T(8,128)S(1)} %get-tuple-element.72.after_ref.um_ref, f32[256,512]{1,0:T(8,128)S(1)} %collective-permute-done.at_ref, ...), custom_call_target="tpu_custom_call" | custom-call | flops 1 | bytes 1 | tf_op jit(solution)/shard_map/group_first/pallas_call | solution.py:244
  21.9 2.7 %collective-permute-done.3.amt_ref = f32[256,512]{1,0:T(8,128)S(1)} collective-permute-done((f32[256,512]{1,0:T(8,128)S(1)}, f32[256,512]{1,0:T(8,128)S(1)}, u32[]{:S(2)}, u32[]{:S(2)}) %collective-permute-start.3) | collective-permute-done | bytes 524320 | tf_op jit(solution)/shard_map/ppermute | solution.py:291
  24.6 1.8 %group_second.1 = (f32[256,512]{1,0:T(8,128)S(1)}, f32[256,512]{1,0:T(8,128)S(1)}, bf16[512,512]{1,0:T(8,128)(2,1)S(1)}, bf16[512,512]{1,0:T(8,128)(2,1)S(1)}, b...) custom-call(f32[512,256]{1,0:T(8,128)S(1)} %get-tuple-element.85.u_ref, ...), custom_call_target="tpu_custom_call" | custom-call | flops 1 | bytes 1 | tf_op jit(solution)/shard_map/group_second/pallas_call | solution.py:244
  26.4 0.1 collective-permute-start.6
  26.5 0.5 collective-permute-start.7
  27.0 0.8 users_update.4
  27.8 1.6 %counts.4 = (bf16[2,512,512]{2,1,0:T(8,128)(2,1)S(1)}, f32[2,512,128]{2,1,0:T(8,128)S(1)}, f32[2,8,512]{2,1,0:T(8,128)S(1)}) custom-call(f32[512,256]{1,0:T(8,128)S(1)} %get-tuple-element.93.after_ref.ume_ref, s32[1,16,4,512]{3,2,1,0:T(4,128)} %pu_hbm.7, s32[1,16,4,512]{3,2,1,0:T(4,128)} %pa_hbm.7, s32[1,16,4,2,512]{4,3,2,1,0:T(2,128)} %ng_hbm.7), custom_call_target="tpu_custom_call" | custom-call | flops 1 | bytes 1 | tf_op jit(solution)/shard_map/counts/pallas_call | solution.py:244
  29.4 0.0 collective-permute-done.6.ato_ref
  29.4 0.0 collective-permute-done.4.users_ref
  29.4 7.1 %collective-permute-done.5.ads_ref = f32[2,256,512]{2,1,0:T(8,128)S(1)} collective-permute-done((f32[2,256,512]{2,1,0:T(8,128)S(1)}, f32[2,256,512]{2,1,0:T(8,128)S(1)}, u32[]{:S(2)}, u32[]{:S(2)}) %collective-permute-start.5) | collective-permute-done | bytes 1048608 | tf_op jit(solution)/shard_map/ppermute | solution.py:291
  36.5 2.2 %group_first_pick.1 = (f32[512,256]{1,0:T(8,128)S(1)}, f32[512,256]{1,0:T(8,128)S(1)}, f32[256,512]{1,0:T(8,128)S(1)}) custom-call(f32[512,256]{1,0:T(8,128)S(1)} %get-tuple-element.92.ue_ref, f32[512,256]{1,0:T(8,128)S(1)} %get-tuple-element.93.after_ref.ume_ref, f32[2,512,256]{2,1,0:T(8,128)S(1)} %collective-permute-done.4.users_ref, ...), custom_call_target="tpu_custom_call" | custom-call | flops 1 | bytes 1 | tf_op jit(solution)/shard_map/group_first_pick/pallas_call | solution.py:244
  38.7 0.0 collective-permute-done.7.amto_ref
  38.7 1.8 %group_second_pick.1 = (f32[256,512]{1,0:T(8,128)S(1)}, f32[256,512]{1,0:T(8,128)S(1)}, bf16[512,512]{1,0:T(8,128)(2,1)S(1)}, bf16[512,512]{1,0:T(8,128)(2,1)S(1...) custom-call(f32[512,256]{1,0:T(8,128)S(1)} %get-tuple-element.99.u_ref, ...), custom_call_target="tpu_custom_call" | custom-call | flops 1 | bytes 1 | tf_op jit(solution)/shard_map/group_second_pick/pallas_call | solution.py:244
  40.5 0.8 users_update.5
  41.3 0.7 collective-permute-start.8
  42.0 0.1 collective-permute-start.10
  42.1 0.7 collective-permute-start.9
  42.8 1.8 %collective-permute-start.11 = (f32[256,512]{1,0:T(8,128)S(1)}, f32[256,512]{1,0:T(8,128)S(1)}, u32[]{:S(2)}, u32[]{:S(2)}) collective-permute-start(f32[256,512]{1,0:T(8,128)S(1)} %get-tuple-element.110), channel_id=1, source_target_pairs={{0,16},{1,17},{2,18},{3,19},{4,20},{5,21},{6,22},{7,23},{8,24},{9,... | collective-permute-start | bytes 1572872 | tf_op jit(solution)/shard_map/ppermute | solution.py:291
  44.6 1.6 %counts.5 = (bf16[2,512,512]{2,1,0:T(8,128)(2,1)S(1)}, f32[2,512,128]{2,1,0:T(8,128)S(1)}, f32[2,8,512]{2,1,0:T(8,128)S(1)}) custom-call(f32[512,256]{1,0:T(8,128)S(1)} %get-tuple-element.108.after_ref, s32[1,16,4,512]{3,2,1,0:T(4,128)} %pu_hbm.7, s32[1,16,4,512]{3,2,1,0:T(4,128)} %pa_hbm.7, s32[1,16,4,2,512]{4,3,2,1,0:T(2,128)} %ng_hbm.7), custom_call_target="tpu_custom_call" | custom-call | flops 1 | bytes 1 | tf_op jit(solution)/shard_map/counts/pallas_call | solution.py:244
  46.2 0.0 collective-permute-done.8.u_ref
  46.2 7.8 %collective-permute-done.10.at_ref = f32[256,512]{1,0:T(8,128)S(1)} collective-permute-done((f32[256,512]{1,0:T(8,128)S(1)}, f32[256,512]{1,0:T(8,128)S(1)}, u32[]{:S(2)}, u32[]{:S(2)}) %collective-permute-start.10) | collective-permute-done | bytes 524320 | tf_op jit(solution)/shard_map/ppermute | solution.py:291
  54.0 2.0 %group_first_gradients.1 = (f32[512,256]{1,0:T(8,128)S(1)}, f32[256,512]{1,0:T(8,128)S(1)}) custom-call(f32[512,256]{1,0:T(8,128)S(1)} %collective-permute-done.8.u_ref, f32[256,512]{1,0:T(8,128)S(1)} %collective-permute-done.10.at_ref, bf16[2,512,512]{2,1,0:T(8,128)(2,1)S(1)} %get-tuple-element.111.mh, f32[2,512,128]{2,1,0:T(8,128)S(1)} %get-tuple-element.112.cu, ...), custom_call_target="tpu_custom_call" | custom-call | flops 1 | bytes 1 | tf_op jit(solution)/shard_map/group_first_gradients/pallas_call | solution.py:244
  56.0 0.0 collective-permute-done.9.um_ref
  56.0 3.6 %collective-permute-done.11.amt_ref = f32[256,512]{1,0:T(8,128)S(1)} collective-permute-done((f32[256,512]{1,0:T(8,128)S(1)}, f32[256,512]{1,0:T(8,128)S(1)}, u32[]{:S(2)}, u32[]{:S(2)}) %collective-permute-start.11) | collective-permute-done | bytes 524320 | tf_op jit(solution)/shard_map/ppermute | solution.py:291
  59.6 1.9 %group_second_both.1 = (f32[512,256]{1,0:T(8,128)S(1)}, f32[512,256]{1,0:T(8,128)S(1)}, f32[256,512]{1,0:T(8,128)S(1)}, f32[256,512]{1,0:T(8,128)S(1)}, bf16[512...) custom-call(f32[512,256]{1,0:T(8,128)S(1)} %collective-permute-done., ...), custom_call_target="tpu_custom_call" | custom-call | flops 1 | bytes 1 | tf_op jit(solution)/shard_map/group_second_both/pallas_call | solution.py:244
  61.6 0.1 collective-permute-start.12
  61.7 0.1 collective-permute-start.13
  61.8 1.8 %users_last.1 = (f32[512,256]{1,0:T(8,128)}, f32[512,256]{1,0:T(8,128)}) custom-call(f32[512,256]{1,0:T(8,128)S(1)} %get-tuple-element.116.u_ref, f32[512,256]{1,0:T(8,128)S(1)} %get-tuple-element.117.um_ref, bf16[512,512]{1,0:T(8,128)(2,1)S(1)} %get-tuple-element.118.gh_ref, bf16[512,512]{1,0:T(8,128)(2,1)S(1)} %get-tuple-element.119.gl_ref, ...), custom_call_target="tpu_custom_call" | custom-call | flops 1 | bytes 1 | tf_op jit(solution)/shard_map/users_last/pallas_call | solution.py:244
  63.5 10.4 %collective-permute-done.12.xt_ref = f32[256,512]{1,0:T(8,128)S(1)} collective-permute-done((f32[256,512]{1,0:T(8,128)S(1)}, f32[256,512]{1,0:T(8,128)S(1)}, u32[]{:S(2)}, u32[]{:S(2)}) %collective-permute-start.12) | collective-permute-done | bytes 524320 | tf_op jit(solution)/shard_map/ppermute | solution.py:291
  74.0 0.9 %ads_out.2 = f32[512,256]{1,0:T(8,128)} custom-call(f32[256,512]{1,0:T(8,128)S(1)} %collective-permute-done.12.xt_ref), custom_call_target="tpu_custom_call" | custom-call | bytes 1048576 | tf_op jit(solution)/shard_map/ads_out/pallas_call | solution.py:271
  74.9 10.0 %collective-permute-done.13.xt_ref = f32[256,512]{1,0:T(8,128)S(1)} collective-permute-done((f32[256,512]{1,0:T(8,128)S(1)}, f32[256,512]{1,0:T(8,128)S(1)}, u32[]{:S(2)}, u32[]{:S(2)}) %collective-permute-start.13) | collective-permute-done | bytes 524320 | tf_op jit(solution)/shard_map/ppermute | solution.py:291
  84.9 0.9 %ads_out.3 = f32[512,256]{1,0:T(8,128)} custom-call(f32[256,512]{1,0:T(8,128)S(1)} %collective-permute-done.13.xt_ref), custom_call_target="tpu_custom_call" | custom-call | bytes 1048576 | tf_op jit(solution)/shard_map/ads_out/pallas_call | solution.py:271
Async XLA Ops:
  6.1 6.3 %collective-permute-start.1 = (f32[256,512]{1,0:T(8,128)S(1)}, f32[256,512]{1,0:T(8,128)S(1)}, u32[]{:S(2)}, u32[]{:S(2)}) collective-permute-start(f32[256,512]{1,0:T(8,128)S(1)} %get-tuple-element.73), channel_id=1, source_target_pairs={{0,16},{1,17},{2,18},{3,19},{4,20},{5,21},{6,22},{7,23},{8,24},{9,... | collective-permute-start | bytes 1572872 | tf_op jit(solution)/shard_map/ppermute | solution.py:291
  6.2 8.4 %collective-permute-start.2 = (f32[256,512]{1,0:T(8,128)S(1)}, f32[256,512]{1,0:T(8,128)S(1)}, u32[]{:S(2)}, u32[]{:S(2)}) collective-permute-start(f32[256,512]{1,0:T(8,128)S(1)} %get-tuple-element.79), channel_id=1, source_target_pairs={{0,16},{1,17},{2,18},{3,19},{4,20},{5,21},{6,22},{7,23},{8,24},{9,... | collective-permute-start | bytes 1572872 | tf_op jit(solution)/shard_map/ppermute | solution.py:291
  6.7 13.1 %collective-permute-start = (f32[256,512]{1,0:T(8,128)S(1)}, f32[256,512]{1,0:T(8,128)S(1)}, u32[]{:S(2)}, u32[]{:S(2)}) collective-permute-start(f32[256,512]{1,0:T(8,128)S(1)} %get-tuple-element.73), channel_id=1, source_target_pairs={{0,16},{1,17},{2,18},{3,19},{4,20},{5,21},{6,22},{7,23},{8,24},{9,... | collective-permute-start | bytes 1572872 | tf_op jit(solution)/shard_map/ppermute | solution.py:291
  6.8 17.8 %collective-permute-start.3 = (f32[256,512]{1,0:T(8,128)S(1)}, f32[256,512]{1,0:T(8,128)S(1)}, u32[]{:S(2)}, u32[]{:S(2)}) collective-permute-start(f32[256,512]{1,0:T(8,128)S(1)} %get-tuple-element.79), channel_id=1, source_target_pairs={{0,16},{1,17},{2,18},{3,19},{4,20},{5,21},{6,22},{7,23},{8,24},{9,... | collective-permute-start | bytes 1572872 | tf_op jit(solution)/shard_map/ppermute | solution.py:291
  17.1 12.3 %collective-permute-start.4 = (f32[2,512,256]{2,1,0:T(8,128)S(1)}, f32[2,512,256]{2,1,0:T(8,128)S(1)}, u32[]{:S(2)}, u32[]{:S(2)}) collective-permute-start(f32[2,512,256]{2,1,0:T(8,128)S(1)} %users_update_pair.1.refs_0_), channel_id=1, source_target_pairs={{0,0},{1,1},{2,2},{3,3},{4,4},{5,5},{6,6},{7,7},{8,8},{9,9},{10,10... | collective-permute-start | bytes 3145736 | tf_op jit(solution)/shard_map/ppermute | solution.py:291
  17.9 18.6 %collective-permute-start.5 = (f32[2,256,512]{2,1,0:T(8,128)S(1)}, f32[2,256,512]{2,1,0:T(8,128)S(1)}, u32[]{:S(2)}, u32[]{:S(2)}) collective-permute-start(f32[2,256,512]{2,1,0:T(8,128)S(1)} %get-tuple-element.94), channel_id=1, source_target_pairs={{0,16},{1,17},{2,18},{3,19},{4,20},{5,21},{6,22},{7,23},{8,24},{9,... | collective-permute-start | bytes 3145736 | tf_op jit(solution)/shard_map/ppermute | solution.py:291
  26.4 3.0 %collective-permute-start.6 = (f32[256,512]{1,0:T(8,128)S(1)}, f32[256,512]{1,0:T(8,128)S(1)}, u32[]{:S(2)}, u32[]{:S(2)}) collective-permute-start(f32[256,512]{1,0:T(8,128)S(1)} %get-tuple-element.95), channel_id=1, source_target_pairs={{0,16},{1,17},{2,18},{3,19},{4,20},{5,21},{6,22},{7,23},{8,24},{9,... | collective-permute-start | bytes 1572872 | tf_op jit(solution)/shard_map/ppermute | solution.py:291
  26.5 12.2 %collective-permute-start.7 = (f32[256,512]{1,0:T(8,128)S(1)}, f32[256,512]{1,0:T(8,128)S(1)}, u32[]{:S(2)}, u32[]{:S(2)}) collective-permute-start(f32[256,512]{1,0:T(8,128)S(1)} %get-tuple-element.101), channel_id=1, source_target_pairs={{0,16},{1,17},{2,18},{3,19},{4,20},{5,21},{6,22},{7,23},{8,24},{9,... | collective-permute-start | bytes 1572872 | tf_op jit(solution)/shard_map/ppermute | solution.py:291
  41.3 4.9 %collective-permute-start.8 = (f32[512,256]{1,0:T(8,128)S(1)}, f32[512,256]{1,0:T(8,128)S(1)}, u32[]{:S(2)}, u32[]{:S(2)}) collective-permute-start(f32[512,256]{1,0:T(8,128)S(1)} %get-tuple-element.107), channel_id=1, source_target_pairs={{0,0},{1,1},{2,2},{3,3},{4,4},{5,5},{6,6},{7,7},{8,8},{9,9},{10,10... | collective-permute-start | bytes 1572872 | tf_op jit(solution)/shard_map/ppermute | solution.py:291
  42.0 12.0 %collective-permute-start.10 = (f32[256,512]{1,0:T(8,128)S(1)}, f32[256,512]{1,0:T(8,128)S(1)}, u32[]{:S(2)}, u32[]{:S(2)}) collective-permute-start(f32[256,512]{1,0:T(8,128)S(1)} %get-tuple-element.109), channel_id=1, source_target_pairs={{0,16},{1,17},{2,18},{3,19},{4,20},{5,21},{6,22},{7,23},{8,24},{9,... | collective-permute-start | bytes 1572872 | tf_op jit(solution)/shard_map/ppermute | solution.py:291
  42.1 13.9 %collective-permute-start.9 = (f32[512,256]{1,0:T(8,128)S(1)}, f32[512,256]{1,0:T(8,128)S(1)}, u32[]{:S(2)}, u32[]{:S(2)}) collective-permute-start(f32[512,256]{1,0:T(8,128)S(1)} %get-tuple-element.108.after_ref), channel_id=1, source_target_pairs={{0,0},{1,1},{2,2},{3,3},{4,4},{5,5},{6,6},{7,7},{8,8},{9,9},{10,10... | collective-permute-start | bytes 1572872 | tf_op jit(solution)/shard_map/ppermute | solution.py:291
  42.8 16.8 %collective-permute-start.11 = (f32[256,512]{1,0:T(8,128)S(1)}, f32[256,512]{1,0:T(8,128)S(1)}, u32[]{:S(2)}, u32[]{:S(2)}) collective-permute-start(f32[256,512]{1,0:T(8,128)S(1)} %get-tuple-element.110), channel_id=1, source_target_pairs={{0,16},{1,17},{2,18},{3,19},{4,20},{5,21},{6,22},{7,23},{8,24},{9,... | collective-permute-start | bytes 1572872 | tf_op jit(solution)/shard_map/ppermute | solution.py:291
  61.6 12.4 %collective-permute-start.12 = (f32[256,512]{1,0:T(8,128)S(1)}, f32[256,512]{1,0:T(8,128)S(1)}, u32[]{:S(2)}, u32[]{:S(2)}) collective-permute-start(f32[256,512]{1,0:T(8,128)S(1)} %get-tuple-element.124), channel_id=1, source_target_pairs={{0,216},{1,217},{2,218},{3,219},{4,220},{5,221},{6,222},{7,223},{8... | collective-permute-start | bytes 1572872 | tf_op jit(solution)/shard_map/ppermute | solution.py:291
  61.7 23.2 %collective-permute-start.13 = (f32[256,512]{1,0:T(8,128)S(1)}, f32[256,512]{1,0:T(8,128)S(1)}, u32[]{:S(2)}, u32[]{:S(2)}) collective-permute-start(f32[256,512]{1,0:T(8,128)S(1)} %get-tuple-element.125), channel_id=1, source_target_pairs={{0,216},{1,217},{2,218},{3,219},{4,220},{5,221},{6,222},{7,223},{8... | collective-permute-start | bytes 1572872 | tf_op jit(solution)/shard_map/ppermute | solution.py:291

commit v3 on v2

--- a/solution.py
+++ b/solution.py
@@ -11,6 +11,8 @@
 EPS = 1e-08
 F32 = jnp.float32
 BF16 = jnp.bfloat16
+LANES = 128
+PARTS_OUT = 4
 AXES = ("blk", "pair")
 VMEM_LIMIT = 28 * 1024 * 1024
 
@@ -46,7 +48,11 @@
     mh_ref[group] = (0.5 * dot(hot_u, hot_a, 1, 1)).astype(BF16)
     ones = jnp.ones((pu.shape[1], 128), BF16)
     cu_ref[group] = dot(hot_u, ones, 1, 0) * F32(0.5 / n**0.5)
-    cn_ref[group] = dot(jnp.ones((8, n), BF16), onehot(ng, ads), 1, 1)
+    hi = lax.shift_right_logical(ng, LANES.bit_length() - 1)
+    counts = dot(onehot(hi, 8), onehot(ng - hi * LANES, LANES), 1, 1)
+    for k in range(ads // LANES):
+        cols = pl.ds(k * LANES, LANES)
+        cn_ref[group, :, cols] = jnp.broadcast_to(counts[k : k + 1, :], (8, LANES))
 
 
 def gradient_matrix(u_hl, at_hl, mh, cu, cn):
@@ -108,6 +114,13 @@
     for c in copies:
         c.start()
     return copies
+
+
+def pack_lists(rnd, pu, pa, ng, lists_ref):
+    lists_ref[...] = jnp.zeros_like(lists_ref)
+    lists_ref[0:1, pl.ds(0, pu.shape[1])] = pu[rnd : rnd + 1, :]
+    lists_ref[1:2, pl.ds(0, pa.shape[1])] = pa[rnd : rnd + 1, :]
+    lists_ref[pl.ds(2, ng.shape[1]), pl.ds(0, ng.shape[2])] = ng[rnd]
 
 
 def prepare_round(rnd, pu, pa, ng, users, ads, prep):
@@ -168,8 +181,11 @@
     second_group(u_ref, at1, amt1, ato_ref, amto_ref, (mh, cu, cn), gh_ref, gl_ref, ah_ref, al_ref)
 
 
-def moment_pair_kernel(u_ref, at_ref, amt_ref, ga_ref, mh, cu, cn, ads_ref, *parts):
-    moment_kernel(u_ref, at_ref, amt_ref, ga_ref, mh, cu, cn, ads_ref.at[0], ads_ref.at[1], *parts)
+def early_kernel(u_ref, um_ref, at_ref, amt_ref, ga_ref, mh, cu, cn, ads_ref, users_ref):
+    at1, amt1 = adagrad(at_ref[...], amt_ref[...], ga_ref[...])
+    put = update_users(reader(u_ref), reader(um_ref), users_ref.at[0], users_ref.at[1])
+    ga = group_pass(1, reader(u_ref), u_ref.shape[0], split(at1), (mh, cu, cn), put)
+    ads_ref[0], ads_ref[1] = adagrad(at1, amt1, ga)
 
 
 def embedding_pick_kernel(ue_ref, ume_ref, users_ref, ads_ref, ato_ref, mh, cu, cn, un_ref, umn_ref, ga_ref):
@@ -181,14 +197,16 @@
 
 
 def moment_pick_kernel(
-    u_ref, ads_ref, ato_ref, amto_ref, ga_ref, mh, cu, cn,
-    atn_ref, amtn_ref, gh_ref, gl_ref, ah_ref, al_ref,
+    u_ref, um_ref, ads_ref, ato_ref, amto_ref, ga_ref, mh, cu, cn,
+    un_ref, umn_ref, atn_ref, amtn_ref,
 ):
     odd = on_odd_core()
     at = jnp.where(odd, ato_ref[...], ads_ref[0])
     amt = jnp.where(odd, amto_ref[...], ads_ref[1])
     at1, amt1 = adagrad(at, amt, ga_ref[...])
-    second_group(u_ref, at1, amt1, atn_ref, amtn_ref, (mh, cu, cn), gh_ref, gl_ref, ah_ref, al_ref)
+    put = update_users(reader(u_ref), reader(um_ref), un_ref, umn_ref)
+    ga = group_pass(1, reader(u_ref), u_ref.shape[0], split(at1), (mh, cu, cn), put)
+    atn_ref[...], amtn_ref[...] = adagrad(at1, amt1, ga)
 
 
 def gradient_kernel(u_ref, at_ref, mh, cu, cn, gu_ref, ga_ref):
@@ -200,11 +218,13 @@
 
 def both_moments_kernel(
     u_ref, um_ref, at_ref, amt_ref, gu_ref, ga_ref, mh, cu, cn,
-    uo_ref, umo_ref, ato_ref, amto_ref, gh_ref, gl_ref, ah_ref, al_ref,
+    uo_ref, umo_ref, ato_ref, amto_ref, u1_ref, um1_ref,
 ):
-    uo_ref[...], umo_ref[...] = adagrad(u_ref[...], um_ref[...], gu_ref[...])
+    u1_ref[...], um1_ref[...] = adagrad(u_ref[...], um_ref[...], gu_ref[...])
     at1, amt1 = adagrad(at_ref[...], amt_ref[...], ga_ref[...])
-    second_group(uo_ref, at1, amt1, ato_ref, amto_ref, (mh, cu, cn), gh_ref, gl_ref, ah_ref, al_ref)
+    put = update_users(reader(u1_ref), reader(um1_ref), uo_ref, umo_ref)
+    ga = group_pass(1, reader(u1_ref), u_ref.shape[0], split(at1), (mh, cu, cn), put)
+    ato_ref[...], amto_ref[...] = adagrad(at1, amt1, ga)
 
 
 def users_kernel(u_ref, um_ref, gh_ref, gl_ref, ah_ref, al_ref, uo_ref, umo_ref):
@@ -215,26 +235,22 @@
         put(rows, dot3((gh_ref[rows, :], gl_ref[rows, :]), at_hl, 1, 1))
 
 
-def users_pair_kernel(u_ref, um_ref, gh_ref, gl_ref, ah_ref, al_ref, users_ref):
-    users_kernel(u_ref, um_ref, gh_ref, gl_ref, ah_ref, al_ref, users_ref.at[0], users_ref.at[1])
-
-
-def prepare_kernel(rnd, away, after_ref, pu_hbm, pa_hbm, ng_hbm, mh, cu, cn, pu, pa, ng, sems):
+def prepare_kernel(rnd, away, pack, after_ref, pu_hbm, pa_hbm, ng_hbm, mh, cu, cn, *refs):
+    *lists, pu, pa, ng, sems = refs
     for c in (copies := fetch_indices(pu_hbm, pa_hbm, ng_hbm, pu, pa, ng, sems, away)):
         c.wait()
     prepare_round(rnd, pu, pa, ng, mh.shape[1], mh.shape[2], (mh, cu, cn))
-
-
-def last_users_kernel(u_ref, um_ref, gh_ref, gl_ref, ah_ref, al_ref, uo_hbm, umo_hbm, uo_ref, umo_ref, sems):
-    users_kernel(u_ref, um_ref, gh_ref, gl_ref, ah_ref, al_ref, uo_ref, umo_ref)
-    copies = [
-        pltpu.make_async_copy(uo_ref, uo_hbm, sems.at[0]),
-        pltpu.make_async_copy(umo_ref, umo_hbm, sems.at[1]),
-    ]
-    for c in copies:
-        c.start()
-    for c in copies:
-        c.wait()
+    if lists:
+        pack_lists(pack, pu, pa, ng, *lists)
+
+
+def prepare_packed_kernel(edges, n, after_ref, lists_ref, mh, cu, cn):
+    groups, users, ads = mh.shape
+    size = edges // groups
+    for g in range(groups):
+        cols = pl.ds(g * size, size)
+        negs = lists_ref[2 + g : 3 + g, pl.ds(0, n)]
+        prepare(g, lists_ref[0:1, cols], lists_ref[1:2, cols], negs, users, ads, mh, cu, cn)
 
 
 def call(kernel, ins, outs, scratch=(), hbm=0, name=None, out_place=pltpu.VMEM):
@@ -253,39 +269,39 @@
     )(*ins[:split_at], *far)
 
 
-def finish_kernel(xt_ref, out_hbm, x_ref, sems):
-    count = sems.shape[0]
-    size = x_ref.shape[0] // count
+def turn_out(xt_ref, out_hbm, x_ref, sems):
+    size = x_ref.shape[0] // PARTS_OUT
     copies = []
-    for k in range(count):
+    for k in range(PARTS_OUT):
         rows = pl.ds(k * size, size)
         x_ref[rows, :] = xt_ref[:, rows].T
         copies.append(pltpu.make_async_copy(x_ref.at[rows, :], out_hbm.at[rows, :], sems.at[k]))
         copies[-1].start()
+    return copies
+
+
+def ads_out_kernel(xt_ref, out_hbm, x_ref, sems):
+    for c in turn_out(xt_ref, out_hbm, x_ref, sems):
+        c.wait()
+
+
+def last_kernel(u_ref, um_ref, xt_ref, u_hbm, um_hbm, x_hbm, x_ref, sems, user_sems):
+    copies = [
+        pltpu.make_async_copy(u_ref, u_hbm, user_sems.at[0]),
+        pltpu.make_async_copy(um_ref, um_hbm, user_sems.at[1]),
+    ]
     for c in copies:
+        c.start()
+    for c in copies + turn_out(xt_ref, x_hbm, x_ref, sems):
         c.wait()
 
 
-def finish(xt):
-    d, rows = xt.shape
-    return pl.pallas_call(
-        finish_kernel,
-        out_shape=pltpu.HBM((rows, d), xt.dtype),
-        in_specs=[pl.BlockSpec(memory_space=pltpu.VMEM)],
-        out_specs=pl.BlockSpec(memory_space=pltpu.HBM),
-        scratch_shapes=[pltpu.VMEM((rows, d), xt.dtype), pltpu.SemaphoreType.DMA((4,))],
-        compiler_params=pltpu.CompilerParams(vmem_limit_bytes=VMEM_LIMIT),
-        cost_estimate=pl.CostEstimate(flops=0, bytes_accessed=2 * xt.size * 4, transcendentals=0),
-        name="ads_out",
-    )(xt)
-
-
-def move(arrays, even, odd):
+def move(arrays, *kinds):
     blocks, cycles = lax.axis_size("blk"), lax.axis_size("pair")
     route = []
     for b in range(blocks):
         for p in range(cycles):
-            steps, flip = odd if b % 2 else even
+            steps, flip = kinds[b % len(kinds)]
             to = (b + steps) % blocks, p ^ (cycles // 2 if flip else 0)
             route.append((b * cycles + p, to[0] * cycles + to[1]))
     return tuple(lax.ppermute(x, AXES, route) for x in arrays)
@@ -312,22 +328,20 @@
     prep_shapes = [shape(groups, nu, na, dtype=BF16), shape(groups, nu, 128), shape(groups, 8, na)]
     prep_scratch = [pltpu.VMEM(s.shape, s.dtype) for s in prep_shapes]
 
-    def prepare_for(rnd, away, after):
+    def prepare_for(rnd, away, after, pack=None):
+        lists = [] if pack is None else [shape(8, max(edges, n), dtype=jnp.int32)]
         return call(
-            functools.partial(prepare_kernel, rnd, away), (after, *indices), prep_shapes,
+            functools.partial(prepare_kernel, rnd, away, pack), (after, *indices), prep_shapes + lists,
             [*index_scratch, sems], hbm=3, name="counts",
         )
 
     def first_group(u, um, at, prep, *after):
         return call(embedding_kernel, (u, um, at, *prep, *after), [table_u, table_u, table_a], name="group_first")
 
-    def second_group_of(u, at, amt, ga, prep):
-        at, amt, *g = call(moment_kernel, (u, at, amt, ga, *prep), [table_a, table_a, *parts], name="group_second")
-        return (at, amt), g
-
     def update(u, um, g):
         return call(users_kernel, (u, um, *g), [table_u, table_u], name="users_update")
 
+    stay, away = (0, False), (0, True)
     u, um, at, amt, *g = call(
         first_round_kernel,
         (*indices, users, ads, user_moms, ad_moments),
@@ -338,19 +352,20 @@
     near = move((at, amt), (1, False), (-1, False))
     far = move((at, amt), (1, False), (1, False))
     u, um = update(u, um, g)
-    prep = prepare_for(1, False, um)
+    *prep, lists = prepare_for(1, False, um, rounds - 1)
+
+    (lists,) = move((lists,), (-4, False), stay, stay, stay)
 
     u_early, um_early, ga = first_group(u, um, near[0], prep)
-    ads_early, *g = call(
-        moment_pair_kernel, (u_early, *near, ga, *prep), [shape(2, d, na), *parts], name="group_second_pair",
+    ads_early, after = call(
+        early_kernel, (u_early, um_early, *near, ga, *prep), [shape(2, d, na), shape(2, nu, d)], name="group_second_early",
     )
     (ads_early,) = move((ads_early,), (1, False), (1, True))
-    (after,) = call(users_pair_kernel, (u_early, um_early, *g), [shape(2, nu, d)], name="users_update_pair")
-    (users_early,) = move((after,), (0, False), (0, True))
+    (users_early,) = move((after,), stay, away)
 
     u, um, ga = first_group(u, um, far[0], prep, after)
-    ads_late, g = second_group_of(u, *far, ga, prep)
-    ads_late = move(ads_late, (1, False), (-1, False))
+    at, amt, *g = call(moment_kernel, (u, *far, ga, *prep), [table_a, table_a, *parts], name="group_second")
+    ads_late = move((at, amt), (1, False), (-1, False))
     u, um = update(u, um, g)
     prep = prepare_for(2, True, um)
 
@@ -358,27 +373,29 @@
         embedding_pick_kernel, (u, um, users_early, ads_early, ads_late[0], *prep), [table_u, table_u, table_a],
         name="group_first_pick",
     )
-    at, amt, *g = call(
-        moment_pick_kernel, (u, ads_early, *ads_late, ga, *prep),
-        [table_a, table_a, *parts], name="group_second_pick",
-    )
-    at, amt = move((at, amt), (1, False), (1, True))
-    u, um = update(u, um, g)
+    u, um, at, amt = call(
+        moment_pick_kernel, (u, um, ads_early, *ads_late, ga, *prep),
+        [table_u, table_u, table_a, table_a], name="group_second_pick",
+    )
     after = um
-    u, um = move((u, um), (0, False), (0, True))
-    prep = prepare_for(3, False, after)
-
+    at, amt = move((at, amt), (1, False), (1, True), (1, False), (-3, True))
+    u, um = move((u, um), (-4, False), away, stay, away)
+    prep = call(functools.partial(prepare_packed_kernel, edges, n), (after, lists), prep_shapes, name="counts_moved")
     gu, ga = call(gradient_kernel, (u, at, *prep), [table_u, table_a], name="group_first_gradients")
-    u, um, at, amt, *g = call(
-        both_moments_kernel, (u, um, at, amt, gu, ga, *prep), [table_u, table_u, table_a, table_a, *parts],
-        name="group_second_both",
-    )
-    at, amt = move((at, amt), (1 - rounds, True), (1 - rounds, True))
-    u, um = call(
-        last_users_kernel, (u, um, *g), [pltpu.HBM((nu, d), F32)] * 2,
-        [pltpu.VMEM((nu, d), F32)] * 2 + [pltpu.SemaphoreType.DMA((2,))], name="users_last", out_place=pltpu.HBM,
-    )
-    return u, um, finish(at), finish(amt)
+    u, um, at, amt = call(
+        both_moments_kernel, (u, um, at, amt, gu, ga, *prep), [table_u, table_u, table_a, table_a],
+        [pltpu.VMEM((nu, d), F32)] * 2, name="group_second_both",
+    )
+    at, amt = move((at, amt), (1, True), (-3, True), (-3, True), (-3, True))
+    u, um = move((u, um), (4, False), stay, stay, stay)
+    upright = pltpu.HBM((na, d), F32)
+    turn_scratch = [pltpu.VMEM((na, d), F32), pltpu.SemaphoreType.DMA((PARTS_OUT,))]
+    (a,) = call(ads_out_kernel, (at,), [upright], turn_scratch, name="ads_out", out_place=pltpu.HBM)
+    u, um, am = call(
+        last_kernel, (u, um, amt), [pltpu.HBM((nu, d), F32)] * 2 + [upright],
+        [*turn_scratch, pltpu.SemaphoreType.DMA((2,))], name="last_out", out_place=pltpu.HBM,
+    )
+    return u, um, a, am
 
 
 def solution(mesh):

time: 87.4 us -> 83.8 us (0.959)
  waiting for transfers between devices: 41.6 us -> 30.8 us
  starting transfers between devices: 10.6 us -> 20.3 us
  Pallas kernels: 32.7 us -> 30 us
    ppermute x14 -> x17, waiting for transfers between devices: 41.6 us -> 30.8 us  [move(): return tuple((lax.ppermute(x, AXES, route) for x in arrays))]
    ppermute x14 -> x17, starting transfers between devices: 10.6 us -> 20.3 us  [move(): return tuple((lax.ppermute(x, AXES, route) for x in arrays))]
    pallas_call x2 -> x0, Pallas kernels: 1.84 us -> none  [finish(): pl.pallas_call(finish_kernel, out_shape=pltpu.HBM((rows, d), xt.dtype), i...]
    pallas_call x17 -> x16, Pallas kernels: 30.9 us -> 30 us  [call(): pl.pallas_call(kernel, out_shape=outs, in_specs=[vmem] * split_at + [pl.B...]
  transfers between devices with their start and end apart: 14 -> 17, of which waited for: 6 -> 6; matrix products, arithmetic and copies ran while one was open for 0% -> 0% of each run, Pallas kernels for 25% -> 23%
where the time goes in v3:
time: 83.8 us; the launch traced here: 82.2 us
  waiting for transfers between devices  30.8 us (37%)
  Pallas kernels  30 us (36%)
  starting transfers between devices  20.3 us (24%)
  between operations  1.09 us (1%)
    ppermute x17, waiting for transfers between devices, move(): return tuple((lax.ppermute(x, AXES, route) for x in arrays))  30.8 us
    pallas_call x16, Pallas kernels, call(): pl.pallas_call(kernel, out_shape=outs, in_specs=[vmem] * split_at + [pl.B...  30 us
    ppermute x17, starting transfers between devices, move(): return tuple((lax.ppermute(x, AXES, route) for x in arrays))  20.3 us
  transfers between devices with their start and end apart: 17, of which 6 were waited for; matrix products, arithmetic and copies ran while one was open for 0% of the time, Pallas kernels for 23%

profile of v3, /device:TPU:192, one launch (start us, length us, event | category | flops | bytes accessed | tf_op | source)
XLA Modules:
  0.0 82.2 jit_solution(7947336806763949893)
XLA Ops:
  0.6 5.3 %round_first.1 = (f32[512,256]{1,0:T(8,128)S(1)}, f32[512,256]{1,0:T(8,128)S(1)}, f32[256,512]{1,0:T(8,128)S(1)}, f32[256,512]{1,0:T(8,128)S(1)}, bf16[512,512]{...) custom-call(s32[1,16,4,512]{3,2,1,0:T(4,128)} %pu_hbm.5, ...), custom_call_target="tpu_custom_call" | custom-call | flops 1 | bytes 1 | tf_op jit(solution)/shard_map/round_first/pallas_call | solution.py:260
  5.9 0.1 collective-permute-start.1
  6.0 0.5 collective-permute-start.2
  6.5 0.1 collective-permute-start
  6.6 3.2 %collective-permute-start.3 = (f32[256,512]{1,0:T(8,128)S(1)}, f32[256,512]{1,0:T(8,128)S(1)}, u32[]{:S(2)}, u32[]{:S(2)}) collective-permute-start(f32[256,512]{1,0:T(8,128)S(1)} %get-tuple-element.70), channel_id=1, source_target_pairs={{0,16},{1,17},{2,18},{3,19},{4,20},{5,21},{6,22},{7,23},{8,24},{9,... | collective-permute-start | bytes 1572872 | tf_op jit(solution)/shard_map/ppermute | solution.py:307
  9.9 0.8 users_update.2
  10.6 1.5 %counts.2 = (bf16[2,512,512]{2,1,0:T(8,128)(2,1)S(1)}, f32[2,512,128]{2,1,0:T(8,128)S(1)}, f32[2,8,512]{2,1,0:T(8,128)S(1)}, s32[8,512]{1,0:T(8,128)S(1)}) custom-call(f32[512,256]{1,0:T(8,128)S(1)} %get-tuple-element.63.after_ref.um_ref, s32[1,16,4,512]{3,2,1,0:T(4,128)} %pu_hbm.5, s32[1,16,4,512]{3,2,1,0:T(4,128)} %pa_hbm.5, s32[1,16,4,2,512]{4,3,2,1,0:T(2,128)} %ng_hbm.5), custom_call_target="tpu_custom_call" | custom-call | flops 1 | bytes 1 | tf_op jit(solution)/shard_map/counts/pallas_call | solution.py:260
  12.2 0.0 collective-permute-done.1.at_ref
  12.2 2.1 %group_first.2 = (f32[512,256]{1,0:T(8,128)S(1)}, f32[512,256]{1,0:T(8,128)S(1)}, f32[256,512]{1,0:T(8,128)S(1)}) custom-call(f32[512,256]{1,0:T(8,128)S(1)} %get-tuple-element.62.u_ref, f32[512,256]{1,0:T(8,128)S(1)} %get-tuple-element.63.after_ref.um_ref, f32[256,512]{1,0:T(8,128)S(1)} %collective-permute-done.1.at_ref, ...), custom_call_target="tpu_custom_call" | custom-call | flops 1 | bytes 1 | tf_op jit(solution)/shard_map/group_first/pallas_call | solution.py:260
  14.3 0.0 collective-permute-done.2.amt_ref
  14.3 2.3 %group_second_early.1 = (f32[2,256,512]{2,1,0:T(8,128)S(1)}, f32[2,512,256]{2,1,0:T(8,128)S(1)}) custom-call(f32[512,256]{1,0:T(8,128)S(1)} %get-tuple-element.68.u_ref, f32[512,256]{1,0:T(8,128)S(1)} %get-tuple-element.69.um_ref, f32[256,512]{1,0:T(8,128)S(1)} %collective-permute-done.1.at_ref, f32[256,512]{1,0:T(8,128)S(1)} %collective-permute-done.2.amt_ref, ...), custom_call_target="tpu_custom_call" | custom-call | flops 1 | bytes 1 | tf_op jit(solution)/shard_map/group_second_early/pallas_call | solution.py:260
  16.7 0.2 collective-permute-start.5
  16.8 0.9 %collective-permute-start.4 = (f32[2,512,256]{2,1,0:T(8,128)S(1)}, f32[2,512,256]{2,1,0:T(8,128)S(1)}, u32[]{:S(2)}, u32[]{:S(2)}) collective-permute-start(f32[2,512,256]{2,1,0:T(8,128)S(1)} %get-tuple-element.72.refs_0_), channel_id=1, source_target_pairs={{0,0},{1,1},{2,2},{3,3},{4,4},{5,5},{6,6},{7,7},{8,8},{9,9},{10,10... | collective-permute-start | bytes 3145736 | tf_op jit(solution)/shard_map/ppermute | solution.py:307
  17.8 1.0 %collective-permute-done.at_ref = f32[256,512]{1,0:T(8,128)S(1)} collective-permute-done((f32[256,512]{1,0:T(8,128)S(1)}, f32[256,512]{1,0:T(8,128)S(1)}, u32[]{:S(2)}, u32[]{:S(2)}) %collective-permute-start) | collective-permute-done | bytes 524320 | tf_op jit(solution)/shard_map/ppermute | solution.py:307
  18.8 2.1 %group_first.3 = (f32[512,256]{1,0:T(8,128)S(1)}, f32[512,256]{1,0:T(8,128)S(1)}, f32[256,512]{1,0:T(8,128)S(1)}) custom-call(f32[512,256]{1,0:T(8,128)S(1)} %get-tuple-element.62.u_ref, f32[512,256]{1,0:T(8,128)S(1)} %get-tuple-element.63.after_ref.um_ref, f32[256,512]{1,0:T(8,128)S(1)} %collective-permute-done.at_ref, ...), custom_call_target="tpu_custom_call" | custom-call | flops 1 | bytes 1 | tf_op jit(solution)/shard_map/group_first/pallas_call | solution.py:260
  20.9 3.5 %collective-permute-done.3.amt_ref = f32[256,512]{1,0:T(8,128)S(1)} collective-permute-done((f32[256,512]{1,0:T(8,128)S(1)}, f32[256,512]{1,0:T(8,128)S(1)}, u32[]{:S(2)}, u32[]{:S(2)}) %collective-permute-start.3) | collective-permute-done | bytes 524320 | tf_op jit(solution)/shard_map/ppermute | solution.py:307
  24.4 1.8 %group_second.1 = (f32[256,512]{1,0:T(8,128)S(1)}, f32[256,512]{1,0:T(8,128)S(1)}, bf16[512,512]{1,0:T(8,128)(2,1)S(1)}, bf16[512,512]{1,0:T(8,128)(2,1)S(1)}, b...) custom-call(f32[512,256]{1,0:T(8,128)S(1)} %get-tuple-element.73.u_ref, ...), custom_call_target="tpu_custom_call" | custom-call | flops 1 | bytes 1 | tf_op jit(solution)/shard_map/group_second/pallas_call | solution.py:260
  26.2 0.1 collective-permute-start.6
  26.3 0.5 collective-permute-start.7
  26.8 0.8 users_update.3
  27.6 1.5 %counts.3 = (bf16[2,512,512]{2,1,0:T(8,128)(2,1)S(1)}, f32[2,512,128]{2,1,0:T(8,128)S(1)}, f32[2,8,512]{2,1,0:T(8,128)S(1)}) custom-call(f32[512,256]{1,0:T(8,128)S(1)} %get-tuple-element.81.after_ref.ume_ref, s32[1,16,4,512]{3,2,1,0:T(4,128)} %pu_hbm.5, s32[1,16,4,512]{3,2,1,0:T(4,128)} %pa_hbm.5, s32[1,16,4,2,512]{4,3,2,1,0:T(2,128)} %ng_hbm.5), custom_call_target="tpu_custom_call" | custom-call | flops 1 | bytes 1 | tf_op jit(solution)/shard_map/counts/pallas_call | solution.py:260
  29.1 0.0 collective-permute-done.6.ato_ref
  29.1 7.2 %collective-permute-done.5.ads_ref = f32[2,256,512]{2,1,0:T(8,128)S(1)} collective-permute-done((f32[2,256,512]{2,1,0:T(8,128)S(1)}, f32[2,256,512]{2,1,0:T(8,128)S(1)}, u32[]{:S(2)}, u32[]{:S(2)}) %collective-permute-start.5) | collective-permute-done | bytes 1048608 | tf_op jit(solution)/shard_map/ppermute | solution.py:307
  36.3 0.0 collective-permute-done.4.users_ref
  36.3 2.2 %group_first_pick.1 = (f32[512,256]{1,0:T(8,128)S(1)}, f32[512,256]{1,0:T(8,128)S(1)}, f32[256,512]{1,0:T(8,128)S(1)}) custom-call(f32[512,256]{1,0:T(8,128)S(1)} %get-tuple-element.80.ue_ref, f32[512,256]{1,0:T(8,128)S(1)} %get-tuple-element.81.after_ref.ume_ref, f32[2,512,256]{2,1,0:T(8,128)S(1)} %collective-permute-done.4.users_ref, ...), custom_call_target="tpu_custom_call" | custom-call | flops 1 | bytes 1 | tf_op jit(solution)/shard_map/group_first_pick/pallas_call | solution.py:260
  38.5 0.0 collective-permute-done.7.amto_ref
  38.5 2.4 %group_second_pick.1 = (f32[512,256]{1,0:T(8,128)S(1)}, f32[512,256]{1,0:T(8,128)S(1)}, f32[256,512]{1,0:T(8,128)S(1)}, f32[256,512]{1,0:T(8,128)S(1)}) custom-call(f32[512,256]{1,0:T(8,128)S(1)} %get-tuple-element.87.u_ref, f32[512,256]{1,0:T(8,128)S(1)} %get-tuple-element.88.um_ref, f32[2,256,512]{2,1,0:T(8,128)S(1)} %collective-permute-done.5.ads_ref, ...), custom_call_target="tpu_custom_call" | custom-call | flops 1 | bytes 1 | tf_op jit(solution)/shard_map/group_second_pick/pallas_call | solution.py:260
  40.9 3.5 %collective-permute-start.8 = (f32[512,256]{1,0:T(8,128)S(1)}, f32[512,256]{1,0:T(8,128)S(1)}, u32[]{:S(2)}, u32[]{:S(2)}) collective-permute-start(f32[512,256]{1,0:T(8,128)S(1)} %get-tuple-element.91), channel_id=1, source_target_pairs={{0,192},{1,193},{2,194},{3,195},{4,196},{5,197},{6,198},{7,199},{8... | collective-permute-start | bytes 1572872 | tf_op jit(solution)/shard_map/ppermute | solution.py:307
  44.4 0.1 collective-permute-start.10
  44.5 0.1 collective-permute-start.11
  44.6 2.7 %collective-permute-start.9 = (f32[512,256]{1,0:T(8,128)S(1)}, f32[512,256]{1,0:T(8,128)S(1)}, u32[]{:S(2)}, u32[]{:S(2)}) collective-permute-start(f32[512,256]{1,0:T(8,128)S(1)} %get-tuple-element.92.after_ref), channel_id=1, source_target_pairs={{0,192},{1,193},{2,194},{3,195},{4,196},{5,197},{6,198},{7,199},{8... | collective-permute-start | bytes 1572872 | tf_op jit(solution)/shard_map/ppermute | solution.py:307
  47.3 2.7 %collective-permute-start.12 = (s32[8,512]{1,0:T(8,128)S(1)}, s32[8,512]{1,0:T(8,128)S(1)}, u32[]{:S(2)}, u32[]{:S(2)}) collective-permute-start(s32[8,512]{1,0:T(8,128)S(1)} %get-tuple-element.95), channel_id=1, source_target_pairs={{0,192},{1,193},{2,194},{3,195},{4,196},{5,197},{6,198},{7,199},{8... | collective-permute-start | bytes 49160 | tf_op jit(solution)/shard_map/ppermute | solution.py:307
  50.0 7.8 %collective-permute-done.12.lists_ref = s32[8,512]{1,0:T(8,128)S(1)} collective-permute-done((s32[8,512]{1,0:T(8,128)S(1)}, s32[8,512]{1,0:T(8,128)S(1)}, u32[]{:S(2)}, u32[]{:S(2)}) %collective-permute-start.12) | collective-permute-done | bytes 16416 | tf_op jit(solution)/shard_map/ppermute | solution.py:307
  57.8 0.7 counts_moved.1
  58.5 0.0 collective-permute-done.8.u_ref
  58.5 0.0 collective-permute-done.10.at_ref
  58.5 2.0 %group_first_gradients.1 = (f32[512,256]{1,0:T(8,128)S(1)}, f32[256,512]{1,0:T(8,128)S(1)}) custom-call(f32[512,256]{1,0:T(8,128)S(1)} %collective-permute-done.8.u_ref, f32[256,512]{1,0:T(8,128)S(1)} %collective-permute-done.10.at_ref, bf16[2,512,512]{2,1,0:T(8,128)(2,1)S(1)} %get-tuple-element.96.mh, f32[2,512,128]{2,1,0:T(8,128)S(1)} %get-tuple-element.97.cu, ...), custom_call_target="tpu_custom_call" | custom-call | flops 1 | bytes 1 | tf_op jit(solution)/shard_map/group_first_gradients/pallas_call | solution.py:260
  60.5 0.0 collective-permute-done.9.um_ref
  60.5 2.4 %group_second_both.1 = (f32[512,256]{1,0:T(8,128)S(1)}, f32[512,256]{1,0:T(8,128)S(1)}, f32[256,512]{1,0:T(8,128)S(1)}, f32[256,512]{1,0:T(8,128)S(1)}) custom-call(f32[512,256]{1,0:T(8,128)S(1)} %collective-permute-done.8.u_ref, f32[512,256]{1,0:T(8,128)S(1)} %collective-permute-done.9.um_ref, f32[256,512]{1,0:T(8,128)S(1)} %collective-permute-done.10.at_ref, ...), custom_call_target="tpu_custom_call" | custom-call | flops 1 | bytes 1 | tf_op jit(solution)/shard_map/group_second_both/pallas_call | solution.py:260
  63.0 2.2 %collective-permute-start.13 = (f32[512,256]{1,0:T(8,128)S(1)}, f32[512,256]{1,0:T(8,128)S(1)}, u32[]{:S(2)}, u32[]{:S(2)}) collective-permute-start(f32[512,256]{1,0:T(8,128)S(1)} %get-tuple-element.101), channel_id=1, source_target_pairs={{0,64},{1,65},{2,66},{3,67},{4,68},{5,69},{6,70},{7,71},{8,72},{9,... | collective-permute-start | bytes 1572872 | tf_op jit(solution)/shard_map/ppermute | solution.py:307
  65.1 0.1 collective-permute-start.16
  65.2 3.4 %collective-permute-start.14 = (f32[512,256]{1,0:T(8,128)S(1)}, f32[512,256]{1,0:T(8,128)S(1)}, u32[]{:S(2)}, u32[]{:S(2)}) collective-permute-start(f32[512,256]{1,0:T(8,128)S(1)} %get-tuple-element.102), channel_id=1, source_target_pairs={{0,64},{1,65},{2,66},{3,67},{4,68},{5,69},{6,70},{7,71},{8,72},{9,... | collective-permute-start | bytes 1572872 | tf_op jit(solution)/shard_map/ppermute | solution.py:307
  68.6 0.1 collective-permute-start.15
  68.7 6.3 %collective-permute-done.16.xt_ref = f32[256,512]{1,0:T(8,128)S(1)} collective-permute-done((f32[256,512]{1,0:T(8,128)S(1)}, f32[256,512]{1,0:T(8,128)S(1)}, u32[]{:S(2)}, u32[]{:S(2)}) %collective-permute-start.16) | collective-permute-done | bytes 524320 | tf_op jit(solution)/shard_map/ppermute | solution.py:307
  75.0 0.9 %ads_out.1 = f32[512,256]{1,0:T(8,128)} custom-call(f32[256,512]{1,0:T(8,128)S(1)} %collective-permute-done.16.xt_ref), custom_call_target="tpu_custom_call" | custom-call | flops 1 | bytes 1 | tf_op jit(solution)/shard_map/ads_out/pallas_call | solution.py:260
  76.0 4.9 %collective-permute-done.14.um_ref = f32[512,256]{1,0:T(8,128)S(1)} collective-permute-done((f32[512,256]{1,0:T(8,128)S(1)}, f32[512,256]{1,0:T(8,128)S(1)}, u32[]{:S(2)}, u32[]{:S(2)}) %collective-permute-start.14) | collective-permute-done | bytes 524320 | tf_op jit(solution)/shard_map/ppermute | solution.py:307
  80.9 0.0 collective-permute-done.15.xt_ref
  80.9 1.2 %last_out.1 = (f32[512,256]{1,0:T(8,128)}, f32[512,256]{1,0:T(8,128)}, f32[512,256]{1,0:T(8,128)}) custom-call(f32[512,256]{1,0:T(8,128)S(1)} %collective-permute-done.13.u_ref, f32[512,256]{1,0:T(8,128)S(1)} %collective-permute-done.14.um_ref, f32[256,512]{1,0:T(8,128)S(1)} %collective-permute-done.15.xt_ref), custom_call_target="tpu_custom_call" | custom-call | flops 1 | bytes 1 | tf_op jit(solution)/shard_map/last_out/pallas_call | solution.py:260
  (2 shorter events, 0.0 us)
Async XLA Ops:
  5.9 6.2 %collective-permute-start.1 = (f32[256,512]{1,0:T(8,128)S(1)}, f32[256,512]{1,0:T(8,128)S(1)}, u32[]{:S(2)}, u32[]{:S(2)}) collective-permute-start(f32[256,512]{1,0:T(8,128)S(1)} %get-tuple-element.64), channel_id=1, source_target_pairs={{0,16},{1,17},{2,18},{3,19},{4,20},{5,21},{6,22},{7,23},{8,24},{9,... | collective-permute-start | bytes 1572872 | tf_op jit(solution)/shard_map/ppermute | solution.py:307
  6.0 8.3 %collective-permute-start.2 = (f32[256,512]{1,0:T(8,128)S(1)}, f32[256,512]{1,0:T(8,128)S(1)}, u32[]{:S(2)}, u32[]{:S(2)}) collective-permute-start(f32[256,512]{1,0:T(8,128)S(1)} %get-tuple-element.70), channel_id=1, source_target_pairs={{0,16},{1,17},{2,18},{3,19},{4,20},{5,21},{6,22},{7,23},{8,24},{9,... | collective-permute-start | bytes 1572872 | tf_op jit(solution)/shard_map/ppermute | solution.py:307
  6.5 12.2 %collective-permute-start = (f32[256,512]{1,0:T(8,128)S(1)}, f32[256,512]{1,0:T(8,128)S(1)}, u32[]{:S(2)}, u32[]{:S(2)}) collective-permute-start(f32[256,512]{1,0:T(8,128)S(1)} %get-tuple-element.64), channel_id=1, source_target_pairs={{0,16},{1,17},{2,18},{3,19},{4,20},{5,21},{6,22},{7,23},{8,24},{9,... | collective-permute-start | bytes 1572872 | tf_op jit(solution)/shard_map/ppermute | solution.py:307
  6.6 17.7 %collective-permute-start.3 = (f32[256,512]{1,0:T(8,128)S(1)}, f32[256,512]{1,0:T(8,128)S(1)}, u32[]{:S(2)}, u32[]{:S(2)}) collective-permute-start(f32[256,512]{1,0:T(8,128)S(1)} %get-tuple-element.70), channel_id=1, source_target_pairs={{0,16},{1,17},{2,18},{3,19},{4,20},{5,21},{6,22},{7,23},{8,24},{9,... | collective-permute-start | bytes 1572872 | tf_op jit(solution)/shard_map/ppermute | solution.py:307
  16.7 19.7 %collective-permute-start.5 = (f32[2,256,512]{2,1,0:T(8,128)S(1)}, f32[2,256,512]{2,1,0:T(8,128)S(1)}, u32[]{:S(2)}, u32[]{:S(2)}) collective-permute-start(f32[2,256,512]{2,1,0:T(8,128)S(1)} %get-tuple-element.82), channel_id=1, source_target_pairs={{0,16},{1,17},{2,18},{3,19},{4,20},{5,21},{6,22},{7,23},{8,24},{9,... | collective-permute-start | bytes 3145736 | tf_op jit(solution)/shard_map/ppermute | solution.py:307
  16.8 19.5 %collective-permute-start.4 = (f32[2,512,256]{2,1,0:T(8,128)S(1)}, f32[2,512,256]{2,1,0:T(8,128)S(1)}, u32[]{:S(2)}, u32[]{:S(2)}) collective-permute-start(f32[2,512,256]{2,1,0:T(8,128)S(1)} %get-tuple-element.72.refs_0_), channel_id=1, source_target_pairs={{0,0},{1,1},{2,2},{3,3},{4,4},{5,5},{6,6},{7,7},{8,8},{9,9},{10,10... | collective-permute-start | bytes 3145736 | tf_op jit(solution)/shard_map/ppermute | solution.py:307
  26.2 2.9 %collective-permute-start.6 = (f32[256,512]{1,0:T(8,128)S(1)}, f32[256,512]{1,0:T(8,128)S(1)}, u32[]{:S(2)}, u32[]{:S(2)}) collective-permute-start(f32[256,512]{1,0:T(8,128)S(1)} %get-tuple-element.83), channel_id=1, source_target_pairs={{0,16},{1,17},{2,18},{3,19},{4,20},{5,21},{6,22},{7,23},{8,24},{9,... | collective-permute-start | bytes 1572872 | tf_op jit(solution)/shard_map/ppermute | solution.py:307
  26.3 12.3 %collective-permute-start.7 = (f32[256,512]{1,0:T(8,128)S(1)}, f32[256,512]{1,0:T(8,128)S(1)}, u32[]{:S(2)}, u32[]{:S(2)}) collective-permute-start(f32[256,512]{1,0:T(8,128)S(1)} %get-tuple-element.89), channel_id=1, source_target_pairs={{0,16},{1,17},{2,18},{3,19},{4,20},{5,21},{6,22},{7,23},{8,24},{9,... | collective-permute-start | bytes 1572872 | tf_op jit(solution)/shard_map/ppermute | solution.py:307
  40.9 17.6 %collective-permute-start.8 = (f32[512,256]{1,0:T(8,128)S(1)}, f32[512,256]{1,0:T(8,128)S(1)}, u32[]{:S(2)}, u32[]{:S(2)}) collective-permute-start(f32[512,256]{1,0:T(8,128)S(1)} %get-tuple-element.91), channel_id=1, source_target_pairs={{0,192},{1,193},{2,194},{3,195},{4,196},{5,197},{6,198},{7,199},{8... | collective-permute-start | bytes 1572872 | tf_op jit(solution)/shard_map/ppermute | solution.py:307
  44.4 14.1 %collective-permute-start.10 = (f32[256,512]{1,0:T(8,128)S(1)}, f32[256,512]{1,0:T(8,128)S(1)}, u32[]{:S(2)}, u32[]{:S(2)}) collective-permute-start(f32[256,512]{1,0:T(8,128)S(1)} %get-tuple-element.93), channel_id=1, source_target_pairs={{0,16},{1,17},{2,18},{3,19},{4,20},{5,21},{6,22},{7,23},{8,24},{9,... | collective-permute-start | bytes 1572872 | tf_op jit(solution)/shard_map/ppermute | solution.py:307
  44.5 16.0 %collective-permute-start.11 = (f32[256,512]{1,0:T(8,128)S(1)}, f32[256,512]{1,0:T(8,128)S(1)}, u32[]{:S(2)}, u32[]{:S(2)}) collective-permute-start(f32[256,512]{1,0:T(8,128)S(1)} %get-tuple-element.94), channel_id=1, source_target_pairs={{0,16},{1,17},{2,18},{3,19},{4,20},{5,21},{6,22},{7,23},{8,24},{9,... | collective-permute-start | bytes 1572872 | tf_op jit(solution)/shard_map/ppermute | solution.py:307
  44.6 15.9 %collective-permute-start.9 = (f32[512,256]{1,0:T(8,128)S(1)}, f32[512,256]{1,0:T(8,128)S(1)}, u32[]{:S(2)}, u32[]{:S(2)}) collective-permute-start(f32[512,256]{1,0:T(8,128)S(1)} %get-tuple-element.92.after_ref), channel_id=1, source_target_pairs={{0,192},{1,193},{2,194},{3,195},{4,196},{5,197},{6,198},{7,199},{8... | collective-permute-start | bytes 1572872 | tf_op jit(solution)/shard_map/ppermute | solution.py:307
  47.3 10.5 %collective-permute-start.12 = (s32[8,512]{1,0:T(8,128)S(1)}, s32[8,512]{1,0:T(8,128)S(1)}, u32[]{:S(2)}, u32[]{:S(2)}) collective-permute-start(s32[8,512]{1,0:T(8,128)S(1)} %get-tuple-element.95), channel_id=1, source_target_pairs={{0,192},{1,193},{2,194},{3,195},{4,196},{5,197},{6,198},{7,199},{8... | collective-permute-start | bytes 49160 | tf_op jit(solution)/shard_map/ppermute | solution.py:307
  63.0 13.0 %collective-permute-start.13 = (f32[512,256]{1,0:T(8,128)S(1)}, f32[512,256]{1,0:T(8,128)S(1)}, u32[]{:S(2)}, u32[]{:S(2)}) collective-permute-start(f32[512,256]{1,0:T(8,128)S(1)} %get-tuple-element.101), channel_id=1, source_target_pairs={{0,64},{1,65},{2,66},{3,67},{4,68},{5,69},{6,70},{7,71},{8,72},{9,... | collective-permute-start | bytes 1572872 | tf_op jit(solution)/shard_map/ppermute | solution.py:307
  65.1 9.9 %collective-permute-start.16 = (f32[256,512]{1,0:T(8,128)S(1)}, f32[256,512]{1,0:T(8,128)S(1)}, u32[]{:S(2)}, u32[]{:S(2)}) collective-permute-start(f32[256,512]{1,0:T(8,128)S(1)} %get-tuple-element.106), channel_id=1, source_target_pairs={{0,24},{1,25},{2,26},{3,27},{4,28},{5,29},{6,30},{7,31},{8,16},{9,... | collective-permute-start | bytes 1572872 | tf_op jit(solution)/shard_map/ppermute | solution.py:307
  65.2 15.6 %collective-permute-start.14 = (f32[512,256]{1,0:T(8,128)S(1)}, f32[512,256]{1,0:T(8,128)S(1)}, u32[]{:S(2)}, u32[]{:S(2)}) collective-permute-start(f32[512,256]{1,0:T(8,128)S(1)} %get-tuple-element.102), channel_id=1, source_target_pairs={{0,64},{1,65},{2,66},{3,67},{4,68},{5,69},{6,70},{7,71},{8,72},{9,... | collective-permute-start | bytes 1572872 | tf_op jit(solution)/shard_map/ppermute | solution.py:307
  68.6 12.2 %collective-permute-start.15 = (f32[256,512]{1,0:T(8,128)S(1)}, f32[256,512]{1,0:T(8,128)S(1)}, u32[]{:S(2)}, u32[]{:S(2)}) collective-permute-start(f32[256,512]{1,0:T(8,128)S(1)} %get-tuple-element.103), channel_id=1, source_target_pairs={{0,24},{1,25},{2,26},{3,27},{4,28},{5,29},{6,30},{7,31},{8,16},{9,... | collective-permute-start | bytes 1572872 | tf_op jit(solution)/shard_map/ppermute | solution.py:307

commit v4 on v3

--- a/solution.py
+++ b/solution.py
@@ -140,7 +140,7 @@
 
 def first_round_kernel(
     pu_hbm, pa_hbm, ng_hbm, u_hbm, a_hbm, um_hbm, am_hbm,
-    uo_ref, umo_ref, ato_ref, amto_ref, gh_ref, gl_ref, ah_ref, al_ref,
+    uo_ref, umo_ref, ads_ref, gh_ref, gl_ref, ah_ref, al_ref,
     pu, pa, ng, mh, cu, cn, u_ref, um_ref, a_ref, am_ref, sems, table_sems,
 ):
     copies = fetch_indices(pu_hbm, pa_hbm, ng_hbm, pu, pa, ng, sems)
@@ -163,50 +163,49 @@
     put = update_users(reader(u_ref), reader(um_ref), uo_ref, umo_ref)
     ga = group_pass(0, reader(u_ref), u_ref.shape[0], split(at), prep, put)
     at1, amt1 = adagrad(at, amt, ga)
-    second_group(uo_ref, at1, amt1, ato_ref, amto_ref, prep, gh_ref, gl_ref, ah_ref, al_ref)
-
-
-def embedding_kernel(u_ref, um_ref, at_ref, mh, cu, cn, *refs):
-    uo_ref, umo_ref, ga_ref = refs[-3:]
+    second_group(uo_ref, at1, amt1, ads_ref.at[0], ads_ref.at[1], prep, gh_ref, gl_ref, ah_ref, al_ref)
+
+
+def meeting(u_read, um_read, at, amt, prep, u1_ref, um1_ref, uo_ref, umo_ref):
+    users = u1_ref.shape[0]
+    ga = group_pass(0, u_read, users, split(at), prep, update_users(u_read, um_read, u1_ref, um1_ref))
+    at1, amt1 = adagrad(at, amt, ga)
+    u_read = reader(u1_ref)
+    ga = group_pass(1, u_read, users, split(at1), prep, update_users(u_read, reader(um1_ref), uo_ref, umo_ref))
+    return adagrad(at1, amt1, ga)
+
+
+def early_kernel(u_ref, um_ref, near_ref, mh, cu, cn, ads_ref, users_ref, u1_ref, um1_ref):
+    ads_ref[0], ads_ref[1] = meeting(
+        reader(u_ref), reader(um_ref), near_ref[0], near_ref[1], (mh, cu, cn),
+        u1_ref, um1_ref, users_ref.at[0], users_ref.at[1],
+    )
+
+
+def late_kernel(
+    u_ref, um_ref, far_ref, mh, cu, cn, after_ref,
+    u1_ref, um1_ref, ato_ref, amto_ref, gh_ref, gl_ref, ah_ref, al_ref,
+):
+    prep = (mh, cu, cn)
+    at = far_ref[0]
     u_read = reader(u_ref)
-    put = update_users(u_read, reader(um_ref), uo_ref, umo_ref)
-    ga_ref[...] = group_pass(0, u_read, u_ref.shape[0], split(at_ref[...]), (mh, cu, cn), put)
-
-
-def moment_kernel(
-    u_ref, at_ref, amt_ref, ga_ref, mh, cu, cn,
-    ato_ref, amto_ref, gh_ref, gl_ref, ah_ref, al_ref,
-):
-    at1, amt1 = adagrad(at_ref[...], amt_ref[...], ga_ref[...])
-    second_group(u_ref, at1, amt1, ato_ref, amto_ref, (mh, cu, cn), gh_ref, gl_ref, ah_ref, al_ref)
-
-
-def early_kernel(u_ref, um_ref, at_ref, amt_ref, ga_ref, mh, cu, cn, ads_ref, users_ref):
-    at1, amt1 = adagrad(at_ref[...], amt_ref[...], ga_ref[...])
-    put = update_users(reader(u_ref), reader(um_ref), users_ref.at[0], users_ref.at[1])
-    ga = group_pass(1, reader(u_ref), u_ref.shape[0], split(at1), (mh, cu, cn), put)
-    ads_ref[0], ads_ref[1] = adagrad(at1, amt1, ga)
-
-
-def embedding_pick_kernel(ue_ref, ume_ref, users_ref, ads_ref, ato_ref, mh, cu, cn, un_ref, umn_ref, ga_ref):
-    odd = on_odd_core()
-    u_read = picker(odd, ue_ref, users_ref.at[0])
-    put = update_users(u_read, picker(odd, ume_ref, users_ref.at[1]), un_ref, umn_ref)
-    at = jnp.where(odd, ato_ref[...], ads_ref[0])
-    ga_ref[...] = group_pass(0, u_read, ue_ref.shape[0], split(at), (mh, cu, cn), put)
-
-
-def moment_pick_kernel(
-    u_ref, um_ref, ads_ref, ato_ref, amto_ref, ga_ref, mh, cu, cn,
-    un_ref, umn_ref, atn_ref, amtn_ref,
+    put = update_users(u_read, reader(um_ref), u1_ref, um1_ref)
+    ga = group_pass(0, u_read, u_ref.shape[0], split(at), prep, put)
+    at1, amt1 = adagrad(at, far_ref[1], ga)
+    second_group(u1_ref, at1, amt1, ato_ref, amto_ref, prep, gh_ref, gl_ref, ah_ref, al_ref)
+
+
+def pick_kernel(
+    ue_ref, ume_ref, users_ref, ads_ref, ato_ref, amto_ref, mh, cu, cn,
+    un_ref, umn_ref, atn_ref, amtn_ref, u1_ref, um1_ref,
 ):
     odd = on_odd_core()
     at = jnp.where(odd, ato_ref[...], ads_ref[0])
     amt = jnp.where(odd, amto_ref[...], ads_ref[1])
-    at1, amt1 = adagrad(at, amt, ga_ref[...])
-    put = update_users(reader(u_ref), reader(um_ref), un_ref, umn_ref)
-    ga = group_pass(1, reader(u_ref), u_ref.shape[0], split(at1), (mh, cu, cn), put)
-    atn_ref[...], amtn_ref[...] = adagrad(at1, amt1, ga)
+    u_read, um_read = picker(odd, ue_ref, users_ref.at[0]), picker(odd, ume_ref, users_ref.at[1])
+    atn_ref[...], amtn_ref[...] = meeting(
+        u_read, um_read, at, amt, (mh, cu, cn), u1_ref, um1_ref, un_ref, umn_ref
+    )
 
 
 def gradient_kernel(u_ref, at_ref, mh, cu, cn, gu_ref, ga_ref):
@@ -218,13 +217,13 @@
 
 def both_moments_kernel(
     u_ref, um_ref, at_ref, amt_ref, gu_ref, ga_ref, mh, cu, cn,
-    uo_ref, umo_ref, ato_ref, amto_ref, u1_ref, um1_ref,
+    uo_ref, umo_ref, ads_ref, u1_ref, um1_ref,
 ):
     u1_ref[...], um1_ref[...] = adagrad(u_ref[...], um_ref[...], gu_ref[...])
     at1, amt1 = adagrad(at_ref[...], amt_ref[...], ga_ref[...])
     put = update_users(reader(u1_ref), reader(um1_ref), uo_ref, umo_ref)
     ga = group_pass(1, reader(u1_ref), u_ref.shape[0], split(at1), (mh, cu, cn), put)
-    ato_ref[...], amto_ref[...] = adagrad(at1, amt1, ga)
+    ads_ref[0], ads_ref[1] = adagrad(at1, amt1, ga)
 
 
 def users_kernel(u_ref, um_ref, gh_ref, gl_ref, ah_ref, al_ref, uo_ref, umo_ref):
@@ -235,22 +234,27 @@
         put(rows, dot3((gh_ref[rows, :], gl_ref[rows, :]), at_hl, 1, 1))
 
 
-def prepare_kernel(rnd, away, pack, after_ref, pu_hbm, pa_hbm, ng_hbm, mh, cu, cn, *refs):
-    *lists, pu, pa, ng, sems = refs
-    for c in (copies := fetch_indices(pu_hbm, pa_hbm, ng_hbm, pu, pa, ng, sems, away)):
+def prepare_kernel(rnd, pack, after_ref, pu_hbm, pa_hbm, ng_hbm, mh, cu, cn, lists_ref, pu, pa, ng, sems):
+    for c in (copies := fetch_indices(pu_hbm, pa_hbm, ng_hbm, pu, pa, ng, sems)):
         c.wait()
     prepare_round(rnd, pu, pa, ng, mh.shape[1], mh.shape[2], (mh, cu, cn))
-    if lists:
-        pack_lists(pack, pu, pa, ng, *lists)
-
-
-def prepare_packed_kernel(edges, n, after_ref, lists_ref, mh, cu, cn):
+    pack_lists(pack, pu, pa, ng, lists_ref)
+
+
+def prepare_both_kernel(
+    rnd, after_ref, lists_ref, pu_hbm, pa_hbm, ng_hbm, mh, cu, cn, mh2, cu2, cn2, pu, pa, ng, sems,
+):
+    copies = fetch_indices(pu_hbm, pa_hbm, ng_hbm, pu, pa, ng, sems, away=True)
     groups, users, ads = mh.shape
-    size = edges // groups
+    n = ng_hbm.shape[-1]
+    size = pu_hbm.shape[-1] // groups
     for g in range(groups):
         cols = pl.ds(g * size, size)
         negs = lists_ref[2 + g : 3 + g, pl.ds(0, n)]
-        prepare(g, lists_ref[0:1, cols], lists_ref[1:2, cols], negs, users, ads, mh, cu, cn)
+        prepare(g, lists_ref[0:1, cols], lists_ref[1:2, cols], negs, users, ads, mh2, cu2, cn2)
+    for c in copies:
+        c.wait()
+    prepare_round(rnd, pu, pa, ng, users, ads, (mh, cu, cn))
 
 
 def call(kernel, ins, outs, scratch=(), hbm=0, name=None, out_place=pltpu.VMEM):
@@ -269,30 +273,21 @@
     )(*ins[:split_at], *far)
 
 
-def turn_out(xt_ref, out_hbm, x_ref, sems):
-    size = x_ref.shape[0] // PARTS_OUT
-    copies = []
-    for k in range(PARTS_OUT):
-        rows = pl.ds(k * size, size)
-        x_ref[rows, :] = xt_ref[:, rows].T
-        copies.append(pltpu.make_async_copy(x_ref.at[rows, :], out_hbm.at[rows, :], sems.at[k]))
-        copies[-1].start()
-    return copies
-
-
-def ads_out_kernel(xt_ref, out_hbm, x_ref, sems):
-    for c in turn_out(xt_ref, out_hbm, x_ref, sems):
-        c.wait()
-
-
-def last_kernel(u_ref, um_ref, xt_ref, u_hbm, um_hbm, x_hbm, x_ref, sems, user_sems):
+def last_kernel(u_ref, um_ref, ads_ref, u_hbm, um_hbm, a_hbm, am_hbm, turned, sems, user_sems):
     copies = [
         pltpu.make_async_copy(u_ref, u_hbm, user_sems.at[0]),
         pltpu.make_async_copy(um_ref, um_hbm, user_sems.at[1]),
     ]
     for c in copies:
         c.start()
-    for c in copies + turn_out(xt_ref, x_hbm, x_ref, sems):
+    size = turned.shape[1] // PARTS_OUT
+    for t, out_hbm in enumerate((a_hbm, am_hbm)):
+        for k in range(PARTS_OUT):
+            rows = pl.ds(k * size, size)
+            turned[t, rows, :] = ads_ref[t, :, rows].T
+            copies.append(pltpu.make_async_copy(turned.at[t, rows, :], out_hbm.at[rows, :], sems.at[t * PARTS_OUT + k]))
+            copies[-1].start()
+    for c in copies:
         c.wait()
 
 
@@ -328,74 +323,61 @@
     prep_shapes = [shape(groups, nu, na, dtype=BF16), shape(groups, nu, 128), shape(groups, 8, na)]
     prep_scratch = [pltpu.VMEM(s.shape, s.dtype) for s in prep_shapes]
 
-    def prepare_for(rnd, away, after, pack=None):
-        lists = [] if pack is None else [shape(8, max(edges, n), dtype=jnp.int32)]
-        return call(
-            functools.partial(prepare_kernel, rnd, away, pack), (after, *indices), prep_shapes + lists,
-            [*index_scratch, sems], hbm=3, name="counts",
-        )
-
-    def first_group(u, um, at, prep, *after):
-        return call(embedding_kernel, (u, um, at, *prep, *after), [table_u, table_u, table_a], name="group_first")
-
     def update(u, um, g):
         return call(users_kernel, (u, um, *g), [table_u, table_u], name="users_update")
 
     stay, away = (0, False), (0, True)
-    u, um, at, amt, *g = call(
+    both_u, both_a = shape(2, nu, d), shape(2, d, na)
+    users_scratch = [pltpu.VMEM((nu, d), F32)] * 2
+    u, um, ads_now, *g = call(
         first_round_kernel,
         (*indices, users, ads, user_moms, ad_moments),
-        [table_u, table_u, table_a, table_a, *parts],
-        [*index_scratch, *prep_scratch, *[pltpu.VMEM((nu, d), F32)] * 2, *[pltpu.VMEM((na, d), F32)] * 2, sems, pltpu.SemaphoreType.DMA((4,))],
+        [table_u, table_u, both_a, *parts],
+        [*index_scratch, *prep_scratch, *users_scratch, *[pltpu.VMEM((na, d), F32)] * 2, sems, pltpu.SemaphoreType.DMA((4,))],
         hbm=7, name="round_first",
     )
-    near = move((at, amt), (1, False), (-1, False))
-    far = move((at, amt), (1, False), (1, False))
+    (near,) = move((ads_now,), (1, False), (-1, False))
+    (far,) = move((ads_now,), (1, False), (1, False))
     u, um = update(u, um, g)
-    *prep, lists = prepare_for(1, False, um, rounds - 1)
-
+    *prep, lists = call(
+        functools.partial(prepare_kernel, 1, rounds - 1), (um, *indices),
+        prep_shapes + [shape(8, max(edges, n), dtype=jnp.int32)], [*index_scratch, sems], hbm=3, name="counts_1",
+    )
     (lists,) = move((lists,), (-4, False), stay, stay, stay)
 
-    u_early, um_early, ga = first_group(u, um, near[0], prep)
-    ads_early, after = call(
-        early_kernel, (u_early, um_early, *near, ga, *prep), [shape(2, d, na), shape(2, nu, d)], name="group_second_early",
-    )
+    ads_early, after = call(early_kernel, (u, um, near, *prep), [both_a, both_u], users_scratch, name="round_early")
     (ads_early,) = move((ads_early,), (1, False), (1, True))
     (users_early,) = move((after,), stay, away)
 
-    u, um, ga = first_group(u, um, far[0], prep, after)
-    at, amt, *g = call(moment_kernel, (u, *far, ga, *prep), [table_a, table_a, *parts], name="group_second")
+    u, um, at, amt, *g = call(
+        late_kernel, (u, um, far, *prep, after), [table_u, table_u, table_a, table_a, *parts], name="round_late",
+    )
     ads_late = move((at, amt), (1, False), (-1, False))
     u, um = update(u, um, g)
-    prep = prepare_for(2, True, um)
-
-    u, um, ga = call(
-        embedding_pick_kernel, (u, um, users_early, ads_early, ads_late[0], *prep), [table_u, table_u, table_a],
-        name="group_first_pick",
-    )
+    preps = call(
+        functools.partial(prepare_both_kernel, 2), (um, lists, *indices), prep_shapes * 2, [*index_scratch, sems], hbm=3,
+        name="counts_23",
+    )
+    prep, prep_last = preps[: len(prep_shapes)], preps[len(prep_shapes) :]
+
     u, um, at, amt = call(
-        moment_pick_kernel, (u, um, ads_early, *ads_late, ga, *prep),
-        [table_u, table_u, table_a, table_a], name="group_second_pick",
-    )
-    after = um
+        pick_kernel, (u, um, users_early, ads_early, *ads_late, *prep), [table_u, table_u, table_a, table_a],
+        users_scratch, name="round_pick",
+    )
     at, amt = move((at, amt), (1, False), (1, True), (1, False), (-3, True))
     u, um = move((u, um), (-4, False), away, stay, away)
-    prep = call(functools.partial(prepare_packed_kernel, edges, n), (after, lists), prep_shapes, name="counts_moved")
-    gu, ga = call(gradient_kernel, (u, at, *prep), [table_u, table_a], name="group_first_gradients")
-    u, um, at, amt = call(
-        both_moments_kernel, (u, um, at, amt, gu, ga, *prep), [table_u, table_u, table_a, table_a],
-        [pltpu.VMEM((nu, d), F32)] * 2, name="group_second_both",
-    )
-    at, amt = move((at, amt), (1, True), (-3, True), (-3, True), (-3, True))
+    gu, ga = call(gradient_kernel, (u, at, *prep_last), [table_u, table_a], name="round_last_gradients")
+    u, um, ads_now = call(
+        both_moments_kernel, (u, um, at, amt, gu, ga, *prep_last), [table_u, table_u, both_a], users_scratch,
+        name="round_last",
+    )
+    (ads_now,) = move((ads_now,), (1, True), (-3, True), (-3, True), (-3, True))
     u, um = move((u, um), (4, False), stay, stay, stay)
-    upright = pltpu.HBM((na, d), F32)
-    turn_scratch = [pltpu.VMEM((na, d), F32), pltpu.SemaphoreType.DMA((PARTS_OUT,))]
-    (a,) = call(ads_out_kernel, (at,), [upright], turn_scratch, name="ads_out", out_place=pltpu.HBM)
-    u, um, am = call(
-        last_kernel, (u, um, amt), [pltpu.HBM((nu, d), F32)] * 2 + [upright],
-        [*turn_scratch, pltpu.SemaphoreType.DMA((2,))], name="last_out", out_place=pltpu.HBM,
-    )
-    return u, um, a, am
+    return call(
+        last_kernel, (u, um, ads_now), [pltpu.HBM((nu, d), F32)] * 2 + [pltpu.HBM((na, d), F32)] * 2,
+        [pltpu.VMEM((2, na, d), F32), pltpu.SemaphoreType.DMA((2 * PARTS_OUT,)), pltpu.SemaphoreType.DMA((2,))],
+        name="last_out", out_place=pltpu.HBM,
+    )
 
 
 def solution(mesh):

time: 83.8 us -> 82.9 us (0.989)
  waiting for transfers between devices: 30.8 us -> 34.3 us
  Pallas kernels: 30 us -> 27.5 us
  starting transfers between devices: 20.3 us -> 19.1 us
    ppermute x17 -> x14, waiting for transfers between devices: 30.8 us -> 34.3 us  [move(): return tuple((lax.ppermute(x, AXES, route) for x in arrays))]
    pallas_call x16 -> x11, Pallas kernels: 30 us -> 27.5 us  [call(): pl.pallas_call(kernel, out_shape=outs, in_specs=[vmem] * split_at + [pl.B...]
    ppermute x17 -> x14, starting transfers between devices: 20.3 us -> 19.1 us  [move(): return tuple((lax.ppermute(x, AXES, route) for x in arrays))]
  transfers between devices with their start and end apart: 17 -> 14, of which waited for: 6 -> 9; matrix products, arithmetic and copies ran while one was open for 0% -> 0% of each run, Pallas kernels for 23% -> 18%
where the time goes in v4:
time: 82.9 us; the launch traced here: 82 us
  waiting for transfers between devices  34.3 us (41%)
  Pallas kernels  27.5 us (33%)
  starting transfers between devices  19.1 us (23%)
  between operations  1 us (1%)
    ppermute x14, waiting for transfers between devices, move(): return tuple((lax.ppermute(x, AXES, route) for x in arrays))  34.3 us
    pallas_call x11, Pallas kernels, call(): pl.pallas_call(kernel, out_shape=outs, in_specs=[vmem] * split_at + [pl.B...  27.5 us
    ppermute x14, starting transfers between devices, move(): return tuple((lax.ppermute(x, AXES, route) for x in arrays))  19.1 us
  transfers between devices with their start and end apart: 14, of which 9 were waited for; matrix products, arithmetic and copies ran while one was open for 0% of the time, Pallas kernels for 18%

profile of v4, /device:TPU:192, one launch (start us, length us, event | category | flops | bytes accessed | tf_op | source)
XLA Modules:
  0.0 82.0 jit_solution(14945406180878757234)
XLA Ops:
  0.6 5.3 %round_first.1 = (f32[512,256]{1,0:T(8,128)S(1)}, f32[512,256]{1,0:T(8,128)S(1)}, f32[2,256,512]{2,1,0:T(8,128)S(1)}, bf16[512,512]{1,0:T(8,128)(2,1)S(1)}, bf16...) custom-call(s32[1,16,4,512]{3,2,1,0:T(4,128)} %pu_hbm.5, ...), custom_call_target="tpu_custom_call" | custom-call | flops 1 | bytes 1 | tf_op jit(solution)/shard_map/round_first/pallas_call | solution.py:264
  5.9 0.1 collective-permute-start.1
  6.0 0.5 collective-permute-start
  6.5 0.8 users_update.2
  7.3 1.5 %counts_1.1 = (bf16[2,512,512]{2,1,0:T(8,128)(2,1)S(1)}, f32[2,512,128]{2,1,0:T(8,128)S(1)}, f32[2,8,512]{2,1,0:T(8,128)S(1)}, s32[8,512]{1,0:T(8,128)S(1)}) custom-call(f32[512,256]{1,0:T(8,128)S(1)} %get-tuple-element.51.after_ref.um_ref, s32[1,16,4,512]{3,2,1,0:T(4,128)} %pu_hbm.5, s32[1,16,4,512]{3,2,1,0:T(4,128)} %pa_hbm.5, s32[1,16,4,2,512]{4,3,2,1,0:T(2,128)} %ng_hbm.5), custom_call_target="tpu_custom_call" | custom-call | flops 1 | bytes 1 | tf_op jit(solution)/shard_map/counts_1/pallas_call | solution.py:264
  8.8 0.0 collective-permute-done.1.near_ref
  8.9 4.0 %round_early.1 = (f32[2,256,512]{2,1,0:T(8,128)S(1)}, f32[2,512,256]{2,1,0:T(8,128)S(1)}) custom-call(f32[512,256]{1,0:T(8,128)S(1)} %get-tuple-element.50.u_ref, f32[512,256]{1,0:T(8,128)S(1)} %get-tuple-element.51.after_ref.um_ref, f32[2,256,512]{2,1,0:T(8,128)S(1)} %collective-permute-done.1.near_ref, bf16[2,512,512]{2,1,0:T(8,128)(2,1)S(1)} %get-tuple-element.53.mh, ...), custom_call_target="tpu_custom_call" | custom-call | flops 1 | bytes 1 | tf_op jit(solution)/shard_map/round_early/pallas_call | solution.py:264
  12.8 3.0 %collective-permute-start.3 = (f32[2,256,512]{2,1,0:T(8,128)S(1)}, f32[2,256,512]{2,1,0:T(8,128)S(1)}, u32[]{:S(2)}, u32[]{:S(2)}) collective-permute-start(f32[2,256,512]{2,1,0:T(8,128)S(1)} %get-tuple-element.65), channel_id=1, source_target_pairs={{0,16},{1,17},{2,18},{3,19},{4,20},{5,21},{6,22},{7,23},{8,24},{9,... | collective-permute-start | bytes 3145736 | tf_op jit(solution)/shard_map/ppermute | solution.py:302
  15.8 0.9 %collective-permute-start.2 = (f32[2,512,256]{2,1,0:T(8,128)S(1)}, f32[2,512,256]{2,1,0:T(8,128)S(1)}, u32[]{:S(2)}, u32[]{:S(2)}) collective-permute-start(f32[2,512,256]{2,1,0:T(8,128)S(1)} %get-tuple-element.56.after_ref), channel_id=1, source_target_pairs={{0,0},{1,1},{2,2},{3,3},{4,4},{5,5},{6,6},{7,7},{8,8},{9,9},{10,10... | collective-permute-start | bytes 3145736 | tf_op jit(solution)/shard_map/ppermute | solution.py:302
  16.7 7.4 %collective-permute-done.far_ref = f32[2,256,512]{2,1,0:T(8,128)S(1)} collective-permute-done((f32[2,256,512]{2,1,0:T(8,128)S(1)}, f32[2,256,512]{2,1,0:T(8,128)S(1)}, u32[]{:S(2)}, u32[]{:S(2)}) %collective-permute-start) | collective-permute-done | bytes 1048608 | tf_op jit(solution)/shard_map/ppermute | solution.py:302
  24.1 3.2 %round_late.1 = (f32[512,256]{1,0:T(8,128)S(1)}, f32[512,256]{1,0:T(8,128)S(1)}, f32[256,512]{1,0:T(8,128)S(1)}, f32[256,512]{1,0:T(8,128)S(1)}, bf16[512,512]{1...) custom-call(f32[512,256]{1,0:T(8,128)S(1)} %get-tuple-element.50.u_re, ...), custom_call_target="tpu_custom_call" | custom-call | flops 1 | bytes 1 | tf_op jit(solution)/shard_map/round_late/pallas_call | solution.py:264
  27.3 0.1 collective-permute-start.4
  27.4 0.5 collective-permute-start.5
  27.9 3.4 %collective-permute-start.6 = (s32[8,512]{1,0:T(8,128)S(1)}, s32[8,512]{1,0:T(8,128)S(1)}, u32[]{:S(2)}, u32[]{:S(2)}) collective-permute-start(s32[8,512]{1,0:T(8,128)S(1)} %get-tuple-element.68), channel_id=1, source_target_pairs={{0,192},{1,193},{2,194},{3,195},{4,196},{5,197},{6,198},{7,199},{8... | collective-permute-start | bytes 49160 | tf_op jit(solution)/shard_map/ppermute | solution.py:302
  31.3 0.8 users_update.3
  32.1 1.4 %collective-permute-done.6.lists_ref = s32[8,512]{1,0:T(8,128)S(1)} collective-permute-done((s32[8,512]{1,0:T(8,128)S(1)}, s32[8,512]{1,0:T(8,128)S(1)}, u32[]{:S(2)}, u32[]{:S(2)}) %collective-permute-start.6) | collective-permute-done | bytes 16416 | tf_op jit(solution)/shard_map/ppermute | solution.py:302
  33.6 2.1 %counts_23.1 = (bf16[2,512,512]{2,1,0:T(8,128)(2,1)S(1)}, f32[2,512,128]{2,1,0:T(8,128)S(1)}, f32[2,8,512]{2,1,0:T(8,128)S(1)}, bf16[2,512,512]{2,1,0:T(8,128)(2...) custom-call(f32[512,256]{1,0:T(8,128)S(1)} %get-tuple-element.64.after_ref.ume_ref, ...), custom_call_target="tpu_custom_call" | custom-call | flops 1 | bytes 1 | tf_op jit(solution)/shard_map/counts_23/pallas_call | solution.py:264
  35.7 0.0 collective-permute-done.4.ato_ref
  35.7 0.0 collective-permute-done.5.amto_ref
  35.7 0.2 collective-permute-done.3.ads_ref
  36.0 0.0 collective-permute-done.2.users_ref
  36.0 4.0 %round_pick.1 = (f32[512,256]{1,0:T(8,128)S(1)}, f32[512,256]{1,0:T(8,128)S(1)}, f32[256,512]{1,0:T(8,128)S(1)}, f32[256,512]{1,0:T(8,128)S(1)}) custom-call(f32[512,256]{1,0:T(8,128)S(1)} %get-tuple-element.63.ue_ref, f32[512,256]{1,0:T(8,128)S(1)} %get-tuple-element.64.after_ref.ume_ref, f32[2,512,256]{2,1,0:T(8,128)S(1)} %collective-permute-done.2.users_ref, ...), custom_call_target="tpu_custom_call" | custom-call | flops 1 | bytes 1 | tf_op jit(solution)/shard_map/round_pick/pallas_call | solution.py:264
  40.0 4.4 %collective-permute-start.7 = (f32[512,256]{1,0:T(8,128)S(1)}, f32[512,256]{1,0:T(8,128)S(1)}, u32[]{:S(2)}, u32[]{:S(2)}) collective-permute-start(f32[512,256]{1,0:T(8,128)S(1)} %get-tuple-element.72), channel_id=1, source_target_pairs={{0,192},{1,193},{2,194},{3,195},{4,196},{5,197},{6,198},{7,199},{8... | collective-permute-start | bytes 1572872 | tf_op jit(solution)/shard_map/ppermute | solution.py:302
  44.4 0.1 collective-permute-start.9
  44.5 1.9 %collective-permute-start.8 = (f32[512,256]{1,0:T(8,128)S(1)}, f32[512,256]{1,0:T(8,128)S(1)}, u32[]{:S(2)}, u32[]{:S(2)}) collective-permute-start(f32[512,256]{1,0:T(8,128)S(1)} %get-tuple-element.73), channel_id=1, source_target_pairs={{0,192},{1,193},{2,194},{3,195},{4,196},{5,197},{6,198},{7,199},{8... | collective-permute-start | bytes 1572872 | tf_op jit(solution)/shard_map/ppermute | solution.py:302
  46.5 0.3 collective-permute-start.10
  46.8 4.3 %collective-permute-done.7.u_ref = f32[512,256]{1,0:T(8,128)S(1)} collective-permute-done((f32[512,256]{1,0:T(8,128)S(1)}, f32[512,256]{1,0:T(8,128)S(1)}, u32[]{:S(2)}, u32[]{:S(2)}) %collective-permute-start.7) | collective-permute-done | bytes 524320 | tf_op jit(solution)/shard_map/ppermute | solution.py:302
  51.1 3.2 %collective-permute-done.9.at_ref = f32[256,512]{1,0:T(8,128)S(1)} collective-permute-done((f32[256,512]{1,0:T(8,128)S(1)}, f32[256,512]{1,0:T(8,128)S(1)}, u32[]{:S(2)}, u32[]{:S(2)}) %collective-permute-start.9) | collective-permute-done | bytes 524320 | tf_op jit(solution)/shard_map/ppermute | solution.py:302
  54.3 2.0 %round_last_gradients.1 = (f32[512,256]{1,0:T(8,128)S(1)}, f32[256,512]{1,0:T(8,128)S(1)}) custom-call(f32[512,256]{1,0:T(8,128)S(1)} %collective-permute-done.7.u_ref, f32[256,512]{1,0:T(8,128)S(1)} %collective-permute-done.9.at_ref, bf16[2,512,512]{2,1,0:T(8,128)(2,1)S(1)} %get-tuple-element.76.mh, f32[2,512,128]{2,1,0:T(8,128)S(1)} %get-tuple-element.77.cu, ...), custom_call_target="tpu_custom_call" | custom-call | flops 1 | bytes 1 | tf_op jit(solution)/shard_map/round_last_gradients/pallas_call | solution.py:264
  56.3 0.4 collective-permute-done.8.um_ref
  56.7 3.2 %collective-permute-done.10.amt_ref = f32[256,512]{1,0:T(8,128)S(1)} collective-permute-done((f32[256,512]{1,0:T(8,128)S(1)}, f32[256,512]{1,0:T(8,128)S(1)}, u32[]{:S(2)}, u32[]{:S(2)}) %collective-permute-start.10) | collective-permute-done | bytes 524320 | tf_op jit(solution)/shard_map/ppermute | solution.py:302
  59.9 2.4 %round_last.1 = (f32[512,256]{1,0:T(8,128)S(1)}, f32[512,256]{1,0:T(8,128)S(1)}, f32[2,256,512]{2,1,0:T(8,128)S(1)}) custom-call(f32[512,256]{1,0:T(8,128)S(1)} %collective-permute-done.7.u_ref, f32[512,256]{1,0:T(8,128)S(1)} %collective-permute-done.8.um_ref, f32[256,512]{1,0:T(8,128)S(1)} %collective-permute-done.9.at_ref, ...), custom_call_target="tpu_custom_call" | custom-call | flops 1 | bytes 1 | tf_op jit(solution)/shard_map/round_last/pallas_call | solution.py:264
  62.4 0.1 collective-permute-start.13
  62.5 1.9 %collective-permute-start.11 = (f32[512,256]{1,0:T(8,128)S(1)}, f32[512,256]{1,0:T(8,128)S(1)}, u32[]{:S(2)}, u32[]{:S(2)}) collective-permute-start(f32[512,256]{1,0:T(8,128)S(1)} %get-tuple-element.81), channel_id=1, source_target_pairs={{0,64},{1,65},{2,66},{3,67},{4,68},{5,69},{6,70},{7,71},{8,72},{9,... | collective-permute-start | bytes 1572872 | tf_op jit(solution)/shard_map/ppermute | solution.py:302
  64.4 1.9 %collective-permute-start.12 = (f32[512,256]{1,0:T(8,128)S(1)}, f32[512,256]{1,0:T(8,128)S(1)}, u32[]{:S(2)}, u32[]{:S(2)}) collective-permute-start(f32[512,256]{1,0:T(8,128)S(1)} %get-tuple-element.82), channel_id=1, source_target_pairs={{0,64},{1,65},{2,66},{3,67},{4,68},{5,69},{6,70},{7,71},{8,72},{9,... | collective-permute-start | bytes 1572872 | tf_op jit(solution)/shard_map/ppermute | solution.py:302
  66.3 8.4 %collective-permute-done.11.u_ref = f32[512,256]{1,0:T(8,128)S(1)} collective-permute-done((f32[512,256]{1,0:T(8,128)S(1)}, f32[512,256]{1,0:T(8,128)S(1)}, u32[]{:S(2)}, u32[]{:S(2)}) %collective-permute-start.11) | collective-permute-done | bytes 524320 | tf_op jit(solution)/shard_map/ppermute | solution.py:302
  74.8 5.6 %collective-permute-done.12.um_ref = f32[512,256]{1,0:T(8,128)S(1)} collective-permute-done((f32[512,256]{1,0:T(8,128)S(1)}, f32[512,256]{1,0:T(8,128)S(1)}, u32[]{:S(2)}, u32[]{:S(2)}) %collective-permute-start.12) | collective-permute-done | bytes 524320 | tf_op jit(solution)/shard_map/ppermute | solution.py:302
  80.4 0.0 collective-permute-done.13.ads_ref
  80.4 1.4 %last_out.1 = (f32[512,256]{1,0:T(8,128)}, f32[512,256]{1,0:T(8,128)}, f32[512,256]{1,0:T(8,128)}, f32[512,256]{1,0:T(8,128)}) custom-call(f32[512,256]{1,0:T(8,128)S(1)} %collective-permute-done.11.u_ref, f32[512,256]{1,0:T(8,128)S(1)} %collective-permute-done.12.um_ref, f32[2,256,512]{2,1,0:T(8,128)S(1)} %collective-permute-done.13.ads_ref), custom_call_target="tpu_custom_call" | custom-call | flops 1 | bytes 1 | tf_op jit(solution)/shard_map/last_out/pallas_call | solution.py:264
Async XLA Ops:
  5.9 2.9 %collective-permute-start.1 = (f32[2,256,512]{2,1,0:T(8,128)S(1)}, f32[2,256,512]{2,1,0:T(8,128)S(1)}, u32[]{:S(2)}, u32[]{:S(2)}) collective-permute-start(f32[2,256,512]{2,1,0:T(8,128)S(1)} %get-tuple-element.52), channel_id=1, source_target_pairs={{0,16},{1,17},{2,18},{3,19},{4,20},{5,21},{6,22},{7,23},{8,24},{9,... | collective-permute-start | bytes 3145736 | tf_op jit(solution)/shard_map/ppermute | solution.py:302
  6.0 18.1 %collective-permute-start = (f32[2,256,512]{2,1,0:T(8,128)S(1)}, f32[2,256,512]{2,1,0:T(8,128)S(1)}, u32[]{:S(2)}, u32[]{:S(2)}) collective-permute-start(f32[2,256,512]{2,1,0:T(8,128)S(1)} %get-tuple-element.52), channel_id=1, source_target_pairs={{0,16},{1,17},{2,18},{3,19},{4,20},{5,21},{6,22},{7,23},{8,24},{9,... | collective-permute-start | bytes 3145736 | tf_op jit(solution)/shard_map/ppermute | solution.py:302
  12.8 23.1 %collective-permute-start.3 = (f32[2,256,512]{2,1,0:T(8,128)S(1)}, f32[2,256,512]{2,1,0:T(8,128)S(1)}, u32[]{:S(2)}, u32[]{:S(2)}) collective-permute-start(f32[2,256,512]{2,1,0:T(8,128)S(1)} %get-tuple-element.65), channel_id=1, source_target_pairs={{0,16},{1,17},{2,18},{3,19},{4,20},{5,21},{6,22},{7,23},{8,24},{9,... | collective-permute-start | bytes 3145736 | tf_op jit(solution)/shard_map/ppermute | solution.py:302
  15.8 20.2 %collective-permute-start.2 = (f32[2,512,256]{2,1,0:T(8,128)S(1)}, f32[2,512,256]{2,1,0:T(8,128)S(1)}, u32[]{:S(2)}, u32[]{:S(2)}) collective-permute-start(f32[2,512,256]{2,1,0:T(8,128)S(1)} %get-tuple-element.56.after_ref), channel_id=1, source_target_pairs={{0,0},{1,1},{2,2},{3,3},{4,4},{5,5},{6,6},{7,7},{8,8},{9,9},{10,10... | collective-permute-start | bytes 3145736 | tf_op jit(solution)/shard_map/ppermute | solution.py:302
  27.3 8.4 %collective-permute-start.4 = (f32[256,512]{1,0:T(8,128)S(1)}, f32[256,512]{1,0:T(8,128)S(1)}, u32[]{:S(2)}, u32[]{:S(2)}) collective-permute-start(f32[256,512]{1,0:T(8,128)S(1)} %get-tuple-element.66), channel_id=1, source_target_pairs={{0,16},{1,17},{2,18},{3,19},{4,20},{5,21},{6,22},{7,23},{8,24},{9,... | collective-permute-start | bytes 1572872 | tf_op jit(solution)/shard_map/ppermute | solution.py:302
  27.4 8.3 %collective-permute-start.5 = (f32[256,512]{1,0:T(8,128)S(1)}, f32[256,512]{1,0:T(8,128)S(1)}, u32[]{:S(2)}, u32[]{:S(2)}) collective-permute-start(f32[256,512]{1,0:T(8,128)S(1)} %get-tuple-element.67), channel_id=1, source_target_pairs={{0,16},{1,17},{2,18},{3,19},{4,20},{5,21},{6,22},{7,23},{8,24},{9,... | collective-permute-start | bytes 1572872 | tf_op jit(solution)/shard_map/ppermute | solution.py:302
  27.9 5.6 %collective-permute-start.6 = (s32[8,512]{1,0:T(8,128)S(1)}, s32[8,512]{1,0:T(8,128)S(1)}, u32[]{:S(2)}, u32[]{:S(2)}) collective-permute-start(s32[8,512]{1,0:T(8,128)S(1)} %get-tuple-element.68), channel_id=1, source_target_pairs={{0,192},{1,193},{2,194},{3,195},{4,196},{5,197},{6,198},{7,199},{8... | collective-permute-start | bytes 49160 | tf_op jit(solution)/shard_map/ppermute | solution.py:302
  40.0 11.1 %collective-permute-start.7 = (f32[512,256]{1,0:T(8,128)S(1)}, f32[512,256]{1,0:T(8,128)S(1)}, u32[]{:S(2)}, u32[]{:S(2)}) collective-permute-start(f32[512,256]{1,0:T(8,128)S(1)} %get-tuple-element.72), channel_id=1, source_target_pairs={{0,192},{1,193},{2,194},{3,195},{4,196},{5,197},{6,198},{7,199},{8... | collective-permute-start | bytes 1572872 | tf_op jit(solution)/shard_map/ppermute | solution.py:302
  44.4 9.9 %collective-permute-start.9 = (f32[256,512]{1,0:T(8,128)S(1)}, f32[256,512]{1,0:T(8,128)S(1)}, u32[]{:S(2)}, u32[]{:S(2)}) collective-permute-start(f32[256,512]{1,0:T(8,128)S(1)} %get-tuple-element.74), channel_id=1, source_target_pairs={{0,16},{1,17},{2,18},{3,19},{4,20},{5,21},{6,22},{7,23},{8,24},{9,... | collective-permute-start | bytes 1572872 | tf_op jit(solution)/shard_map/ppermute | solution.py:302
  44.5 12.2 %collective-permute-start.8 = (f32[512,256]{1,0:T(8,128)S(1)}, f32[512,256]{1,0:T(8,128)S(1)}, u32[]{:S(2)}, u32[]{:S(2)}) collective-permute-start(f32[512,256]{1,0:T(8,128)S(1)} %get-tuple-element.73), channel_id=1, source_target_pairs={{0,192},{1,193},{2,194},{3,195},{4,196},{5,197},{6,198},{7,199},{8... | collective-permute-start | bytes 1572872 | tf_op jit(solution)/shard_map/ppermute | solution.py:302
  46.5 13.5 %collective-permute-start.10 = (f32[256,512]{1,0:T(8,128)S(1)}, f32[256,512]{1,0:T(8,128)S(1)}, u32[]{:S(2)}, u32[]{:S(2)}) collective-permute-start(f32[256,512]{1,0:T(8,128)S(1)} %get-tuple-element.75), channel_id=1, source_target_pairs={{0,16},{1,17},{2,18},{3,19},{4,20},{5,21},{6,22},{7,23},{8,24},{9,... | collective-permute-start | bytes 1572872 | tf_op jit(solution)/shard_map/ppermute | solution.py:302
  62.4 18.0 %collective-permute-start.13 = (f32[2,256,512]{2,1,0:T(8,128)S(1)}, f32[2,256,512]{2,1,0:T(8,128)S(1)}, u32[]{:S(2)}, u32[]{:S(2)}) collective-permute-start(f32[2,256,512]{2,1,0:T(8,128)S(1)} %get-tuple-element.83), channel_id=1, source_target_pairs={{0,24},{1,25},{2,26},{3,27},{4,28},{5,29},{6,30},{7,31},{8,16},{9,... | collective-permute-start | bytes 3145736 | tf_op jit(solution)/shard_map/ppermute | solution.py:302
  62.5 12.3 %collective-permute-start.11 = (f32[512,256]{1,0:T(8,128)S(1)}, f32[512,256]{1,0:T(8,128)S(1)}, u32[]{:S(2)}, u32[]{:S(2)}) collective-permute-start(f32[512,256]{1,0:T(8,128)S(1)} %get-tuple-element.81), channel_id=1, source_target_pairs={{0,64},{1,65},{2,66},{3,67},{4,68},{5,69},{6,70},{7,71},{8,72},{9,... | collective-permute-start | bytes 1572872 | tf_op jit(solution)/shard_map/ppermute | solution.py:302
  64.4 16.0 %collective-permute-start.12 = (f32[512,256]{1,0:T(8,128)S(1)}, f32[512,256]{1,0:T(8,128)S(1)}, u32[]{:S(2)}, u32[]{:S(2)}) collective-permute-start(f32[512,256]{1,0:T(8,128)S(1)} %get-tuple-element.82), channel_id=1, source_target_pairs={{0,64},{1,65},{2,66},{3,67},{4,68},{5,69},{6,70},{7,71},{8,72},{9,... | collective-permute-start | bytes 1572872 | tf_op jit(solution)/shard_map/ppermute | solution.py:302

commit v5 on v4

--- a/solution.py
+++ b/solution.py
@@ -28,7 +28,7 @@
 
 def dot3(a, b, ca, cb):
     (ah, al), (bh, bl) = a, b
-    return dot(ah, bh, ca, cb) + (dot(ah, bl, ca, cb) + dot(al, bh, ca, cb))
+    return dot(jnp.concatenate([ah, al, ah], axis=ca), jnp.concatenate([bh, bh, bl], axis=cb), ca, cb)
 
 
 def adagrad(row, mom, grad):
@@ -55,8 +55,7 @@
         cn_ref[group, :, cols] = jnp.broadcast_to(counts[k : k + 1, :], (8, LANES))
 
 
-def gradient_matrix(u_hl, at_hl, mh, cu, cn):
-    s = dot3(u_hl, at_hl, 1, 0)
+def gradient_matrix(s, mh, cu, cn):
     t = jnp.tanh(0.5 * s)
     w = jnp.concatenate([cu] * (s.shape[1] // 128), axis=1) * cn
     m = mh.astype(F32)
@@ -69,17 +68,18 @@
 def group_pass(group, u_read, users, at_hl, prep, gu_out, g_out=None):
     mh_ref, cu_ref, cn_ref = prep
     cn = cn_ref[group, 0:1, :]
+    blocks = [pl.ds(r, BLOCK) for r in range(0, users, BLOCK)]
+    u_hl = [split(u_read(rows)) for rows in blocks]
+    scores = [dot3(u, at_hl, 1, 0) for u in u_hl]
     ga = None
-    for r in range(0, users, BLOCK):
-        rows = pl.ds(r, BLOCK)
-        u_hl = split(u_read(rows))
-        g_hl = gradient_matrix(u_hl, at_hl, mh_ref[group, rows, :], cu_ref[group, rows, :], cn)
-        part = dot3(u_hl, g_hl, 0, 0)
-        ga = part if ga is None else ga + part
+    for rows, u, s in zip(blocks, u_hl, scores):
+        g_hl = gradient_matrix(s, mh_ref[group, rows, :], cu_ref[group, rows, :], cn)
         if g_out is None:
             gu_out(rows, dot3(g_hl, at_hl, 1, 1))
         else:
             g_out[0][rows, :], g_out[1][rows, :] = g_hl
+        part = dot3(u, g_hl, 0, 0)
+        ga = part if ga is None else ga + part
     return ga
 
 
@@ -183,7 +183,7 @@
 
 
 def late_kernel(
-    u_ref, um_ref, far_ref, mh, cu, cn, after_ref,
+    u_ref, um_ref, far_ref, mh, cu, cn, after_ref, lists_ref,
     u1_ref, um1_ref, ato_ref, amto_ref, gh_ref, gl_ref, ah_ref, al_ref,
 ):
     prep = (mh, cu, cn)
@@ -350,7 +350,7 @@
     (users_early,) = move((after,), stay, away)
 
     u, um, at, amt, *g = call(
-        late_kernel, (u, um, far, *prep, after), [table_u, table_u, table_a, table_a, *parts], name="round_late",
+        late_kernel, (u, um, far, *prep, after, lists), [table_u, table_u, table_a, table_a, *parts], name="round_late",
     )
     ads_late = move((at, amt), (1, False), (-1, False))
     u, um = update(u, um, g)

time: 82.9 us -> 80.1 us (0.966)
  Pallas kernels: 27.5 us -> 24.6 us
  starting transfers between devices: 19.1 us -> 20.9 us
  waiting for transfers between devices: 34.3 us -> 33 us
    pallas_call x11, Pallas kernels: 27.5 us -> 24.6 us  [call(): pl.pallas_call(kernel, out_shape=outs, in_specs=[vmem] * split_at + [pl.B...]
    ppermute x14, starting transfers between devices: 19.1 us -> 20.9 us  [move(): return tuple((lax.ppermute(x, AXES, route) for x in arrays))]
    ppermute x14, waiting for transfers between devices: 34.3 us -> 33 us  [move(): return tuple((lax.ppermute(x, AXES, route) for x in arrays))]
  transfers between devices with their start and end apart: 14 -> 14, of which waited for: 9 -> 9; matrix products, arithmetic and copies ran while one was open for 0% -> 0% of each run, Pallas kernels for 18% -> 16%
where the time goes in v5:
time: 80.1 us; the launch traced here: 79.5 us
  waiting for transfers between devices  33 us (41%)
  Pallas kernels  24.6 us (31%)
  starting transfers between devices  20.9 us (26%)
  between operations  1 us (1%)
    ppermute x14, waiting for transfers between devices, move(): return tuple((lax.ppermute(x, AXES, route) for x in arrays))  33 us
    pallas_call x11, Pallas kernels, call(): pl.pallas_call(kernel, out_shape=outs, in_specs=[vmem] * split_at + [pl.B...  24.6 us
    ppermute x14, starting transfers between devices, move(): return tuple((lax.ppermute(x, AXES, route) for x in arrays))  20.9 us
  transfers between devices with their start and end apart: 14, of which 9 were waited for; matrix products, arithmetic and copies ran while one was open for 0% of the time, Pallas kernels for 16%

profile of v5, /device:TPU:192, one launch (start us, length us, event | category | flops | bytes accessed | tf_op | source)
XLA Modules:
  0.0 79.5 jit_solution(8139049094443038242)
XLA Ops:
  0.6 5.1 %round_first.1 = (f32[512,256]{1,0:T(8,128)S(1)}, f32[512,256]{1,0:T(8,128)S(1)}, f32[2,256,512]{2,1,0:T(8,128)S(1)}, bf16[512,512]{1,0:T(8,128)(2,1)S(1)}, bf16...) custom-call(s32[1,16,4,512]{3,2,1,0:T(4,128)} %pu_hbm.5, ...), custom_call_target="tpu_custom_call" | custom-call | flops 1 | bytes 1 | tf_op jit(solution)/shard_map/round_first/pallas_call | solution.py:264
  5.7 0.1 collective-permute-start.1
  5.8 0.5 collective-permute-start
  6.3 0.8 users_update.2
  7.1 1.5 %counts_1.1 = (bf16[2,512,512]{2,1,0:T(8,128)(2,1)S(1)}, f32[2,512,128]{2,1,0:T(8,128)S(1)}, f32[2,8,512]{2,1,0:T(8,128)S(1)}, s32[8,512]{1,0:T(8,128)S(1)}) custom-call(f32[512,256]{1,0:T(8,128)S(1)} %get-tuple-element.51.after_ref.um_ref, s32[1,16,4,512]{3,2,1,0:T(4,128)} %pu_hbm.5, s32[1,16,4,512]{3,2,1,0:T(4,128)} %pa_hbm.5, s32[1,16,4,2,512]{4,3,2,1,0:T(2,128)} %ng_hbm.5), custom_call_target="tpu_custom_call" | custom-call | flops 1 | bytes 1 | tf_op jit(solution)/shard_map/counts_1/pallas_call | solution.py:264
  8.6 0.0 collective-permute-done.1.near_ref
  8.6 3.2 %round_early.1 = (f32[2,256,512]{2,1,0:T(8,128)S(1)}, f32[2,512,256]{2,1,0:T(8,128)S(1)}) custom-call(f32[512,256]{1,0:T(8,128)S(1)} %get-tuple-element.50.u_ref, f32[512,256]{1,0:T(8,128)S(1)} %get-tuple-element.51.after_ref.um_ref, f32[2,256,512]{2,1,0:T(8,128)S(1)} %collective-permute-done.1.near_ref, bf16[2,512,512]{2,1,0:T(8,128)(2,1)S(1)} %get-tuple-element.53.mh, ...), custom_call_target="tpu_custom_call" | custom-call | flops 1 | bytes 1 | tf_op jit(solution)/shard_map/round_early/pallas_call | solution.py:264
  11.8 3.0 %collective-permute-start.4 = (f32[2,256,512]{2,1,0:T(8,128)S(1)}, f32[2,256,512]{2,1,0:T(8,128)S(1)}, u32[]{:S(2)}, u32[]{:S(2)}) collective-permute-start(f32[2,256,512]{2,1,0:T(8,128)S(1)} %get-tuple-element.66), channel_id=1, source_target_pairs={{0,16},{1,17},{2,18},{3,19},{4,20},{5,21},{6,22},{7,23},{8,24},{9,... | collective-permute-start | bytes 3145736 | tf_op jit(solution)/shard_map/ppermute | solution.py:302
  14.8 0.7 collective-permute-start.3
  15.5 4.9 %collective-permute-start.2 = (s32[8,512]{1,0:T(8,128)S(1)}, s32[8,512]{1,0:T(8,128)S(1)}, u32[]{:S(2)}, u32[]{:S(2)}) collective-permute-start(s32[8,512]{1,0:T(8,128)S(1)} %get-tuple-element.57), channel_id=1, source_target_pairs={{0,192},{1,193},{2,194},{3,195},{4,196},{5,197},{6,198},{7,199},{8... | collective-permute-start | bytes 49160 | tf_op jit(solution)/shard_map/ppermute | solution.py:302
  20.4 1.2 %collective-permute-done.2.lists_ref = s32[8,512]{1,0:T(8,128)S(1)} collective-permute-done((s32[8,512]{1,0:T(8,128)S(1)}, s32[8,512]{1,0:T(8,128)S(1)}, u32[]{:S(2)}, u32[]{:S(2)}) %collective-permute-start.2) | collective-permute-done | bytes 16416 | tf_op jit(solution)/shard_map/ppermute | solution.py:302
  21.6 2.3 %collective-permute-done.far_ref = f32[2,256,512]{2,1,0:T(8,128)S(1)} collective-permute-done((f32[2,256,512]{2,1,0:T(8,128)S(1)}, f32[2,256,512]{2,1,0:T(8,128)S(1)}, u32[]{:S(2)}, u32[]{:S(2)}) %collective-permute-start) | collective-permute-done | bytes 1048608 | tf_op jit(solution)/shard_map/ppermute | solution.py:302
  23.9 3.0 %round_late.1 = (f32[512,256]{1,0:T(8,128)S(1)}, f32[512,256]{1,0:T(8,128)S(1)}, f32[256,512]{1,0:T(8,128)S(1)}, f32[256,512]{1,0:T(8,128)S(1)}, bf16[512,512]{1...) custom-call(f32[512,256]{1,0:T(8,128)S(1)} %get-tuple-element.50.u_re, ...), custom_call_target="tpu_custom_call" | custom-call | flops 1 | bytes 1 | tf_op jit(solution)/shard_map/round_late/pallas_call | solution.py:264
  26.8 0.1 collective-permute-start.5
  26.9 0.5 collective-permute-start.6
  27.4 0.8 users_update.3
  28.2 2.1 %counts_23.1 = (bf16[2,512,512]{2,1,0:T(8,128)(2,1)S(1)}, f32[2,512,128]{2,1,0:T(8,128)S(1)}, f32[2,8,512]{2,1,0:T(8,128)S(1)}, bf16[2,512,512]{2,1,0:T(8,128)(2...) custom-call(f32[512,256]{1,0:T(8,128)S(1)} %get-tuple-element.65.after_ref.ume_ref, ...), custom_call_target="tpu_custom_call" | custom-call | flops 1 | bytes 1 | tf_op jit(solution)/shard_map/counts_23/pallas_call | solution.py:264
  30.4 0.0 collective-permute-done.5.ato_ref
  30.4 0.0 collective-permute-done.6.amto_ref
  30.4 5.3 %collective-permute-done.4.ads_ref = f32[2,256,512]{2,1,0:T(8,128)S(1)} collective-permute-done((f32[2,256,512]{2,1,0:T(8,128)S(1)}, f32[2,256,512]{2,1,0:T(8,128)S(1)}, u32[]{:S(2)}, u32[]{:S(2)}) %collective-permute-start.4) | collective-permute-done | bytes 1048608 | tf_op jit(solution)/shard_map/ppermute | solution.py:302
  35.7 0.0 collective-permute-done.3.users_ref
  35.7 3.3 %round_pick.1 = (f32[512,256]{1,0:T(8,128)S(1)}, f32[512,256]{1,0:T(8,128)S(1)}, f32[256,512]{1,0:T(8,128)S(1)}, f32[256,512]{1,0:T(8,128)S(1)}) custom-call(f32[512,256]{1,0:T(8,128)S(1)} %get-tuple-element.64.ue_ref, f32[512,256]{1,0:T(8,128)S(1)} %get-tuple-element.65.after_ref.ume_ref, f32[2,512,256]{2,1,0:T(8,128)S(1)} %collective-permute-done.3.users_ref, ...), custom_call_target="tpu_custom_call" | custom-call | flops 1 | bytes 1 | tf_op jit(solution)/shard_map/round_pick/pallas_call | solution.py:264
  39.0 3.5 %collective-permute-start.7 = (f32[512,256]{1,0:T(8,128)S(1)}, f32[512,256]{1,0:T(8,128)S(1)}, u32[]{:S(2)}, u32[]{:S(2)}) collective-permute-start(f32[512,256]{1,0:T(8,128)S(1)} %get-tuple-element.72), channel_id=1, source_target_pairs={{0,192},{1,193},{2,194},{3,195},{4,196},{5,197},{6,198},{7,199},{8... | collective-permute-start | bytes 1572872 | tf_op jit(solution)/shard_map/ppermute | solution.py:302
  42.5 0.1 collective-permute-start.9
  42.6 2.7 %collective-permute-start.8 = (f32[512,256]{1,0:T(8,128)S(1)}, f32[512,256]{1,0:T(8,128)S(1)}, u32[]{:S(2)}, u32[]{:S(2)}) collective-permute-start(f32[512,256]{1,0:T(8,128)S(1)} %get-tuple-element.73), channel_id=1, source_target_pairs={{0,192},{1,193},{2,194},{3,195},{4,196},{5,197},{6,198},{7,199},{8... | collective-permute-start | bytes 1572872 | tf_op jit(solution)/shard_map/ppermute | solution.py:302
  45.3 0.3 collective-permute-start.10
  45.6 4.5 %collective-permute-done.7.u_ref = f32[512,256]{1,0:T(8,128)S(1)} collective-permute-done((f32[512,256]{1,0:T(8,128)S(1)}, f32[512,256]{1,0:T(8,128)S(1)}, u32[]{:S(2)}, u32[]{:S(2)}) %collective-permute-start.7) | collective-permute-done | bytes 524320 | tf_op jit(solution)/shard_map/ppermute | solution.py:302
  50.1 2.3 %collective-permute-done.9.at_ref = f32[256,512]{1,0:T(8,128)S(1)} collective-permute-done((f32[256,512]{1,0:T(8,128)S(1)}, f32[256,512]{1,0:T(8,128)S(1)}, u32[]{:S(2)}, u32[]{:S(2)}) %collective-permute-start.9) | collective-permute-done | bytes 524320 | tf_op jit(solution)/shard_map/ppermute | solution.py:302
  52.4 1.5 %round_last_gradients.1 = (f32[512,256]{1,0:T(8,128)S(1)}, f32[256,512]{1,0:T(8,128)S(1)}) custom-call(f32[512,256]{1,0:T(8,128)S(1)} %collective-permute-done.7.u_ref, f32[256,512]{1,0:T(8,128)S(1)} %collective-permute-done.9.at_ref, bf16[2,512,512]{2,1,0:T(8,128)(2,1)S(1)} %get-tuple-element.76.mh, f32[2,512,128]{2,1,0:T(8,128)S(1)} %get-tuple-element.77.cu, ...), custom_call_target="tpu_custom_call" | custom-call | flops 1 | bytes 1 | tf_op jit(solution)/shard_map/round_last_gradients/pallas_call | solution.py:264
  53.9 1.8 %collective-permute-done.8.um_ref = f32[512,256]{1,0:T(8,128)S(1)} collective-permute-done((f32[512,256]{1,0:T(8,128)S(1)}, f32[512,256]{1,0:T(8,128)S(1)}, u32[]{:S(2)}, u32[]{:S(2)}) %collective-permute-start.8) | collective-permute-done | bytes 524320 | tf_op jit(solution)/shard_map/ppermute | solution.py:302
  55.7 2.3 %collective-permute-done.10.amt_ref = f32[256,512]{1,0:T(8,128)S(1)} collective-permute-done((f32[256,512]{1,0:T(8,128)S(1)}, f32[256,512]{1,0:T(8,128)S(1)}, u32[]{:S(2)}, u32[]{:S(2)}) %collective-permute-start.10) | collective-permute-done | bytes 524320 | tf_op jit(solution)/shard_map/ppermute | solution.py:302
  58.0 2.0 %round_last.1 = (f32[512,256]{1,0:T(8,128)S(1)}, f32[512,256]{1,0:T(8,128)S(1)}, f32[2,256,512]{2,1,0:T(8,128)S(1)}) custom-call(f32[512,256]{1,0:T(8,128)S(1)} %collective-permute-done.7.u_ref, f32[512,256]{1,0:T(8,128)S(1)} %collective-permute-done.8.um_ref, f32[256,512]{1,0:T(8,128)S(1)} %collective-permute-done.9.at_ref, ...), custom_call_target="tpu_custom_call" | custom-call | flops 1 | bytes 1 | tf_op jit(solution)/shard_map/round_last/pallas_call | solution.py:264
  60.0 0.1 collective-permute-start.13
  60.1 2.4 %collective-permute-start.11 = (f32[512,256]{1,0:T(8,128)S(1)}, f32[512,256]{1,0:T(8,128)S(1)}, u32[]{:S(2)}, u32[]{:S(2)}) collective-permute-start(f32[512,256]{1,0:T(8,128)S(1)} %get-tuple-element.81), channel_id=1, source_target_pairs={{0,64},{1,65},{2,66},{3,67},{4,68},{5,69},{6,70},{7,71},{8,72},{9,... | collective-permute-start | bytes 1572872 | tf_op jit(solution)/shard_map/ppermute | solution.py:302
  62.5 2.2 %collective-permute-start.12 = (f32[512,256]{1,0:T(8,128)S(1)}, f32[512,256]{1,0:T(8,128)S(1)}, u32[]{:S(2)}, u32[]{:S(2)}) collective-permute-start(f32[512,256]{1,0:T(8,128)S(1)} %get-tuple-element.82), channel_id=1, source_target_pairs={{0,64},{1,65},{2,66},{3,67},{4,68},{5,69},{6,70},{7,71},{8,72},{9,... | collective-permute-start | bytes 1572872 | tf_op jit(solution)/shard_map/ppermute | solution.py:302
  64.7 7.7 %collective-permute-done.11.u_ref = f32[512,256]{1,0:T(8,128)S(1)} collective-permute-done((f32[512,256]{1,0:T(8,128)S(1)}, f32[512,256]{1,0:T(8,128)S(1)}, u32[]{:S(2)}, u32[]{:S(2)}) %collective-permute-start.11) | collective-permute-done | bytes 524320 | tf_op jit(solution)/shard_map/ppermute | solution.py:302
  72.4 5.6 %collective-permute-done.12.um_ref = f32[512,256]{1,0:T(8,128)S(1)} collective-permute-done((f32[512,256]{1,0:T(8,128)S(1)}, f32[512,256]{1,0:T(8,128)S(1)}, u32[]{:S(2)}, u32[]{:S(2)}) %collective-permute-start.12) | collective-permute-done | bytes 524320 | tf_op jit(solution)/shard_map/ppermute | solution.py:302
  78.0 0.0 collective-permute-done.13.ads_ref
  78.0 1.4 %last_out.1 = (f32[512,256]{1,0:T(8,128)}, f32[512,256]{1,0:T(8,128)}, f32[512,256]{1,0:T(8,128)}, f32[512,256]{1,0:T(8,128)}) custom-call(f32[512,256]{1,0:T(8,128)S(1)} %collective-permute-done.11.u_ref, f32[512,256]{1,0:T(8,128)S(1)} %collective-permute-done.12.um_ref, f32[2,256,512]{2,1,0:T(8,128)S(1)} %collective-permute-done.13.ads_ref), custom_call_target="tpu_custom_call" | custom-call | flops 1 | bytes 1 | tf_op jit(solution)/shard_map/last_out/pallas_call | solution.py:264
Async XLA Ops:
  5.7 2.9 %collective-permute-start.1 = (f32[2,256,512]{2,1,0:T(8,128)S(1)}, f32[2,256,512]{2,1,0:T(8,128)S(1)}, u32[]{:S(2)}, u32[]{:S(2)}) collective-permute-start(f32[2,256,512]{2,1,0:T(8,128)S(1)} %get-tuple-element.52), channel_id=1, source_target_pairs={{0,16},{1,17},{2,18},{3,19},{4,20},{5,21},{6,22},{7,23},{8,24},{9,... | collective-permute-start | bytes 3145736 | tf_op jit(solution)/shard_map/ppermute | solution.py:302
  5.8 18.1 %collective-permute-start = (f32[2,256,512]{2,1,0:T(8,128)S(1)}, f32[2,256,512]{2,1,0:T(8,128)S(1)}, u32[]{:S(2)}, u32[]{:S(2)}) collective-permute-start(f32[2,256,512]{2,1,0:T(8,128)S(1)} %get-tuple-element.52), channel_id=1, source_target_pairs={{0,16},{1,17},{2,18},{3,19},{4,20},{5,21},{6,22},{7,23},{8,24},{9,... | collective-permute-start | bytes 3145736 | tf_op jit(solution)/shard_map/ppermute | solution.py:302
  11.8 23.9 %collective-permute-start.4 = (f32[2,256,512]{2,1,0:T(8,128)S(1)}, f32[2,256,512]{2,1,0:T(8,128)S(1)}, u32[]{:S(2)}, u32[]{:S(2)}) collective-permute-start(f32[2,256,512]{2,1,0:T(8,128)S(1)} %get-tuple-element.66), channel_id=1, source_target_pairs={{0,16},{1,17},{2,18},{3,19},{4,20},{5,21},{6,22},{7,23},{8,24},{9,... | collective-permute-start | bytes 3145736 | tf_op jit(solution)/shard_map/ppermute | solution.py:302
  14.8 21.0 %collective-permute-start.3 = (f32[2,512,256]{2,1,0:T(8,128)S(1)}, f32[2,512,256]{2,1,0:T(8,128)S(1)}, u32[]{:S(2)}, u32[]{:S(2)}) collective-permute-start(f32[2,512,256]{2,1,0:T(8,128)S(1)} %get-tuple-element.56.after_ref), channel_id=1, source_target_pairs={{0,0},{1,1},{2,2},{3,3},{4,4},{5,5},{6,6},{7,7},{8,8},{9,9},{10,10... | collective-permute-start | bytes 3145736 | tf_op jit(solution)/shard_map/ppermute | solution.py:302
  15.5 6.1 %collective-permute-start.2 = (s32[8,512]{1,0:T(8,128)S(1)}, s32[8,512]{1,0:T(8,128)S(1)}, u32[]{:S(2)}, u32[]{:S(2)}) collective-permute-start(s32[8,512]{1,0:T(8,128)S(1)} %get-tuple-element.57), channel_id=1, source_target_pairs={{0,192},{1,193},{2,194},{3,195},{4,196},{5,197},{6,198},{7,199},{8... | collective-permute-start | bytes 49160 | tf_op jit(solution)/shard_map/ppermute | solution.py:302
  26.8 3.5 %collective-permute-start.5 = (f32[256,512]{1,0:T(8,128)S(1)}, f32[256,512]{1,0:T(8,128)S(1)}, u32[]{:S(2)}, u32[]{:S(2)}) collective-permute-start(f32[256,512]{1,0:T(8,128)S(1)} %get-tuple-element.67), channel_id=1, source_target_pairs={{0,16},{1,17},{2,18},{3,19},{4,20},{5,21},{6,22},{7,23},{8,24},{9,... | collective-permute-start | bytes 1572872 | tf_op jit(solution)/shard_map/ppermute | solution.py:302
  26.9 3.4 %collective-permute-start.6 = (f32[256,512]{1,0:T(8,128)S(1)}, f32[256,512]{1,0:T(8,128)S(1)}, u32[]{:S(2)}, u32[]{:S(2)}) collective-permute-start(f32[256,512]{1,0:T(8,128)S(1)} %get-tuple-element.68), channel_id=1, source_target_pairs={{0,16},{1,17},{2,18},{3,19},{4,20},{5,21},{6,22},{7,23},{8,24},{9,... | collective-permute-start | bytes 1572872 | tf_op jit(solution)/shard_map/ppermute | solution.py:302
  39.0 11.1 %collective-permute-start.7 = (f32[512,256]{1,0:T(8,128)S(1)}, f32[512,256]{1,0:T(8,128)S(1)}, u32[]{:S(2)}, u32[]{:S(2)}) collective-permute-start(f32[512,256]{1,0:T(8,128)S(1)} %get-tuple-element.72), channel_id=1, source_target_pairs={{0,192},{1,193},{2,194},{3,195},{4,196},{5,197},{6,198},{7,199},{8... | collective-permute-start | bytes 1572872 | tf_op jit(solution)/shard_map/ppermute | solution.py:302
  42.5 9.9 %collective-permute-start.9 = (f32[256,512]{1,0:T(8,128)S(1)}, f32[256,512]{1,0:T(8,128)S(1)}, u32[]{:S(2)}, u32[]{:S(2)}) collective-permute-start(f32[256,512]{1,0:T(8,128)S(1)} %get-tuple-element.74), channel_id=1, source_target_pairs={{0,16},{1,17},{2,18},{3,19},{4,20},{5,21},{6,22},{7,23},{8,24},{9,... | collective-permute-start | bytes 1572872 | tf_op jit(solution)/shard_map/ppermute | solution.py:302
  42.6 13.1 %collective-permute-start.8 = (f32[512,256]{1,0:T(8,128)S(1)}, f32[512,256]{1,0:T(8,128)S(1)}, u32[]{:S(2)}, u32[]{:S(2)}) collective-permute-start(f32[512,256]{1,0:T(8,128)S(1)} %get-tuple-element.73), channel_id=1, source_target_pairs={{0,192},{1,193},{2,194},{3,195},{4,196},{5,197},{6,198},{7,199},{8... | collective-permute-start | bytes 1572872 | tf_op jit(solution)/shard_map/ppermute | solution.py:302
  45.3 12.7 %collective-permute-start.10 = (f32[256,512]{1,0:T(8,128)S(1)}, f32[256,512]{1,0:T(8,128)S(1)}, u32[]{:S(2)}, u32[]{:S(2)}) collective-permute-start(f32[256,512]{1,0:T(8,128)S(1)} %get-tuple-element.75), channel_id=1, source_target_pairs={{0,16},{1,17},{2,18},{3,19},{4,20},{5,21},{6,22},{7,23},{8,24},{9,... | collective-permute-start | bytes 1572872 | tf_op jit(solution)/shard_map/ppermute | solution.py:302
  60.0 18.0 %collective-permute-start.13 = (f32[2,256,512]{2,1,0:T(8,128)S(1)}, f32[2,256,512]{2,1,0:T(8,128)S(1)}, u32[]{:S(2)}, u32[]{:S(2)}) collective-permute-start(f32[2,256,512]{2,1,0:T(8,128)S(1)} %get-tuple-element.83), channel_id=1, source_target_pairs={{0,24},{1,25},{2,26},{3,27},{4,28},{5,29},{6,30},{7,31},{8,16},{9,... | collective-permute-start | bytes 3145736 | tf_op jit(solution)/shard_map/ppermute | solution.py:302
  60.1 12.3 %collective-permute-start.11 = (f32[512,256]{1,0:T(8,128)S(1)}, f32[512,256]{1,0:T(8,128)S(1)}, u32[]{:S(2)}, u32[]{:S(2)}) collective-permute-start(f32[512,256]{1,0:T(8,128)S(1)} %get-tuple-element.81), channel_id=1, source_target_pairs={{0,64},{1,65},{2,66},{3,67},{4,68},{5,69},{6,70},{7,71},{8,72},{9,... | collective-permute-start | bytes 1572872 | tf_op jit(solution)/shard_map/ppermute | solution.py:302
  62.5 15.5 %collective-permute-start.12 = (f32[512,256]{1,0:T(8,128)S(1)}, f32[512,256]{1,0:T(8,128)S(1)}, u32[]{:S(2)}, u32[]{:S(2)}) collective-permute-start(f32[512,256]{1,0:T(8,128)S(1)} %get-tuple-element.82), channel_id=1, source_target_pairs={{0,64},{1,65},{2,66},{3,67},{4,68},{5,69},{6,70},{7,71},{8,72},{9,... | collective-permute-start | bytes 1572872 | tf_op jit(solution)/shard_map/ppermute | solution.py:302

commit v6 on v5

--- a/solution.py
+++ b/solution.py
@@ -140,8 +140,8 @@
 
 def first_round_kernel(
     pu_hbm, pa_hbm, ng_hbm, u_hbm, a_hbm, um_hbm, am_hbm,
-    uo_ref, umo_ref, ads_ref, gh_ref, gl_ref, ah_ref, al_ref,
-    pu, pa, ng, mh, cu, cn, u_ref, um_ref, a_ref, am_ref, sems, table_sems,
+    uo_ref, umo_ref, ads_ref, gh_ref, gl_ref, ah_ref, al_ref, pu, pa, ng,
+    mh, cu, cn, u_ref, um_ref, a_ref, am_ref, sems, table_sems,
 ):
     copies = fetch_indices(pu_hbm, pa_hbm, ng_hbm, pu, pa, ng, sems)
     tables = [
@@ -197,33 +197,23 @@
 
 def pick_kernel(
     ue_ref, ume_ref, users_ref, ads_ref, ato_ref, amto_ref, mh, cu, cn,
-    un_ref, umn_ref, atn_ref, amtn_ref, u1_ref, um1_ref,
+    ads_out_ref, users_out_ref, u1_ref, um1_ref,
 ):
     odd = on_odd_core()
     at = jnp.where(odd, ato_ref[...], ads_ref[0])
     amt = jnp.where(odd, amto_ref[...], ads_ref[1])
     u_read, um_read = picker(odd, ue_ref, users_ref.at[0]), picker(odd, ume_ref, users_ref.at[1])
-    atn_ref[...], amtn_ref[...] = meeting(
-        u_read, um_read, at, amt, (mh, cu, cn), u1_ref, um1_ref, un_ref, umn_ref
-    )
-
-
-def gradient_kernel(u_ref, at_ref, mh, cu, cn, gu_ref, ga_ref):
-    def put(rows, grad):
-        gu_ref[rows, :] = grad
-
-    ga_ref[...] = group_pass(0, reader(u_ref), u_ref.shape[0], split(at_ref[...]), (mh, cu, cn), put)
-
-
-def both_moments_kernel(
-    u_ref, um_ref, at_ref, amt_ref, gu_ref, ga_ref, mh, cu, cn,
-    uo_ref, umo_ref, ads_ref, u1_ref, um1_ref,
-):
-    u1_ref[...], um1_ref[...] = adagrad(u_ref[...], um_ref[...], gu_ref[...])
-    at1, amt1 = adagrad(at_ref[...], amt_ref[...], ga_ref[...])
-    put = update_users(reader(u1_ref), reader(um1_ref), uo_ref, umo_ref)
-    ga = group_pass(1, reader(u1_ref), u_ref.shape[0], split(at1), (mh, cu, cn), put)
-    ads_ref[0], ads_ref[1] = adagrad(at1, amt1, ga)
+    ads_out_ref[0], ads_out_ref[1] = meeting(
+        u_read, um_read, at, amt, (mh, cu, cn), u1_ref, um1_ref, users_out_ref.at[0], users_out_ref.at[1]
+    )
+
+
+def whole_kernel(users_ref, ads_ref, mh, cu, cn, ads_out_ref, users_out_ref, u1_ref, um1_ref):
+    u_read, um_read = reader(users_ref.at[0]), reader(users_ref.at[1])
+    ads_out_ref[0], ads_out_ref[1] = meeting(
+        u_read, um_read, ads_ref[0], ads_ref[1], (mh, cu, cn), u1_ref, um1_ref,
+        users_out_ref.at[0], users_out_ref.at[1],
+    )
 
 
 def users_kernel(u_ref, um_ref, gh_ref, gl_ref, ah_ref, al_ref, uo_ref, umo_ref):
@@ -234,9 +224,7 @@
         put(rows, dot3((gh_ref[rows, :], gl_ref[rows, :]), at_hl, 1, 1))
 
 
-def prepare_kernel(rnd, pack, after_ref, pu_hbm, pa_hbm, ng_hbm, mh, cu, cn, lists_ref, pu, pa, ng, sems):
-    for c in (copies := fetch_indices(pu_hbm, pa_hbm, ng_hbm, pu, pa, ng, sems)):
-        c.wait()
+def prepare_kernel(rnd, pack, after_ref, pu, pa, ng, mh, cu, cn, lists_ref):
     prepare_round(rnd, pu, pa, ng, mh.shape[1], mh.shape[2], (mh, cu, cn))
     pack_lists(pack, pu, pa, ng, lists_ref)
 
@@ -273,10 +261,10 @@
     )(*ins[:split_at], *far)
 
 
-def last_kernel(u_ref, um_ref, ads_ref, u_hbm, um_hbm, a_hbm, am_hbm, turned, sems, user_sems):
+def last_kernel(ads_ref, users_ref, u_hbm, um_hbm, a_hbm, am_hbm, turned, sems, user_sems):
     copies = [
-        pltpu.make_async_copy(u_ref, u_hbm, user_sems.at[0]),
-        pltpu.make_async_copy(um_ref, um_hbm, user_sems.at[1]),
+        pltpu.make_async_copy(users_ref.at[0], u_hbm, user_sems.at[0]),
+        pltpu.make_async_copy(users_ref.at[1], um_hbm, user_sems.at[1]),
     ]
     for c in copies:
         c.start()
@@ -329,19 +317,21 @@
     stay, away = (0, False), (0, True)
     both_u, both_a = shape(2, nu, d), shape(2, d, na)
     users_scratch = [pltpu.VMEM((nu, d), F32)] * 2
-    u, um, ads_now, *g = call(
+    own_lists = [shape(rounds, edges, dtype=jnp.int32)] * 2 + [shape(rounds, groups, n, dtype=jnp.int32)]
+    u, um, ads_now, *rest = call(
         first_round_kernel,
         (*indices, users, ads, user_moms, ad_moments),
-        [table_u, table_u, both_a, *parts],
-        [*index_scratch, *prep_scratch, *users_scratch, *[pltpu.VMEM((na, d), F32)] * 2, sems, pltpu.SemaphoreType.DMA((4,))],
+        [table_u, table_u, both_a, *parts, *own_lists],
+        [*prep_scratch, *users_scratch, *[pltpu.VMEM((na, d), F32)] * 2, sems, pltpu.SemaphoreType.DMA((4,))],
         hbm=7, name="round_first",
     )
+    g, own_lists = rest[: len(parts)], rest[len(parts) :]
     (near,) = move((ads_now,), (1, False), (-1, False))
     (far,) = move((ads_now,), (1, False), (1, False))
     u, um = update(u, um, g)
     *prep, lists = call(
-        functools.partial(prepare_kernel, 1, rounds - 1), (um, *indices),
-        prep_shapes + [shape(8, max(edges, n), dtype=jnp.int32)], [*index_scratch, sems], hbm=3, name="counts_1",
+        functools.partial(prepare_kernel, 1, rounds - 1), (um, *own_lists),
+        prep_shapes + [shape(8, max(edges, n), dtype=jnp.int32)], name="counts_1",
     )
     (lists,) = move((lists,), (-4, False), stay, stay, stay)
 
@@ -360,21 +350,18 @@
     )
     prep, prep_last = preps[: len(prep_shapes)], preps[len(prep_shapes) :]
 
-    u, um, at, amt = call(
-        pick_kernel, (u, um, users_early, ads_early, *ads_late, *prep), [table_u, table_u, table_a, table_a],
-        users_scratch, name="round_pick",
-    )
-    at, amt = move((at, amt), (1, False), (1, True), (1, False), (-3, True))
-    u, um = move((u, um), (-4, False), away, stay, away)
-    gu, ga = call(gradient_kernel, (u, at, *prep_last), [table_u, table_a], name="round_last_gradients")
-    u, um, ads_now = call(
-        both_moments_kernel, (u, um, at, amt, gu, ga, *prep_last), [table_u, table_u, both_a], users_scratch,
-        name="round_last",
-    )
+    ads_now, users_now = call(
+        pick_kernel, (u, um, users_early, ads_early, *ads_late, *prep), [both_a, both_u], users_scratch, name="round_pick",
+    )
+    (users_now,) = move((users_now,), (-4, False), away, stay, away)
+    (ads_now,) = move((ads_now,), (1, False), (1, True), (1, False), (-3, True))
+    ads_now, users_now = call(
+        whole_kernel, (users_now, ads_now, *prep_last), [both_a, both_u], users_scratch, name="round_last",
+    )
+    (users_now,) = move((users_now,), (4, False), stay, stay, stay)
     (ads_now,) = move((ads_now,), (1, True), (-3, True), (-3, True), (-3, True))
-    u, um = move((u, um), (4, False), stay, stay, stay)
     return call(
-        last_kernel, (u, um, ads_now), [pltpu.HBM((nu, d), F32)] * 2 + [pltpu.HBM((na, d), F32)] * 2,
+        last_kernel, (ads_now, users_now), [pltpu.HBM((nu, d), F32)] * 2 + [pltpu.HBM((na, d), F32)] * 2,
         [pltpu.VMEM((2, na, d), F32), pltpu.SemaphoreType.DMA((2 * PARTS_OUT,)), pltpu.SemaphoreType.DMA((2,))],
         name="last_out", out_place=pltpu.HBM,
     )

time: 80.1 us -> 81.4 us (1.016)
  waiting for transfers between devices: 33 us -> 41.2 us
  starting transfers between devices: 20.9 us -> 15.3 us
  Pallas kernels: 24.6 us -> 23.6 us
    ppermute x14 -> x11, waiting for transfers between devices: 33 us -> 41.2 us  [move(): return tuple((lax.ppermute(x, AXES, route) for x in arrays))]
    ppermute x14 -> x11, starting transfers between devices: 20.9 us -> 15.3 us  [move(): return tuple((lax.ppermute(x, AXES, route) for x in arrays))]
    pallas_call x11 -> x10, Pallas kernels: 24.6 us -> 23.6 us  [call(): pl.pallas_call(kernel, out_shape=outs, in_specs=[vmem] * split_at + [pl.B...]
  transfers between devices with their start and end apart: 14 -> 11, of which waited for: 9 -> 8; matrix products, arithmetic and copies ran while one was open for 0% -> 0% of each run, Pallas kernels for 16% -> 13%
where the time goes in v6:
time: 81.4 us; the launch traced here: 81.1 us
  waiting for transfers between devices  41.2 us (51%)
  Pallas kernels  23.6 us (29%)
  starting transfers between devices  15.3 us (19%)
  between operations  0.95 us (1%)
    ppermute x11, waiting for transfers between devices, move(): return tuple((lax.ppermute(x, AXES, route) for x in arrays))  41.2 us
    pallas_call x10, Pallas kernels, call(): pl.pallas_call(kernel, out_shape=outs, in_specs=[vmem] * split_at + [pl.B...  23.6 us
    ppermute x11, starting transfers between devices, move(): return tuple((lax.ppermute(x, AXES, route) for x in arrays))  15.3 us
  transfers between devices with their start and end apart: 11, of which 8 were waited for; matrix products, arithmetic and copies ran while one was open for 0% of the time, Pallas kernels for 13%

profile of v6, /device:TPU:192, one launch (start us, length us, event | category | flops | bytes accessed | tf_op | source)
XLA Modules:
  0.0 81.1 jit_solution(9964896720090516158)
XLA Ops:
  0.6 5.1 %round_first.1 = (f32[512,256]{1,0:T(8,128)S(1)}, f32[512,256]{1,0:T(8,128)S(1)}, f32[2,256,512]{2,1,0:T(8,128)S(1)}, bf16[512,512]{1,0:T(8,128)(2,1)S(1)}, bf16...) custom-call(s32[1,16,4,512]{3,2,1,0:T(4,128)} %pu_hbm.3, ...), custom_call_target="tpu_custom_call" | custom-call | flops 1 | bytes 1 | tf_op jit(solution)/shard_map/round_first/pallas_call | solution.py:252
  5.7 0.1 collective-permute-start.1
  5.8 0.5 collective-permute-start
  6.3 0.8 users_update.2
  7.1 0.7 counts_1.1
  7.8 0.6 collective-permute-done.1.near_ref
  8.4 3.2 %round_early.1 = (f32[2,256,512]{2,1,0:T(8,128)S(1)}, f32[2,512,256]{2,1,0:T(8,128)S(1)}) custom-call(f32[512,256]{1,0:T(8,128)S(1)} %get-tuple-element.48.u_ref, f32[512,256]{1,0:T(8,128)S(1)} %get-tuple-element.49.after_ref.um_ref, f32[2,256,512]{2,1,0:T(8,128)S(1)} %collective-permute-done.1.near_ref, bf16[2,512,512]{2,1,0:T(8,128)(2,1)S(1)} %get-tuple-element.54.mh, ...), custom_call_target="tpu_custom_call" | custom-call | flops 1 | bytes 1 | tf_op jit(solution)/shard_map/round_early/pallas_call | solution.py:252
  11.6 2.3 %collective-permute-start.4 = (f32[2,256,512]{2,1,0:T(8,128)S(1)}, f32[2,256,512]{2,1,0:T(8,128)S(1)}, u32[]{:S(2)}, u32[]{:S(2)}) collective-permute-start(f32[2,256,512]{2,1,0:T(8,128)S(1)} %get-tuple-element.67), channel_id=1, source_target_pairs={{0,16},{1,17},{2,18},{3,19},{4,20},{5,21},{6,22},{7,23},{8,24},{9,... | collective-permute-start | bytes 3145736 | tf_op jit(solution)/shard_map/ppermute | solution.py:290
  14.0 0.7 collective-permute-start.3
  14.7 4.8 %collective-permute-start.2 = (s32[8,512]{1,0:T(8,128)S(1)}, s32[8,512]{1,0:T(8,128)S(1)}, u32[]{:S(2)}, u32[]{:S(2)}) collective-permute-start(s32[8,512]{1,0:T(8,128)S(1)} %get-tuple-element.58), channel_id=1, source_target_pairs={{0,192},{1,193},{2,194},{3,195},{4,196},{5,197},{6,198},{7,199},{8... | collective-permute-start | bytes 49160 | tf_op jit(solution)/shard_map/ppermute | solution.py:290
  19.6 1.2 %collective-permute-done.2.lists_ref = s32[8,512]{1,0:T(8,128)S(1)} collective-permute-done((s32[8,512]{1,0:T(8,128)S(1)}, s32[8,512]{1,0:T(8,128)S(1)}, u32[]{:S(2)}, u32[]{:S(2)}) %collective-permute-start.2) | collective-permute-done | bytes 16416 | tf_op jit(solution)/shard_map/ppermute | solution.py:290
  20.8 3.1 %collective-permute-done.far_ref = f32[2,256,512]{2,1,0:T(8,128)S(1)} collective-permute-done((f32[2,256,512]{2,1,0:T(8,128)S(1)}, f32[2,256,512]{2,1,0:T(8,128)S(1)}, u32[]{:S(2)}, u32[]{:S(2)}) %collective-permute-start) | collective-permute-done | bytes 1048608 | tf_op jit(solution)/shard_map/ppermute | solution.py:290
  23.9 3.0 %round_late.1 = (f32[512,256]{1,0:T(8,128)S(1)}, f32[512,256]{1,0:T(8,128)S(1)}, f32[256,512]{1,0:T(8,128)S(1)}, f32[256,512]{1,0:T(8,128)S(1)}, bf16[512,512]{1...) custom-call(f32[512,256]{1,0:T(8,128)S(1)} %get-tuple-element.48.u_re, ...), custom_call_target="tpu_custom_call" | custom-call | flops 1 | bytes 1 | tf_op jit(solution)/shard_map/round_late/pallas_call | solution.py:252
  26.8 0.1 collective-permute-start.5
  26.9 0.5 collective-permute-start.6
  27.4 0.8 users_update.3
  28.2 2.1 %counts_23.1 = (bf16[2,512,512]{2,1,0:T(8,128)(2,1)S(1)}, f32[2,512,128]{2,1,0:T(8,128)S(1)}, f32[2,8,512]{2,1,0:T(8,128)S(1)}, bf16[2,512,512]{2,1,0:T(8,128)(2...) custom-call(f32[512,256]{1,0:T(8,128)S(1)} %get-tuple-element.66.after_ref.ume_ref, ...), custom_call_target="tpu_custom_call" | custom-call | flops 1 | bytes 1 | tf_op jit(solution)/shard_map/counts_23/pallas_call | solution.py:252
  30.4 0.0 collective-permute-done.5.ato_ref
  30.4 0.0 collective-permute-done.6.amto_ref
  30.4 5.3 %collective-permute-done.4.ads_ref = f32[2,256,512]{2,1,0:T(8,128)S(1)} collective-permute-done((f32[2,256,512]{2,1,0:T(8,128)S(1)}, f32[2,256,512]{2,1,0:T(8,128)S(1)}, u32[]{:S(2)}, u32[]{:S(2)}) %collective-permute-start.4) | collective-permute-done | bytes 1048608 | tf_op jit(solution)/shard_map/ppermute | solution.py:290
  35.7 0.0 collective-permute-done.3.users_ref
  35.7 3.3 %round_pick.1 = (f32[2,256,512]{2,1,0:T(8,128)S(1)}, f32[2,512,256]{2,1,0:T(8,128)S(1)}) custom-call(f32[512,256]{1,0:T(8,128)S(1)} %get-tuple-element.65.ue_ref, f32[512,256]{1,0:T(8,128)S(1)} %get-tuple-element.66.after_ref.ume_ref, f32[2,512,256]{2,1,0:T(8,128)S(1)} %collective-permute-done.3.users_ref, ...), custom_call_target="tpu_custom_call" | custom-call | flops 1 | bytes 1 | tf_op jit(solution)/shard_map/round_pick/pallas_call | solution.py:252
  39.0 3.5 %collective-permute-start.7 = (f32[2,512,256]{2,1,0:T(8,128)S(1)}, f32[2,512,256]{2,1,0:T(8,128)S(1)}, u32[]{:S(2)}, u32[]{:S(2)}) collective-permute-start(f32[2,512,256]{2,1,0:T(8,128)S(1)} %get-tuple-element.73), channel_id=1, source_target_pairs={{0,192},{1,193},{2,194},{3,195},{4,196},{5,197},{6,198},{7,199},{8... | collective-permute-start | bytes 3145736 | tf_op jit(solution)/shard_map/ppermute | solution.py:290
  42.5 0.3 collective-permute-start.8
  42.8 12.9 %collective-permute-done.7.users_ref = f32[2,512,256]{2,1,0:T(8,128)S(1)} collective-permute-done((f32[2,512,256]{2,1,0:T(8,128)S(1)}, f32[2,512,256]{2,1,0:T(8,128)S(1)}, u32[]{:S(2)}, u32[]{:S(2)}) %collective-permute-start.7) | collective-permute-done | bytes 1048608 | tf_op jit(solution)/shard_map/ppermute | solution.py:290
  55.7 2.5 %collective-permute-done.8.ads_ref = f32[2,256,512]{2,1,0:T(8,128)S(1)} collective-permute-done((f32[2,256,512]{2,1,0:T(8,128)S(1)}, f32[2,256,512]{2,1,0:T(8,128)S(1)}, u32[]{:S(2)}, u32[]{:S(2)}) %collective-permute-start.8) | collective-permute-done | bytes 1048608 | tf_op jit(solution)/shard_map/ppermute | solution.py:290
  58.2 3.2 %round_last.1 = (f32[2,256,512]{2,1,0:T(8,128)S(1)}, f32[2,512,256]{2,1,0:T(8,128)S(1)}) custom-call(f32[2,512,256]{2,1,0:T(8,128)S(1)} %collective-permute-done.7.users_ref, f32[2,256,512]{2,1,0:T(8,128)S(1)} %collective-permute-done.8.ads_ref, bf16[2,512,512]{2,1,0:T(8,128)(2,1)S(1)} %get-tuple-element.75.mh, f32[2,512,128]{2,1,0:T(8,128)S(1)} %get-tuple-element.76.cu, ...), custom_call_target="tpu_custom_call" | custom-call | flops 1 | bytes 1 | tf_op jit(solution)/shard_map/round_last/pallas_call | solution.py:252
  61.4 0.1 collective-permute-start.9
  61.5 2.4 %collective-permute-start.10 = (f32[2,512,256]{2,1,0:T(8,128)S(1)}, f32[2,512,256]{2,1,0:T(8,128)S(1)}, u32[]{:S(2)}, u32[]{:S(2)}) collective-permute-start(f32[2,512,256]{2,1,0:T(8,128)S(1)} %get-tuple-element.79), channel_id=1, source_target_pairs={{0,64},{1,65},{2,66},{3,67},{4,68},{5,69},{6,70},{7,71},{8,72},{9,... | collective-permute-start | bytes 3145736 | tf_op jit(solution)/shard_map/ppermute | solution.py:290
  63.9 13.0 %collective-permute-done.9.ads_ref = f32[2,256,512]{2,1,0:T(8,128)S(1)} collective-permute-done((f32[2,256,512]{2,1,0:T(8,128)S(1)}, f32[2,256,512]{2,1,0:T(8,128)S(1)}, u32[]{:S(2)}, u32[]{:S(2)}) %collective-permute-start.9) | collective-permute-done | bytes 1048608 | tf_op jit(solution)/shard_map/ppermute | solution.py:290
  76.9 2.5 %collective-permute-done.10.users_ref = f32[2,512,256]{2,1,0:T(8,128)S(1)} collective-permute-done((f32[2,512,256]{2,1,0:T(8,128)S(1)}, f32[2,512,256]{2,1,0:T(8,128)S(1)}, u32[]{:S(2)}, u32[]{:S(2)}) %collective-permute-start.10) | collective-permute-done | bytes 1048608 | tf_op jit(solution)/shard_map/ppermute | solution.py:290
  79.4 1.5 %last_out.1 = (f32[512,256]{1,0:T(8,128)}, f32[512,256]{1,0:T(8,128)}, f32[512,256]{1,0:T(8,128)}, f32[512,256]{1,0:T(8,128)}) custom-call(f32[2,256,512]{2,1,0:T(8,128)S(1)} %collective-permute-done.9.ads_ref, f32[2,512,256]{2,1,0:T(8,128)S(1)} %collective-permute-done.10.users_ref), custom_call_target="tpu_custom_call" | custom-call | flops 1 | bytes 1 | tf_op jit(solution)/shard_map/last_out/pallas_call | solution.py:252
Async XLA Ops:
  5.7 2.7 %collective-permute-start.1 = (f32[2,256,512]{2,1,0:T(8,128)S(1)}, f32[2,256,512]{2,1,0:T(8,128)S(1)}, u32[]{:S(2)}, u32[]{:S(2)}) collective-permute-start(f32[2,256,512]{2,1,0:T(8,128)S(1)} %get-tuple-element.50), channel_id=1, source_target_pairs={{0,16},{1,17},{2,18},{3,19},{4,20},{5,21},{6,22},{7,23},{8,24},{9,... | collective-permute-start | bytes 3145736 | tf_op jit(solution)/shard_map/ppermute | solution.py:290
  5.8 18.1 %collective-permute-start = (f32[2,256,512]{2,1,0:T(8,128)S(1)}, f32[2,256,512]{2,1,0:T(8,128)S(1)}, u32[]{:S(2)}, u32[]{:S(2)}) collective-permute-start(f32[2,256,512]{2,1,0:T(8,128)S(1)} %get-tuple-element.50), channel_id=1, source_target_pairs={{0,16},{1,17},{2,18},{3,19},{4,20},{5,21},{6,22},{7,23},{8,24},{9,... | collective-permute-start | bytes 3145736 | tf_op jit(solution)/shard_map/ppermute | solution.py:290
  11.6 24.1 %collective-permute-start.4 = (f32[2,256,512]{2,1,0:T(8,128)S(1)}, f32[2,256,512]{2,1,0:T(8,128)S(1)}, u32[]{:S(2)}, u32[]{:S(2)}) collective-permute-start(f32[2,256,512]{2,1,0:T(8,128)S(1)} %get-tuple-element.67), channel_id=1, source_target_pairs={{0,16},{1,17},{2,18},{3,19},{4,20},{5,21},{6,22},{7,23},{8,24},{9,... | collective-permute-start | bytes 3145736 | tf_op jit(solution)/shard_map/ppermute | solution.py:290
  14.0 21.7 %collective-permute-start.3 = (f32[2,512,256]{2,1,0:T(8,128)S(1)}, f32[2,512,256]{2,1,0:T(8,128)S(1)}, u32[]{:S(2)}, u32[]{:S(2)}) collective-permute-start(f32[2,512,256]{2,1,0:T(8,128)S(1)} %get-tuple-element.57.after_ref), channel_id=1, source_target_pairs={{0,0},{1,1},{2,2},{3,3},{4,4},{5,5},{6,6},{7,7},{8,8},{9,9},{10,10... | collective-permute-start | bytes 3145736 | tf_op jit(solution)/shard_map/ppermute | solution.py:290
  14.7 6.1 %collective-permute-start.2 = (s32[8,512]{1,0:T(8,128)S(1)}, s32[8,512]{1,0:T(8,128)S(1)}, u32[]{:S(2)}, u32[]{:S(2)}) collective-permute-start(s32[8,512]{1,0:T(8,128)S(1)} %get-tuple-element.58), channel_id=1, source_target_pairs={{0,192},{1,193},{2,194},{3,195},{4,196},{5,197},{6,198},{7,199},{8... | collective-permute-start | bytes 49160 | tf_op jit(solution)/shard_map/ppermute | solution.py:290
  26.8 3.5 %collective-permute-start.5 = (f32[256,512]{1,0:T(8,128)S(1)}, f32[256,512]{1,0:T(8,128)S(1)}, u32[]{:S(2)}, u32[]{:S(2)}) collective-permute-start(f32[256,512]{1,0:T(8,128)S(1)} %get-tuple-element.68), channel_id=1, source_target_pairs={{0,16},{1,17},{2,18},{3,19},{4,20},{5,21},{6,22},{7,23},{8,24},{9,... | collective-permute-start | bytes 1572872 | tf_op jit(solution)/shard_map/ppermute | solution.py:290
  26.9 3.5 %collective-permute-start.6 = (f32[256,512]{1,0:T(8,128)S(1)}, f32[256,512]{1,0:T(8,128)S(1)}, u32[]{:S(2)}, u32[]{:S(2)}) collective-permute-start(f32[256,512]{1,0:T(8,128)S(1)} %get-tuple-element.69), channel_id=1, source_target_pairs={{0,16},{1,17},{2,18},{3,19},{4,20},{5,21},{6,22},{7,23},{8,24},{9,... | collective-permute-start | bytes 1572872 | tf_op jit(solution)/shard_map/ppermute | solution.py:290
  39.0 16.7 %collective-permute-start.7 = (f32[2,512,256]{2,1,0:T(8,128)S(1)}, f32[2,512,256]{2,1,0:T(8,128)S(1)}, u32[]{:S(2)}, u32[]{:S(2)}) collective-permute-start(f32[2,512,256]{2,1,0:T(8,128)S(1)} %get-tuple-element.73), channel_id=1, source_target_pairs={{0,192},{1,193},{2,194},{3,195},{4,196},{5,197},{6,198},{7,199},{8... | collective-permute-start | bytes 3145736 | tf_op jit(solution)/shard_map/ppermute | solution.py:290
  42.5 15.7 %collective-permute-start.8 = (f32[2,256,512]{2,1,0:T(8,128)S(1)}, f32[2,256,512]{2,1,0:T(8,128)S(1)}, u32[]{:S(2)}, u32[]{:S(2)}) collective-permute-start(f32[2,256,512]{2,1,0:T(8,128)S(1)} %get-tuple-element.74), channel_id=1, source_target_pairs={{0,16},{1,17},{2,18},{3,19},{4,20},{5,21},{6,22},{7,23},{8,24},{9,... | collective-permute-start | bytes 3145736 | tf_op jit(solution)/shard_map/ppermute | solution.py:290
  61.4 15.5 %collective-permute-start.9 = (f32[2,256,512]{2,1,0:T(8,128)S(1)}, f32[2,256,512]{2,1,0:T(8,128)S(1)}, u32[]{:S(2)}, u32[]{:S(2)}) collective-permute-start(f32[2,256,512]{2,1,0:T(8,128)S(1)} %get-tuple-element.78), channel_id=1, source_target_pairs={{0,24},{1,25},{2,26},{3,27},{4,28},{5,29},{6,30},{7,31},{8,16},{9,... | collective-permute-start | bytes 3145736 | tf_op jit(solution)/shard_map/ppermute | solution.py:290
  61.5 17.9 %collective-permute-start.10 = (f32[2,512,256]{2,1,0:T(8,128)S(1)}, f32[2,512,256]{2,1,0:T(8,128)S(1)}, u32[]{:S(2)}, u32[]{:S(2)}) collective-permute-start(f32[2,512,256]{2,1,0:T(8,128)S(1)} %get-tuple-element.79), channel_id=1, source_target_pairs={{0,64},{1,65},{2,66},{3,67},{4,68},{5,69},{6,70},{7,71},{8,72},{9,... | collective-permute-start | bytes 3145736 | tf_op jit(solution)/shard_map/ppermute | solution.py:290

commit v7 on v6

--- a/solution.py
+++ b/solution.py
@@ -131,11 +131,11 @@
         prepare(g, pu[rnd : rnd + 1, cols], pa[rnd : rnd + 1, cols], ng[rnd, g : g + 1, :], users, ads, *prep)
 
 
-def second_group(u_ref, at1, amt1, ato_ref, amto_ref, prep, gh_ref, gl_ref, ah_ref, al_ref):
+def second_group(u_ref, at1, amt1, prep, gh_ref, gl_ref, ah_ref, al_ref):
     at_hl = split(at1)
     ah_ref[...], al_ref[...] = at_hl
     ga = group_pass(1, reader(u_ref), u_ref.shape[0], at_hl, prep, None, (gh_ref, gl_ref))
-    ato_ref[...], amto_ref[...] = adagrad(at1, amt1, ga)
+    return adagrad(at1, amt1, ga)
 
 
 def first_round_kernel(
@@ -163,7 +163,7 @@
     put = update_users(reader(u_ref), reader(um_ref), uo_ref, umo_ref)
     ga = group_pass(0, reader(u_ref), u_ref.shape[0], split(at), prep, put)
     at1, amt1 = adagrad(at, amt, ga)
-    second_group(uo_ref, at1, amt1, ads_ref.at[0], ads_ref.at[1], prep, gh_ref, gl_ref, ah_ref, al_ref)
+    ads_ref[0], ads_ref[1] = second_group(uo_ref, at1, amt1, prep, gh_ref, gl_ref, ah_ref, al_ref)
 
 
 def meeting(u_read, um_read, at, amt, prep, u1_ref, um1_ref, uo_ref, umo_ref):
@@ -192,28 +192,37 @@
     put = update_users(u_read, reader(um_ref), u1_ref, um1_ref)
     ga = group_pass(0, u_read, u_ref.shape[0], split(at), prep, put)
     at1, amt1 = adagrad(at, far_ref[1], ga)
-    second_group(u1_ref, at1, amt1, ato_ref, amto_ref, prep, gh_ref, gl_ref, ah_ref, al_ref)
+    ato_ref[...], amto_ref[...] = second_group(u1_ref, at1, amt1, prep, gh_ref, gl_ref, ah_ref, al_ref)
 
 
 def pick_kernel(
     ue_ref, ume_ref, users_ref, ads_ref, ato_ref, amto_ref, mh, cu, cn,
-    ads_out_ref, users_out_ref, u1_ref, um1_ref,
+    un_ref, umn_ref, atn_ref, amtn_ref, u1_ref, um1_ref,
 ):
     odd = on_odd_core()
     at = jnp.where(odd, ato_ref[...], ads_ref[0])
     amt = jnp.where(odd, amto_ref[...], ads_ref[1])
     u_read, um_read = picker(odd, ue_ref, users_ref.at[0]), picker(odd, ume_ref, users_ref.at[1])
-    ads_out_ref[0], ads_out_ref[1] = meeting(
-        u_read, um_read, at, amt, (mh, cu, cn), u1_ref, um1_ref, users_out_ref.at[0], users_out_ref.at[1]
-    )
-
-
-def whole_kernel(users_ref, ads_ref, mh, cu, cn, ads_out_ref, users_out_ref, u1_ref, um1_ref):
-    u_read, um_read = reader(users_ref.at[0]), reader(users_ref.at[1])
-    ads_out_ref[0], ads_out_ref[1] = meeting(
-        u_read, um_read, ads_ref[0], ads_ref[1], (mh, cu, cn), u1_ref, um1_ref,
-        users_out_ref.at[0], users_out_ref.at[1],
-    )
+    atn_ref[...], amtn_ref[...] = meeting(
+        u_read, um_read, at, amt, (mh, cu, cn), u1_ref, um1_ref, un_ref, umn_ref
+    )
+
+
+def gradient_kernel(u_ref, at_ref, mh, cu, cn, gu_ref, ga_ref):
+    def put(rows, grad):
+        gu_ref[rows, :] = grad
+
+    ga_ref[...] = group_pass(0, reader(u_ref), u_ref.shape[0], split(at_ref[...]), (mh, cu, cn), put)
+
+
+def last_end_kernel(
+    u_ref, um_ref, at_ref, amt_ref, gu_ref, ga_ref, mh, cu, cn, ads_ref, users_ref, u1_ref, um1_ref,
+):
+    u1_ref[...], um1_ref[...] = adagrad(u_ref[...], um_ref[...], gu_ref[...])
+    at1, amt1 = adagrad(at_ref[...], amt_ref[...], ga_ref[...])
+    put = update_users(reader(u1_ref), reader(um1_ref), users_ref.at[0], users_ref.at[1])
+    ga = group_pass(1, reader(u1_ref), u1_ref.shape[0], split(at1), (mh, cu, cn), put)
+    ads_ref[0], ads_ref[1] = adagrad(at1, amt1, ga)
 
 
 def users_kernel(u_ref, um_ref, gh_ref, gl_ref, ah_ref, al_ref, uo_ref, umo_ref):
@@ -261,7 +270,7 @@
     )(*ins[:split_at], *far)
 
 
-def last_kernel(ads_ref, users_ref, u_hbm, um_hbm, a_hbm, am_hbm, turned, sems, user_sems):
+def last_kernel(users_ref, ads_ref, u_hbm, um_hbm, a_hbm, am_hbm, turned, sems, user_sems):
     copies = [
         pltpu.make_async_copy(users_ref.at[0], u_hbm, user_sems.at[0]),
         pltpu.make_async_copy(users_ref.at[1], um_hbm, user_sems.at[1]),
@@ -350,18 +359,20 @@
     )
     prep, prep_last = preps[: len(prep_shapes)], preps[len(prep_shapes) :]
 
+    u, um, at, amt = call(
+        pick_kernel, (u, um, users_early, ads_early, *ads_late, *prep), [table_u, table_u, table_a, table_a],
+        users_scratch, name="round_pick",
+    )
+    u, um = move((u, um), (-4, False), away, stay, away)
+    at, amt = move((at, amt), (1, False), (1, True), (1, False), (-3, True))
+    gu, ga = call(gradient_kernel, (u, at, *prep_last), [table_u, table_a], name="round_last_gradients")
     ads_now, users_now = call(
-        pick_kernel, (u, um, users_early, ads_early, *ads_late, *prep), [both_a, both_u], users_scratch, name="round_pick",
-    )
-    (users_now,) = move((users_now,), (-4, False), away, stay, away)
-    (ads_now,) = move((ads_now,), (1, False), (1, True), (1, False), (-3, True))
-    ads_now, users_now = call(
-        whole_kernel, (users_now, ads_now, *prep_last), [both_a, both_u], users_scratch, name="round_last",
+        last_end_kernel, (u, um, at, amt, gu, ga, *prep_last), [both_a, both_u], users_scratch, name="round_last_end",
     )
     (users_now,) = move((users_now,), (4, False), stay, stay, stay)
     (ads_now,) = move((ads_now,), (1, True), (-3, True), (-3, True), (-3, True))
     return call(
-        last_kernel, (ads_now, users_now), [pltpu.HBM((nu, d), F32)] * 2 + [pltpu.HBM((na, d), F32)] * 2,
+        last_kernel, (users_now, ads_now), [pltpu.HBM((nu, d), F32)] * 2 + [pltpu.HBM((na, d), F32)] * 2,
         [pltpu.VMEM((2, na, d), F32), pltpu.SemaphoreType.DMA((2 * PARTS_OUT,)), pltpu.SemaphoreType.DMA((2,))],
         name="last_out", out_place=pltpu.HBM,
     )

time: 81.4 us -> 79.9 us (0.982)
  waiting for transfers between devices: 41.2 us -> 36.5 us
  starting transfers between devices: 15.3 us -> 18.1 us
    ppermute x11 -> x13, waiting for transfers between devices: 41.2 us -> 36.5 us  [move(): return tuple((lax.ppermute(x, AXES, route) for x in arrays))]
    ppermute x11 -> x13, starting transfers between devices: 15.3 us -> 18.1 us  [move(): return tuple((lax.ppermute(x, AXES, route) for x in arrays))]
    pallas_call x10 -> x11, Pallas kernels: 23.6 us -> 23.9 us  [call(): pl.pallas_call(kernel, out_shape=outs, in_specs=[vmem] * split_at + [pl.B...]
  transfers between devices with their start and end apart: 11 -> 13, of which waited for: 8 -> 9; matrix products, arithmetic and copies ran while one was open for 0% -> 0% of each run, Pallas kernels for 13% -> 15%
where the time goes in v7:
time: 79.9 us; the launch traced here: 79.5 us
  waiting for transfers between devices  36.5 us (46%)
  Pallas kernels  23.9 us (30%)
  starting transfers between devices  18.1 us (23%)
  between operations  0.98 us (1%)
    ppermute x13, waiting for transfers between devices, move(): return tuple((lax.ppermute(x, AXES, route) for x in arrays))  36.5 us
    pallas_call x11, Pallas kernels, call(): pl.pallas_call(kernel, out_shape=outs, in_specs=[vmem] * split_at + [pl.B...  23.9 us
    ppermute x13, starting transfers between devices, move(): return tuple((lax.ppermute(x, AXES, route) for x in arrays))  18.1 us
  transfers between devices with their start and end apart: 13, of which 9 were waited for; matrix products, arithmetic and copies ran while one was open for 0% of the time, Pallas kernels for 15%

profile of v7, /device:TPU:192, one launch (start us, length us, event | category | flops | bytes accessed | tf_op | source)
XLA Modules:
  0.0 79.5 jit_solution(1873310276698091028)
XLA Ops:
  0.6 5.1 %round_first.1 = (f32[512,256]{1,0:T(8,128)S(1)}, f32[512,256]{1,0:T(8,128)S(1)}, f32[2,256,512]{2,1,0:T(8,128)S(1)}, bf16[512,512]{1,0:T(8,128)(2,1)S(1)}, bf16...) custom-call(s32[1,16,4,512]{3,2,1,0:T(4,128)} %pu_hbm.3, ...), custom_call_target="tpu_custom_call" | custom-call | flops 1 | bytes 1 | tf_op jit(solution)/shard_map/round_first/pallas_call | solution.py:261
  5.7 0.1 collective-permute-start.1
  5.8 0.5 collective-permute-start
  6.3 0.8 users_update.2
  7.1 0.7 counts_1.1
  7.8 0.6 collective-permute-done.1.near_ref
  8.4 3.2 %round_early.1 = (f32[2,256,512]{2,1,0:T(8,128)S(1)}, f32[2,512,256]{2,1,0:T(8,128)S(1)}) custom-call(f32[512,256]{1,0:T(8,128)S(1)} %get-tuple-element.52.u_ref, f32[512,256]{1,0:T(8,128)S(1)} %get-tuple-element.53.after_ref.um_ref, f32[2,256,512]{2,1,0:T(8,128)S(1)} %collective-permute-done.1.near_ref, bf16[2,512,512]{2,1,0:T(8,128)(2,1)S(1)} %get-tuple-element.58.mh, ...), custom_call_target="tpu_custom_call" | custom-call | flops 1 | bytes 1 | tf_op jit(solution)/shard_map/round_early/pallas_call | solution.py:261
  11.6 2.3 %collective-permute-start.4 = (f32[2,256,512]{2,1,0:T(8,128)S(1)}, f32[2,256,512]{2,1,0:T(8,128)S(1)}, u32[]{:S(2)}, u32[]{:S(2)}) collective-permute-start(f32[2,256,512]{2,1,0:T(8,128)S(1)} %get-tuple-element.71), channel_id=1, source_target_pairs={{0,16},{1,17},{2,18},{3,19},{4,20},{5,21},{6,22},{7,23},{8,24},{9,... | collective-permute-start | bytes 3145736 | tf_op jit(solution)/shard_map/ppermute | solution.py:299
  14.0 0.7 collective-permute-start.3
  14.7 4.8 %collective-permute-start.2 = (s32[8,512]{1,0:T(8,128)S(1)}, s32[8,512]{1,0:T(8,128)S(1)}, u32[]{:S(2)}, u32[]{:S(2)}) collective-permute-start(s32[8,512]{1,0:T(8,128)S(1)} %get-tuple-element.62), channel_id=1, source_target_pairs={{0,192},{1,193},{2,194},{3,195},{4,196},{5,197},{6,198},{7,199},{8... | collective-permute-start | bytes 49160 | tf_op jit(solution)/shard_map/ppermute | solution.py:299
  19.6 1.2 %collective-permute-done.2.lists_ref = s32[8,512]{1,0:T(8,128)S(1)} collective-permute-done((s32[8,512]{1,0:T(8,128)S(1)}, s32[8,512]{1,0:T(8,128)S(1)}, u32[]{:S(2)}, u32[]{:S(2)}) %collective-permute-start.2) | collective-permute-done | bytes 16416 | tf_op jit(solution)/shard_map/ppermute | solution.py:299
  20.8 3.1 %collective-permute-done.far_ref = f32[2,256,512]{2,1,0:T(8,128)S(1)} collective-permute-done((f32[2,256,512]{2,1,0:T(8,128)S(1)}, f32[2,256,512]{2,1,0:T(8,128)S(1)}, u32[]{:S(2)}, u32[]{:S(2)}) %collective-permute-start) | collective-permute-done | bytes 1048608 | tf_op jit(solution)/shard_map/ppermute | solution.py:299
  23.9 3.0 %round_late.1 = (f32[512,256]{1,0:T(8,128)S(1)}, f32[512,256]{1,0:T(8,128)S(1)}, f32[256,512]{1,0:T(8,128)S(1)}, f32[256,512]{1,0:T(8,128)S(1)}, bf16[512,512]{1...) custom-call(f32[512,256]{1,0:T(8,128)S(1)} %get-tuple-element.52.u_re, ...), custom_call_target="tpu_custom_call" | custom-call | flops 1 | bytes 1 | tf_op jit(solution)/shard_map/round_late/pallas_call | solution.py:261
  26.8 0.1 collective-permute-start.5
  26.9 0.5 collective-permute-start.6
  27.4 0.8 users_update.3
  28.2 2.1 %counts_23.1 = (bf16[2,512,512]{2,1,0:T(8,128)(2,1)S(1)}, f32[2,512,128]{2,1,0:T(8,128)S(1)}, f32[2,8,512]{2,1,0:T(8,128)S(1)}, bf16[2,512,512]{2,1,0:T(8,128)(2...) custom-call(f32[512,256]{1,0:T(8,128)S(1)} %get-tuple-element.70.after_ref.ume_ref, ...), custom_call_target="tpu_custom_call" | custom-call | flops 1 | bytes 1 | tf_op jit(solution)/shard_map/counts_23/pallas_call | solution.py:261
  30.4 0.0 collective-permute-done.5.ato_ref
  30.4 0.0 collective-permute-done.6.amto_ref
  30.4 5.3 %collective-permute-done.4.ads_ref = f32[2,256,512]{2,1,0:T(8,128)S(1)} collective-permute-done((f32[2,256,512]{2,1,0:T(8,128)S(1)}, f32[2,256,512]{2,1,0:T(8,128)S(1)}, u32[]{:S(2)}, u32[]{:S(2)}) %collective-permute-start.4) | collective-permute-done | bytes 1048608 | tf_op jit(solution)/shard_map/ppermute | solution.py:299
  35.7 0.0 collective-permute-done.3.users_ref
  35.7 3.3 %round_pick.1 = (f32[512,256]{1,0:T(8,128)S(1)}, f32[512,256]{1,0:T(8,128)S(1)}, f32[256,512]{1,0:T(8,128)S(1)}, f32[256,512]{1,0:T(8,128)S(1)}) custom-call(f32[512,256]{1,0:T(8,128)S(1)} %get-tuple-element.69.ue_ref, f32[512,256]{1,0:T(8,128)S(1)} %get-tuple-element.70.after_ref.ume_ref, f32[2,512,256]{2,1,0:T(8,128)S(1)} %collective-permute-done.3.users_ref, ...), custom_call_target="tpu_custom_call" | custom-call | flops 1 | bytes 1 | tf_op jit(solution)/shard_map/round_pick/pallas_call | solution.py:261
  39.0 3.5 %collective-permute-start.7 = (f32[512,256]{1,0:T(8,128)S(1)}, f32[512,256]{1,0:T(8,128)S(1)}, u32[]{:S(2)}, u32[]{:S(2)}) collective-permute-start(f32[512,256]{1,0:T(8,128)S(1)} %get-tuple-element.77), channel_id=1, source_target_pairs={{0,192},{1,193},{2,194},{3,195},{4,196},{5,197},{6,198},{7,199},{8... | collective-permute-start | bytes 1572872 | tf_op jit(solution)/shard_map/ppermute | solution.py:299
  42.5 0.1 collective-permute-start.9
  42.6 2.7 %collective-permute-start.8 = (f32[512,256]{1,0:T(8,128)S(1)}, f32[512,256]{1,0:T(8,128)S(1)}, u32[]{:S(2)}, u32[]{:S(2)}) collective-permute-start(f32[512,256]{1,0:T(8,128)S(1)} %get-tuple-element.78), channel_id=1, source_target_pairs={{0,192},{1,193},{2,194},{3,195},{4,196},{5,197},{6,198},{7,199},{8... | collective-permute-start | bytes 1572872 | tf_op jit(solution)/shard_map/ppermute | solution.py:299
  45.3 0.3 collective-permute-start.10
  45.6 4.4 %collective-permute-done.7.u_ref = f32[512,256]{1,0:T(8,128)S(1)} collective-permute-done((f32[512,256]{1,0:T(8,128)S(1)}, f32[512,256]{1,0:T(8,128)S(1)}, u32[]{:S(2)}, u32[]{:S(2)}) %collective-permute-start.7) | collective-permute-done | bytes 524320 | tf_op jit(solution)/shard_map/ppermute | solution.py:299
  50.1 2.3 %collective-permute-done.9.at_ref = f32[256,512]{1,0:T(8,128)S(1)} collective-permute-done((f32[256,512]{1,0:T(8,128)S(1)}, f32[256,512]{1,0:T(8,128)S(1)}, u32[]{:S(2)}, u32[]{:S(2)}) %collective-permute-start.9) | collective-permute-done | bytes 524320 | tf_op jit(solution)/shard_map/ppermute | solution.py:299
  52.4 1.5 %round_last_gradients.1 = (f32[512,256]{1,0:T(8,128)S(1)}, f32[256,512]{1,0:T(8,128)S(1)}) custom-call(f32[512,256]{1,0:T(8,128)S(1)} %collective-permute-done.7.u_ref, f32[256,512]{1,0:T(8,128)S(1)} %collective-permute-done.9.at_ref, bf16[2,512,512]{2,1,0:T(8,128)(2,1)S(1)} %get-tuple-element.81.mh, f32[2,512,128]{2,1,0:T(8,128)S(1)} %get-tuple-element.82.cu, ...), custom_call_target="tpu_custom_call" | custom-call | flops 1 | bytes 1 | tf_op jit(solution)/shard_map/round_last_gradients/pallas_call | solution.py:261
  53.9 1.8 %collective-permute-done.8.um_ref = f32[512,256]{1,0:T(8,128)S(1)} collective-permute-done((f32[512,256]{1,0:T(8,128)S(1)}, f32[512,256]{1,0:T(8,128)S(1)}, u32[]{:S(2)}, u32[]{:S(2)}) %collective-permute-start.8) | collective-permute-done | bytes 524320 | tf_op jit(solution)/shard_map/ppermute | solution.py:299
  55.7 2.3 %collective-permute-done.10.amt_ref = f32[256,512]{1,0:T(8,128)S(1)} collective-permute-done((f32[256,512]{1,0:T(8,128)S(1)}, f32[256,512]{1,0:T(8,128)S(1)}, u32[]{:S(2)}, u32[]{:S(2)}) %collective-permute-start.10) | collective-permute-done | bytes 524320 | tf_op jit(solution)/shard_map/ppermute | solution.py:299
  58.0 2.0 %round_last_end.1 = (f32[2,256,512]{2,1,0:T(8,128)S(1)}, f32[2,512,256]{2,1,0:T(8,128)S(1)}) custom-call(f32[512,256]{1,0:T(8,128)S(1)} %collective-permute-done.7.u_ref, f32[512,256]{1,0:T(8,128)S(1)} %collective-permute-done.8.um_ref, f32[256,512]{1,0:T(8,128)S(1)} %collective-permute-done.9.at_ref, f32[256,512]{1,0:T(8,128)S(1)} %collective-permute-done.10.amt_ref, ...), custom_call_target="tpu_custom_call" | custom-call | flops 1 | bytes 1 | tf_op jit(solution)/shard_map/round_last_end/pallas_call | solution.py:261
  60.0 2.4 %collective-permute-start.11 = (f32[2,512,256]{2,1,0:T(8,128)S(1)}, f32[2,512,256]{2,1,0:T(8,128)S(1)}, u32[]{:S(2)}, u32[]{:S(2)}) collective-permute-start(f32[2,512,256]{2,1,0:T(8,128)S(1)} %get-tuple-element.86), channel_id=1, source_target_pairs={{0,64},{1,65},{2,66},{3,67},{4,68},{5,69},{6,70},{7,71},{8,72},{9,... | collective-permute-start | bytes 3145736 | tf_op jit(solution)/shard_map/ppermute | solution.py:299
  62.3 0.1 collective-permute-start.12
  62.4 15.4 %collective-permute-done.11.users_ref = f32[2,512,256]{2,1,0:T(8,128)S(1)} collective-permute-done((f32[2,512,256]{2,1,0:T(8,128)S(1)}, f32[2,512,256]{2,1,0:T(8,128)S(1)}, u32[]{:S(2)}, u32[]{:S(2)}) %collective-permute-start.11) | collective-permute-done | bytes 1048608 | tf_op jit(solution)/shard_map/ppermute | solution.py:299
  77.9 0.0 collective-permute-done.12.ads_ref
  77.9 1.5 %last_out.1 = (f32[512,256]{1,0:T(8,128)}, f32[512,256]{1,0:T(8,128)}, f32[512,256]{1,0:T(8,128)}, f32[512,256]{1,0:T(8,128)}) custom-call(f32[2,512,256]{2,1,0:T(8,128)S(1)} %collective-permute-done.11.users_ref, f32[2,256,512]{2,1,0:T(8,128)S(1)} %collective-permute-done.12.ads_ref), custom_call_target="tpu_custom_call" | custom-call | flops 1 | bytes 1 | tf_op jit(solution)/shard_map/last_out/pallas_call | solution.py:261
Async XLA Ops:
  5.7 2.7 %collective-permute-start.1 = (f32[2,256,512]{2,1,0:T(8,128)S(1)}, f32[2,256,512]{2,1,0:T(8,128)S(1)}, u32[]{:S(2)}, u32[]{:S(2)}) collective-permute-start(f32[2,256,512]{2,1,0:T(8,128)S(1)} %get-tuple-element.54), channel_id=1, source_target_pairs={{0,16},{1,17},{2,18},{3,19},{4,20},{5,21},{6,22},{7,23},{8,24},{9,... | collective-permute-start | bytes 3145736 | tf_op jit(solution)/shard_map/ppermute | solution.py:299
  5.8 18.1 %collective-permute-start = (f32[2,256,512]{2,1,0:T(8,128)S(1)}, f32[2,256,512]{2,1,0:T(8,128)S(1)}, u32[]{:S(2)}, u32[]{:S(2)}) collective-permute-start(f32[2,256,512]{2,1,0:T(8,128)S(1)} %get-tuple-element.54), channel_id=1, source_target_pairs={{0,16},{1,17},{2,18},{3,19},{4,20},{5,21},{6,22},{7,23},{8,24},{9,... | collective-permute-start | bytes 3145736 | tf_op jit(solution)/shard_map/ppermute | solution.py:299
  11.6 24.1 %collective-permute-start.4 = (f32[2,256,512]{2,1,0:T(8,128)S(1)}, f32[2,256,512]{2,1,0:T(8,128)S(1)}, u32[]{:S(2)}, u32[]{:S(2)}) collective-permute-start(f32[2,256,512]{2,1,0:T(8,128)S(1)} %get-tuple-element.71), channel_id=1, source_target_pairs={{0,16},{1,17},{2,18},{3,19},{4,20},{5,21},{6,22},{7,23},{8,24},{9,... | collective-permute-start | bytes 3145736 | tf_op jit(solution)/shard_map/ppermute | solution.py:299
  14.0 21.7 %collective-permute-start.3 = (f32[2,512,256]{2,1,0:T(8,128)S(1)}, f32[2,512,256]{2,1,0:T(8,128)S(1)}, u32[]{:S(2)}, u32[]{:S(2)}) collective-permute-start(f32[2,512,256]{2,1,0:T(8,128)S(1)} %get-tuple-element.61.after_ref), channel_id=1, source_target_pairs={{0,0},{1,1},{2,2},{3,3},{4,4},{5,5},{6,6},{7,7},{8,8},{9,9},{10,10... | collective-permute-start | bytes 3145736 | tf_op jit(solution)/shard_map/ppermute | solution.py:299
  14.7 6.1 %collective-permute-start.2 = (s32[8,512]{1,0:T(8,128)S(1)}, s32[8,512]{1,0:T(8,128)S(1)}, u32[]{:S(2)}, u32[]{:S(2)}) collective-permute-start(s32[8,512]{1,0:T(8,128)S(1)} %get-tuple-element.62), channel_id=1, source_target_pairs={{0,192},{1,193},{2,194},{3,195},{4,196},{5,197},{6,198},{7,199},{8... | collective-permute-start | bytes 49160 | tf_op jit(solution)/shard_map/ppermute | solution.py:299
  26.8 3.5 %collective-permute-start.5 = (f32[256,512]{1,0:T(8,128)S(1)}, f32[256,512]{1,0:T(8,128)S(1)}, u32[]{:S(2)}, u32[]{:S(2)}) collective-permute-start(f32[256,512]{1,0:T(8,128)S(1)} %get-tuple-element.72), channel_id=1, source_target_pairs={{0,16},{1,17},{2,18},{3,19},{4,20},{5,21},{6,22},{7,23},{8,24},{9,... | collective-permute-start | bytes 1572872 | tf_op jit(solution)/shard_map/ppermute | solution.py:299
  26.9 3.5 %collective-permute-start.6 = (f32[256,512]{1,0:T(8,128)S(1)}, f32[256,512]{1,0:T(8,128)S(1)}, u32[]{:S(2)}, u32[]{:S(2)}) collective-permute-start(f32[256,512]{1,0:T(8,128)S(1)} %get-tuple-element.73), channel_id=1, source_target_pairs={{0,16},{1,17},{2,18},{3,19},{4,20},{5,21},{6,22},{7,23},{8,24},{9,... | collective-permute-start | bytes 1572872 | tf_op jit(solution)/shard_map/ppermute | solution.py:299
  39.0 11.1 %collective-permute-start.7 = (f32[512,256]{1,0:T(8,128)S(1)}, f32[512,256]{1,0:T(8,128)S(1)}, u32[]{:S(2)}, u32[]{:S(2)}) collective-permute-start(f32[512,256]{1,0:T(8,128)S(1)} %get-tuple-element.77), channel_id=1, source_target_pairs={{0,192},{1,193},{2,194},{3,195},{4,196},{5,197},{6,198},{7,199},{8... | collective-permute-start | bytes 1572872 | tf_op jit(solution)/shard_map/ppermute | solution.py:299
  42.5 9.9 %collective-permute-start.9 = (f32[256,512]{1,0:T(8,128)S(1)}, f32[256,512]{1,0:T(8,128)S(1)}, u32[]{:S(2)}, u32[]{:S(2)}) collective-permute-start(f32[256,512]{1,0:T(8,128)S(1)} %get-tuple-element.79), channel_id=1, source_target_pairs={{0,16},{1,17},{2,18},{3,19},{4,20},{5,21},{6,22},{7,23},{8,24},{9,... | collective-permute-start | bytes 1572872 | tf_op jit(solution)/shard_map/ppermute | solution.py:299
  42.6 13.1 %collective-permute-start.8 = (f32[512,256]{1,0:T(8,128)S(1)}, f32[512,256]{1,0:T(8,128)S(1)}, u32[]{:S(2)}, u32[]{:S(2)}) collective-permute-start(f32[512,256]{1,0:T(8,128)S(1)} %get-tuple-element.78), channel_id=1, source_target_pairs={{0,192},{1,193},{2,194},{3,195},{4,196},{5,197},{6,198},{7,199},{8... | collective-permute-start | bytes 1572872 | tf_op jit(solution)/shard_map/ppermute | solution.py:299
  45.3 12.7 %collective-permute-start.10 = (f32[256,512]{1,0:T(8,128)S(1)}, f32[256,512]{1,0:T(8,128)S(1)}, u32[]{:S(2)}, u32[]{:S(2)}) collective-permute-start(f32[256,512]{1,0:T(8,128)S(1)} %get-tuple-element.80), channel_id=1, source_target_pairs={{0,16},{1,17},{2,18},{3,19},{4,20},{5,21},{6,22},{7,23},{8,24},{9,... | collective-permute-start | bytes 1572872 | tf_op jit(solution)/shard_map/ppermute | solution.py:299
  60.0 17.9 %collective-permute-start.11 = (f32[2,512,256]{2,1,0:T(8,128)S(1)}, f32[2,512,256]{2,1,0:T(8,128)S(1)}, u32[]{:S(2)}, u32[]{:S(2)}) collective-permute-start(f32[2,512,256]{2,1,0:T(8,128)S(1)} %get-tuple-element.86), channel_id=1, source_target_pairs={{0,64},{1,65},{2,66},{3,67},{4,68},{5,69},{6,70},{7,71},{8,72},{9,... | collective-permute-start | bytes 3145736 | tf_op jit(solution)/shard_map/ppermute | solution.py:299
  62.3 15.5 %collective-permute-start.12 = (f32[2,256,512]{2,1,0:T(8,128)S(1)}, f32[2,256,512]{2,1,0:T(8,128)S(1)}, u32[]{:S(2)}, u32[]{:S(2)}) collective-permute-start(f32[2,256,512]{2,1,0:T(8,128)S(1)} %get-tuple-element.87), channel_id=1, source_target_pairs={{0,24},{1,25},{2,26},{3,27},{4,28},{5,29},{6,30},{7,31},{8,16},{9,... | collective-permute-start | bytes 3145736 | tf_op jit(solution)/shard_map/ppermute | solution.py:299

commit v8 on v7

--- a/solution.py
+++ b/solution.py
@@ -270,14 +270,22 @@
     )(*ins[:split_at], *far)
 
 
-def last_kernel(users_ref, ads_ref, u_hbm, um_hbm, a_hbm, am_hbm, turned, sems, user_sems):
-    copies = [
-        pltpu.make_async_copy(users_ref.at[0], u_hbm, user_sems.at[0]),
-        pltpu.make_async_copy(users_ref.at[1], um_hbm, user_sems.at[1]),
-    ]
+def users_out_kernel(users_ref, after_hbm, u_hbm, um_hbm, sems):
+    size = users_ref.shape[1] // PARTS_OUT
+    copies = []
+    for t, out_hbm in enumerate((u_hbm, um_hbm)):
+        for k in range(PARTS_OUT):
+            rows = pl.ds(k * size, size)
+            copies.append(pltpu.make_async_copy(users_ref.at[t, rows, :], out_hbm.at[rows, :], sems.at[t * PARTS_OUT + k]))
     for c in copies:
         c.start()
+    for c in copies:
+        c.wait()
+
+
+def ads_out_kernel(ads_ref, a_hbm, am_hbm, turned, sems):
     size = turned.shape[1] // PARTS_OUT
+    copies = []
     for t, out_hbm in enumerate((a_hbm, am_hbm)):
         for k in range(PARTS_OUT):
             rows = pl.ds(k * size, size)
@@ -369,13 +377,17 @@
     ads_now, users_now = call(
         last_end_kernel, (u, um, at, amt, gu, ga, *prep_last), [both_a, both_u], users_scratch, name="round_last_end",
     )
+    (ads_now,) = move((ads_now,), (1, True), (-3, True), (-3, True), (-3, True))
     (users_now,) = move((users_now,), (4, False), stay, stay, stay)
-    (ads_now,) = move((ads_now,), (1, True), (-3, True), (-3, True), (-3, True))
-    return call(
-        last_kernel, (users_now, ads_now), [pltpu.HBM((nu, d), F32)] * 2 + [pltpu.HBM((na, d), F32)] * 2,
-        [pltpu.VMEM((2, na, d), F32), pltpu.SemaphoreType.DMA((2 * PARTS_OUT,)), pltpu.SemaphoreType.DMA((2,))],
-        name="last_out", out_place=pltpu.HBM,
-    )
+    out_sems = pltpu.SemaphoreType.DMA((2 * PARTS_OUT,))
+    a, am = call(
+        ads_out_kernel, (ads_now,), [pltpu.HBM((na, d), F32)] * 2, [pltpu.VMEM((2, na, d), F32), out_sems],
+        name="ads_out", out_place=pltpu.HBM,
+    )
+    u, um = call(
+        users_out_kernel, (users_now, am), [pltpu.HBM((nu, d), F32)] * 2, [out_sems], hbm=1, name="users_out", out_place=pltpu.HBM,
+    )
+    return u, um, a, am
 
 
 def solution(mesh):

time: 79.9 us -> 79.5 us (level)
  waiting for transfers between devices: 36.5 us -> 35.5 us
    ppermute x13, waiting for transfers between devices: 36.5 us -> 35.5 us  [move(): return tuple((lax.ppermute(x, AXES, route) for x in arrays))]
    pallas_call x11 -> x12, Pallas kernels: 23.9 us -> 24.5 us  [call(): pl.pallas_call(kernel, out_shape=outs, in_specs=[vmem] * split_at + [pl.B...]
  transfers between devices with their start and end apart: 13 -> 13, of which waited for: 9 -> 10; matrix products, arithmetic and copies ran while one was open for 0% -> 0% of each run, Pallas kernels for 15% -> 17%
where the time goes in v8:
time: 79.5 us; the launch traced here: 79.2 us
  waiting for transfers between devices  35.5 us (45%)
  Pallas kernels  24.5 us (31%)
  starting transfers between devices  18.1 us (23%)
  between operations  0.99 us (1%)
    ppermute x13, waiting for transfers between devices, move(): return tuple((lax.ppermute(x, AXES, route) for x in arrays))  35.5 us
    pallas_call x12, Pallas kernels, call(): pl.pallas_call(kernel, out_shape=outs, in_specs=[vmem] * split_at + [pl.B...  24.5 us
    ppermute x13, starting transfers between devices, move(): return tuple((lax.ppermute(x, AXES, route) for x in arrays))  18.1 us
  transfers between devices with their start and end apart: 13, of which 10 were waited for; matrix products, arithmetic and copies ran while one was open for 0% of the time, Pallas kernels for 17%

profile of v8, /device:TPU:192, one launch (start us, length us, event | category | flops | bytes accessed | tf_op | source)
XLA Modules:
  0.0 79.2 jit_solution(4327290994394682336)
XLA Ops:
  0.6 5.1 %round_first.1 = (f32[512,256]{1,0:T(8,128)S(1)}, f32[512,256]{1,0:T(8,128)S(1)}, f32[2,256,512]{2,1,0:T(8,128)S(1)}, bf16[512,512]{1,0:T(8,128)(2,1)S(1)}, bf16...) custom-call(s32[1,16,4,512]{3,2,1,0:T(4,128)} %pu_hbm.3, ...), custom_call_target="tpu_custom_call" | custom-call | flops 1 | bytes 1 | tf_op jit(solution)/shard_map/round_first/pallas_call | solution.py:261
  5.7 0.1 collective-permute-start.1
  5.8 0.5 collective-permute-start
  6.3 0.8 users_update.2
  7.1 0.7 counts_1.1
  7.8 0.6 collective-permute-done.1.near_ref
  8.4 3.2 %round_early.1 = (f32[2,256,512]{2,1,0:T(8,128)S(1)}, f32[2,512,256]{2,1,0:T(8,128)S(1)}) custom-call(f32[512,256]{1,0:T(8,128)S(1)} %get-tuple-element.56.u_ref, f32[512,256]{1,0:T(8,128)S(1)} %get-tuple-element.57.after_ref.um_ref, f32[2,256,512]{2,1,0:T(8,128)S(1)} %collective-permute-done.1.near_ref, bf16[2,512,512]{2,1,0:T(8,128)(2,1)S(1)} %get-tuple-element.62.mh, ...), custom_call_target="tpu_custom_call" | custom-call | flops 1 | bytes 1 | tf_op jit(solution)/shard_map/round_early/pallas_call | solution.py:261
  11.6 2.3 %collective-permute-start.4 = (f32[2,256,512]{2,1,0:T(8,128)S(1)}, f32[2,256,512]{2,1,0:T(8,128)S(1)}, u32[]{:S(2)}, u32[]{:S(2)}) collective-permute-start(f32[2,256,512]{2,1,0:T(8,128)S(1)} %get-tuple-element.75), channel_id=1, source_target_pairs={{0,16},{1,17},{2,18},{3,19},{4,20},{5,21},{6,22},{7,23},{8,24},{9,... | collective-permute-start | bytes 3145736 | tf_op jit(solution)/shard_map/ppermute | solution.py:307
  14.0 0.7 collective-permute-start.3
  14.7 4.8 %collective-permute-start.2 = (s32[8,512]{1,0:T(8,128)S(1)}, s32[8,512]{1,0:T(8,128)S(1)}, u32[]{:S(2)}, u32[]{:S(2)}) collective-permute-start(s32[8,512]{1,0:T(8,128)S(1)} %get-tuple-element.66), channel_id=1, source_target_pairs={{0,192},{1,193},{2,194},{3,195},{4,196},{5,197},{6,198},{7,199},{8... | collective-permute-start | bytes 49160 | tf_op jit(solution)/shard_map/ppermute | solution.py:307
  19.6 1.2 %collective-permute-done.2.lists_ref = s32[8,512]{1,0:T(8,128)S(1)} collective-permute-done((s32[8,512]{1,0:T(8,128)S(1)}, s32[8,512]{1,0:T(8,128)S(1)}, u32[]{:S(2)}, u32[]{:S(2)}) %collective-permute-start.2) | collective-permute-done | bytes 16416 | tf_op jit(solution)/shard_map/ppermute | solution.py:307
  20.8 3.1 %collective-permute-done.far_ref = f32[2,256,512]{2,1,0:T(8,128)S(1)} collective-permute-done((f32[2,256,512]{2,1,0:T(8,128)S(1)}, f32[2,256,512]{2,1,0:T(8,128)S(1)}, u32[]{:S(2)}, u32[]{:S(2)}) %collective-permute-start) | collective-permute-done | bytes 1048608 | tf_op jit(solution)/shard_map/ppermute | solution.py:307
  23.9 3.0 %round_late.1 = (f32[512,256]{1,0:T(8,128)S(1)}, f32[512,256]{1,0:T(8,128)S(1)}, f32[256,512]{1,0:T(8,128)S(1)}, f32[256,512]{1,0:T(8,128)S(1)}, bf16[512,512]{1...) custom-call(f32[512,256]{1,0:T(8,128)S(1)} %get-tuple-element.56.u_re, ...), custom_call_target="tpu_custom_call" | custom-call | flops 1 | bytes 1 | tf_op jit(solution)/shard_map/round_late/pallas_call | solution.py:261
  26.8 0.1 collective-permute-start.5
  26.9 0.5 collective-permute-start.6
  27.4 0.8 users_update.3
  28.2 2.1 %counts_23.1 = (bf16[2,512,512]{2,1,0:T(8,128)(2,1)S(1)}, f32[2,512,128]{2,1,0:T(8,128)S(1)}, f32[2,8,512]{2,1,0:T(8,128)S(1)}, bf16[2,512,512]{2,1,0:T(8,128)(2...) custom-call(f32[512,256]{1,0:T(8,128)S(1)} %get-tuple-element.74.after_ref.ume_ref, ...), custom_call_target="tpu_custom_call" | custom-call | flops 1 | bytes 1 | tf_op jit(solution)/shard_map/counts_23/pallas_call | solution.py:261
  30.4 0.0 collective-permute-done.5.ato_ref
  30.4 0.0 collective-permute-done.6.amto_ref
  30.4 5.3 %collective-permute-done.4.ads_ref = f32[2,256,512]{2,1,0:T(8,128)S(1)} collective-permute-done((f32[2,256,512]{2,1,0:T(8,128)S(1)}, f32[2,256,512]{2,1,0:T(8,128)S(1)}, u32[]{:S(2)}, u32[]{:S(2)}) %collective-permute-start.4) | collective-permute-done | bytes 1048608 | tf_op jit(solution)/shard_map/ppermute | solution.py:307
  35.7 0.0 collective-permute-done.3.users_ref
  35.7 3.3 %round_pick.1 = (f32[512,256]{1,0:T(8,128)S(1)}, f32[512,256]{1,0:T(8,128)S(1)}, f32[256,512]{1,0:T(8,128)S(1)}, f32[256,512]{1,0:T(8,128)S(1)}) custom-call(f32[512,256]{1,0:T(8,128)S(1)} %get-tuple-element.73.ue_ref, f32[512,256]{1,0:T(8,128)S(1)} %get-tuple-element.74.after_ref.ume_ref, f32[2,512,256]{2,1,0:T(8,128)S(1)} %collective-permute-done.3.users_ref, ...), custom_call_target="tpu_custom_call" | custom-call | flops 1 | bytes 1 | tf_op jit(solution)/shard_map/round_pick/pallas_call | solution.py:261
  39.0 3.5 %collective-permute-start.7 = (f32[512,256]{1,0:T(8,128)S(1)}, f32[512,256]{1,0:T(8,128)S(1)}, u32[]{:S(2)}, u32[]{:S(2)}) collective-permute-start(f32[512,256]{1,0:T(8,128)S(1)} %get-tuple-element.81), channel_id=1, source_target_pairs={{0,192},{1,193},{2,194},{3,195},{4,196},{5,197},{6,198},{7,199},{8... | collective-permute-start | bytes 1572872 | tf_op jit(solution)/shard_map/ppermute | solution.py:307
  42.5 0.1 collective-permute-start.9
  42.6 2.7 %collective-permute-start.8 = (f32[512,256]{1,0:T(8,128)S(1)}, f32[512,256]{1,0:T(8,128)S(1)}, u32[]{:S(2)}, u32[]{:S(2)}) collective-permute-start(f32[512,256]{1,0:T(8,128)S(1)} %get-tuple-element.82), channel_id=1, source_target_pairs={{0,192},{1,193},{2,194},{3,195},{4,196},{5,197},{6,198},{7,199},{8... | collective-permute-start | bytes 1572872 | tf_op jit(solution)/shard_map/ppermute | solution.py:307
  45.3 0.3 collective-permute-start.10
  45.6 4.4 %collective-permute-done.7.u_ref = f32[512,256]{1,0:T(8,128)S(1)} collective-permute-done((f32[512,256]{1,0:T(8,128)S(1)}, f32[512,256]{1,0:T(8,128)S(1)}, u32[]{:S(2)}, u32[]{:S(2)}) %collective-permute-start.7) | collective-permute-done | bytes 524320 | tf_op jit(solution)/shard_map/ppermute | solution.py:307
  50.1 2.3 %collective-permute-done.9.at_ref = f32[256,512]{1,0:T(8,128)S(1)} collective-permute-done((f32[256,512]{1,0:T(8,128)S(1)}, f32[256,512]{1,0:T(8,128)S(1)}, u32[]{:S(2)}, u32[]{:S(2)}) %collective-permute-start.9) | collective-permute-done | bytes 524320 | tf_op jit(solution)/shard_map/ppermute | solution.py:307
  52.4 1.5 %round_last_gradients.1 = (f32[512,256]{1,0:T(8,128)S(1)}, f32[256,512]{1,0:T(8,128)S(1)}) custom-call(f32[512,256]{1,0:T(8,128)S(1)} %collective-permute-done.7.u_ref, f32[256,512]{1,0:T(8,128)S(1)} %collective-permute-done.9.at_ref, bf16[2,512,512]{2,1,0:T(8,128)(2,1)S(1)} %get-tuple-element.85.mh, f32[2,512,128]{2,1,0:T(8,128)S(1)} %get-tuple-element.86.cu, ...), custom_call_target="tpu_custom_call" | custom-call | flops 1 | bytes 1 | tf_op jit(solution)/shard_map/round_last_gradients/pallas_call | solution.py:261
  53.9 1.8 %collective-permute-done.8.um_ref = f32[512,256]{1,0:T(8,128)S(1)} collective-permute-done((f32[512,256]{1,0:T(8,128)S(1)}, f32[512,256]{1,0:T(8,128)S(1)}, u32[]{:S(2)}, u32[]{:S(2)}) %collective-permute-start.8) | collective-permute-done | bytes 524320 | tf_op jit(solution)/shard_map/ppermute | solution.py:307
  55.7 2.3 %collective-permute-done.10.amt_ref = f32[256,512]{1,0:T(8,128)S(1)} collective-permute-done((f32[256,512]{1,0:T(8,128)S(1)}, f32[256,512]{1,0:T(8,128)S(1)}, u32[]{:S(2)}, u32[]{:S(2)}) %collective-permute-start.10) | collective-permute-done | bytes 524320 | tf_op jit(solution)/shard_map/ppermute | solution.py:307
  58.0 2.0 %round_last_end.1 = (f32[2,256,512]{2,1,0:T(8,128)S(1)}, f32[2,512,256]{2,1,0:T(8,128)S(1)}) custom-call(f32[512,256]{1,0:T(8,128)S(1)} %collective-permute-done.7.u_ref, f32[512,256]{1,0:T(8,128)S(1)} %collective-permute-done.8.um_ref, f32[256,512]{1,0:T(8,128)S(1)} %collective-permute-done.9.at_ref, f32[256,512]{1,0:T(8,128)S(1)} %collective-permute-done.10.amt_ref, ...), custom_call_target="tpu_custom_call" | custom-call | flops 1 | bytes 1 | tf_op jit(solution)/shard_map/round_last_end/pallas_call | solution.py:261
  60.0 0.1 collective-permute-start.12
  60.1 2.4 %collective-permute-start.11 = (f32[2,512,256]{2,1,0:T(8,128)S(1)}, f32[2,512,256]{2,1,0:T(8,128)S(1)}, u32[]{:S(2)}, u32[]{:S(2)}) collective-permute-start(f32[2,512,256]{2,1,0:T(8,128)S(1)} %get-tuple-element.90), channel_id=1, source_target_pairs={{0,64},{1,65},{2,66},{3,67},{4,68},{5,69},{6,70},{7,71},{8,72},{9,... | collective-permute-start | bytes 3145736 | tf_op jit(solution)/shard_map/ppermute | solution.py:307
  62.4 13.0 %collective-permute-done.12.ads_ref = f32[2,256,512]{2,1,0:T(8,128)S(1)} collective-permute-done((f32[2,256,512]{2,1,0:T(8,128)S(1)}, f32[2,256,512]{2,1,0:T(8,128)S(1)}, u32[]{:S(2)}, u32[]{:S(2)}) %collective-permute-start.12) | collective-permute-done | bytes 1048608 | tf_op jit(solution)/shard_map/ppermute | solution.py:307
  75.5 1.1 %ads_out.1 = (f32[512,256]{1,0:T(8,128)}, f32[512,256]{1,0:T(8,128)}) custom-call(f32[2,256,512]{2,1,0:T(8,128)S(1)} %collective-permute-done.12.ads_ref), custom_call_target="tpu_custom_call" | custom-call | flops 1 | bytes 1 | tf_op jit(solution)/shard_map/ads_out/pallas_call | solution.py:261
  76.6 1.3 %collective-permute-done.11.users_ref = f32[2,512,256]{2,1,0:T(8,128)S(1)} collective-permute-done((f32[2,512,256]{2,1,0:T(8,128)S(1)}, f32[2,512,256]{2,1,0:T(8,128)S(1)}, u32[]{:S(2)}, u32[]{:S(2)}) %collective-permute-start.11) | collective-permute-done | bytes 1048608 | tf_op jit(solution)/shard_map/ppermute | solution.py:307
  78.0 1.0 %users_out.1 = (f32[512,256]{1,0:T(8,128)}, f32[512,256]{1,0:T(8,128)}) custom-call(f32[2,512,256]{2,1,0:T(8,128)S(1)} %collective-permute-done.11.users_ref, f32[512,256]{1,0:T(8,128)} %get-tuple-element.49.after_hbm), custom_call_target="tpu_custom_call" | custom-call | flops 1 | bytes 1 | tf_op jit(solution)/shard_map/users_out/pallas_call | solution.py:261
Async XLA Ops:
  5.7 2.7 %collective-permute-start.1 = (f32[2,256,512]{2,1,0:T(8,128)S(1)}, f32[2,256,512]{2,1,0:T(8,128)S(1)}, u32[]{:S(2)}, u32[]{:S(2)}) collective-permute-start(f32[2,256,512]{2,1,0:T(8,128)S(1)} %get-tuple-element.58), channel_id=1, source_target_pairs={{0,16},{1,17},{2,18},{3,19},{4,20},{5,21},{6,22},{7,23},{8,24},{9,... | collective-permute-start | bytes 3145736 | tf_op jit(solution)/shard_map/ppermute | solution.py:307
  5.8 18.1 %collective-permute-start = (f32[2,256,512]{2,1,0:T(8,128)S(1)}, f32[2,256,512]{2,1,0:T(8,128)S(1)}, u32[]{:S(2)}, u32[]{:S(2)}) collective-permute-start(f32[2,256,512]{2,1,0:T(8,128)S(1)} %get-tuple-element.58), channel_id=1, source_target_pairs={{0,16},{1,17},{2,18},{3,19},{4,20},{5,21},{6,22},{7,23},{8,24},{9,... | collective-permute-start | bytes 3145736 | tf_op jit(solution)/shard_map/ppermute | solution.py:307
  11.6 24.1 %collective-permute-start.4 = (f32[2,256,512]{2,1,0:T(8,128)S(1)}, f32[2,256,512]{2,1,0:T(8,128)S(1)}, u32[]{:S(2)}, u32[]{:S(2)}) collective-permute-start(f32[2,256,512]{2,1,0:T(8,128)S(1)} %get-tuple-element.75), channel_id=1, source_target_pairs={{0,16},{1,17},{2,18},{3,19},{4,20},{5,21},{6,22},{7,23},{8,24},{9,... | collective-permute-start | bytes 3145736 | tf_op jit(solution)/shard_map/ppermute | solution.py:307
  14.0 21.7 %collective-permute-start.3 = (f32[2,512,256]{2,1,0:T(8,128)S(1)}, f32[2,512,256]{2,1,0:T(8,128)S(1)}, u32[]{:S(2)}, u32[]{:S(2)}) collective-permute-start(f32[2,512,256]{2,1,0:T(8,128)S(1)} %get-tuple-element.65.after_ref), channel_id=1, source_target_pairs={{0,0},{1,1},{2,2},{3,3},{4,4},{5,5},{6,6},{7,7},{8,8},{9,9},{10,10... | collective-permute-start | bytes 3145736 | tf_op jit(solution)/shard_map/ppermute | solution.py:307
  14.7 6.1 %collective-permute-start.2 = (s32[8,512]{1,0:T(8,128)S(1)}, s32[8,512]{1,0:T(8,128)S(1)}, u32[]{:S(2)}, u32[]{:S(2)}) collective-permute-start(s32[8,512]{1,0:T(8,128)S(1)} %get-tuple-element.66), channel_id=1, source_target_pairs={{0,192},{1,193},{2,194},{3,195},{4,196},{5,197},{6,198},{7,199},{8... | collective-permute-start | bytes 49160 | tf_op jit(solution)/shard_map/ppermute | solution.py:307
  26.8 3.5 %collective-permute-start.5 = (f32[256,512]{1,0:T(8,128)S(1)}, f32[256,512]{1,0:T(8,128)S(1)}, u32[]{:S(2)}, u32[]{:S(2)}) collective-permute-start(f32[256,512]{1,0:T(8,128)S(1)} %get-tuple-element.76), channel_id=1, source_target_pairs={{0,16},{1,17},{2,18},{3,19},{4,20},{5,21},{6,22},{7,23},{8,24},{9,... | collective-permute-start | bytes 1572872 | tf_op jit(solution)/shard_map/ppermute | solution.py:307
  26.9 3.5 %collective-permute-start.6 = (f32[256,512]{1,0:T(8,128)S(1)}, f32[256,512]{1,0:T(8,128)S(1)}, u32[]{:S(2)}, u32[]{:S(2)}) collective-permute-start(f32[256,512]{1,0:T(8,128)S(1)} %get-tuple-element.77), channel_id=1, source_target_pairs={{0,16},{1,17},{2,18},{3,19},{4,20},{5,21},{6,22},{7,23},{8,24},{9,... | collective-permute-start | bytes 1572872 | tf_op jit(solution)/shard_map/ppermute | solution.py:307
  39.0 11.1 %collective-permute-start.7 = (f32[512,256]{1,0:T(8,128)S(1)}, f32[512,256]{1,0:T(8,128)S(1)}, u32[]{:S(2)}, u32[]{:S(2)}) collective-permute-start(f32[512,256]{1,0:T(8,128)S(1)} %get-tuple-element.81), channel_id=1, source_target_pairs={{0,192},{1,193},{2,194},{3,195},{4,196},{5,197},{6,198},{7,199},{8... | collective-permute-start | bytes 1572872 | tf_op jit(solution)/shard_map/ppermute | solution.py:307
  42.5 9.9 %collective-permute-start.9 = (f32[256,512]{1,0:T(8,128)S(1)}, f32[256,512]{1,0:T(8,128)S(1)}, u32[]{:S(2)}, u32[]{:S(2)}) collective-permute-start(f32[256,512]{1,0:T(8,128)S(1)} %get-tuple-element.83), channel_id=1, source_target_pairs={{0,16},{1,17},{2,18},{3,19},{4,20},{5,21},{6,22},{7,23},{8,24},{9,... | collective-permute-start | bytes 1572872 | tf_op jit(solution)/shard_map/ppermute | solution.py:307
  42.6 13.1 %collective-permute-start.8 = (f32[512,256]{1,0:T(8,128)S(1)}, f32[512,256]{1,0:T(8,128)S(1)}, u32[]{:S(2)}, u32[]{:S(2)}) collective-permute-start(f32[512,256]{1,0:T(8,128)S(1)} %get-tuple-element.82), channel_id=1, source_target_pairs={{0,192},{1,193},{2,194},{3,195},{4,196},{5,197},{6,198},{7,199},{8... | collective-permute-start | bytes 1572872 | tf_op jit(solution)/shard_map/ppermute | solution.py:307
  45.3 12.7 %collective-permute-start.10 = (f32[256,512]{1,0:T(8,128)S(1)}, f32[256,512]{1,0:T(8,128)S(1)}, u32[]{:S(2)}, u32[]{:S(2)}) collective-permute-start(f32[256,512]{1,0:T(8,128)S(1)} %get-tuple-element.84), channel_id=1, source_target_pairs={{0,16},{1,17},{2,18},{3,19},{4,20},{5,21},{6,22},{7,23},{8,24},{9,... | collective-permute-start | bytes 1572872 | tf_op jit(solution)/shard_map/ppermute | solution.py:307
  60.0 15.5 %collective-permute-start.12 = (f32[2,256,512]{2,1,0:T(8,128)S(1)}, f32[2,256,512]{2,1,0:T(8,128)S(1)}, u32[]{:S(2)}, u32[]{:S(2)}) collective-permute-start(f32[2,256,512]{2,1,0:T(8,128)S(1)} %get-tuple-element.91), channel_id=1, source_target_pairs={{0,24},{1,25},{2,26},{3,27},{4,28},{5,29},{6,30},{7,31},{8,16},{9,... | collective-permute-start | bytes 3145736 | tf_op jit(solution)/shard_map/ppermute | solution.py:307
  60.1 17.9 %collective-permute-start.11 = (f32[2,512,256]{2,1,0:T(8,128)S(1)}, f32[2,512,256]{2,1,0:T(8,128)S(1)}, u32[]{:S(2)}, u32[]{:S(2)}) collective-permute-start(f32[2,512,256]{2,1,0:T(8,128)S(1)} %get-tuple-element.90), channel_id=1, source_target_pairs={{0,64},{1,65},{2,66},{3,67},{4,68},{5,69},{6,70},{7,71},{8,72},{9,... | collective-permute-start | bytes 3145736 | tf_op jit(solution)/shard_map/ppermute | solution.py:307

commit v9 on v8

--- a/solution.py
+++ b/solution.py
@@ -216,7 +216,7 @@
 
 
 def last_end_kernel(
-    u_ref, um_ref, at_ref, amt_ref, gu_ref, ga_ref, mh, cu, cn, ads_ref, users_ref, u1_ref, um1_ref,
+    u_ref, at_ref, amt_ref, um_ref, gu_ref, ga_ref, mh, cu, cn, ads_ref, users_ref, u1_ref, um1_ref,
 ):
     u1_ref[...], um1_ref[...] = adagrad(u_ref[...], um_ref[...], gu_ref[...])
     at1, amt1 = adagrad(at_ref[...], amt_ref[...], ga_ref[...])
@@ -375,7 +375,7 @@
     at, amt = move((at, amt), (1, False), (1, True), (1, False), (-3, True))
     gu, ga = call(gradient_kernel, (u, at, *prep_last), [table_u, table_a], name="round_last_gradients")
     ads_now, users_now = call(
-        last_end_kernel, (u, um, at, amt, gu, ga, *prep_last), [both_a, both_u], users_scratch, name="round_last_end",
+        last_end_kernel, (u, at, amt, um, gu, ga, *prep_last), [both_a, both_u], users_scratch, name="round_last_end",
     )
     (ads_now,) = move((ads_now,), (1, True), (-3, True), (-3, True), (-3, True))
     (users_now,) = move((users_now,), (4, False), stay, stay, stay)

time: 79.5 us -> 79.5 us (level)
  transfers between devices with their start and end apart: 13 -> 13, of which waited for: 10 -> 9; matrix products, arithmetic and copies ran while one was open for 0% -> 0% of each run, Pallas kernels for 17% -> 17%
where the time goes in v9:
time: 79.5 us; the launch traced here: 79.2 us
  waiting for transfers between devices  35.5 us (45%)
  Pallas kernels  24.5 us (31%)
  starting transfers between devices  18.1 us (23%)
  between operations  0.99 us (1%)
    ppermute x13, waiting for transfers between devices, move(): return tuple((lax.ppermute(x, AXES, route) for x in arrays))  35.5 us
    pallas_call x12, Pallas kernels, call(): pl.pallas_call(kernel, out_shape=outs, in_specs=[vmem] * split_at + [pl.B...  24.5 us
    ppermute x13, starting transfers between devices, move(): return tuple((lax.ppermute(x, AXES, route) for x in arrays))  18.1 us
  transfers between devices with their start and end apart: 13, of which 9 were waited for; matrix products, arithmetic and copies ran while one was open for 0% of the time, Pallas kernels for 17%

profile of v9, /device:TPU:192, one launch (start us, length us, event | category | flops | bytes accessed | tf_op | source)
XLA Modules:
  0.0 79.2 jit_solution(9836482615529606282)
XLA Ops:
  0.6 5.1 %round_first.1 = (f32[512,256]{1,0:T(8,128)S(1)}, f32[512,256]{1,0:T(8,128)S(1)}, f32[2,256,512]{2,1,0:T(8,128)S(1)}, bf16[512,512]{1,0:T(8,128)(2,1)S(1)}, bf16...) custom-call(s32[1,16,4,512]{3,2,1,0:T(4,128)} %pu_hbm.3, ...), custom_call_target="tpu_custom_call" | custom-call | flops 1 | bytes 1 | tf_op jit(solution)/shard_map/round_first/pallas_call | solution.py:261
  5.7 0.1 collective-permute-start.1
  5.8 0.5 collective-permute-start
  6.3 0.8 users_update.2
  7.1 0.7 counts_1.1
  7.8 0.6 collective-permute-done.1.near_ref
  8.4 3.2 %round_early.1 = (f32[2,256,512]{2,1,0:T(8,128)S(1)}, f32[2,512,256]{2,1,0:T(8,128)S(1)}) custom-call(f32[512,256]{1,0:T(8,128)S(1)} %get-tuple-element.56.u_ref, f32[512,256]{1,0:T(8,128)S(1)} %get-tuple-element.57.after_ref.um_ref, f32[2,256,512]{2,1,0:T(8,128)S(1)} %collective-permute-done.1.near_ref, bf16[2,512,512]{2,1,0:T(8,128)(2,1)S(1)} %get-tuple-element.62.mh, ...), custom_call_target="tpu_custom_call" | custom-call | flops 1 | bytes 1 | tf_op jit(solution)/shard_map/round_early/pallas_call | solution.py:261
  11.6 2.3 %collective-permute-start.4 = (f32[2,256,512]{2,1,0:T(8,128)S(1)}, f32[2,256,512]{2,1,0:T(8,128)S(1)}, u32[]{:S(2)}, u32[]{:S(2)}) collective-permute-start(f32[2,256,512]{2,1,0:T(8,128)S(1)} %get-tuple-element.75), channel_id=1, source_target_pairs={{0,16},{1,17},{2,18},{3,19},{4,20},{5,21},{6,22},{7,23},{8,24},{9,... | collective-permute-start | bytes 3145736 | tf_op jit(solution)/shard_map/ppermute | solution.py:307
  14.0 0.7 collective-permute-start.3
  14.7 4.8 %collective-permute-start.2 = (s32[8,512]{1,0:T(8,128)S(1)}, s32[8,512]{1,0:T(8,128)S(1)}, u32[]{:S(2)}, u32[]{:S(2)}) collective-permute-start(s32[8,512]{1,0:T(8,128)S(1)} %get-tuple-element.66), channel_id=1, source_target_pairs={{0,192},{1,193},{2,194},{3,195},{4,196},{5,197},{6,198},{7,199},{8... | collective-permute-start | bytes 49160 | tf_op jit(solution)/shard_map/ppermute | solution.py:307
  19.6 1.2 %collective-permute-done.2.lists_ref = s32[8,512]{1,0:T(8,128)S(1)} collective-permute-done((s32[8,512]{1,0:T(8,128)S(1)}, s32[8,512]{1,0:T(8,128)S(1)}, u32[]{:S(2)}, u32[]{:S(2)}) %collective-permute-start.2) | collective-permute-done | bytes 16416 | tf_op jit(solution)/shard_map/ppermute | solution.py:307
  20.8 3.1 %collective-permute-done.far_ref = f32[2,256,512]{2,1,0:T(8,128)S(1)} collective-permute-done((f32[2,256,512]{2,1,0:T(8,128)S(1)}, f32[2,256,512]{2,1,0:T(8,128)S(1)}, u32[]{:S(2)}, u32[]{:S(2)}) %collective-permute-start) | collective-permute-done | bytes 1048608 | tf_op jit(solution)/shard_map/ppermute | solution.py:307
  23.9 3.0 %round_late.1 = (f32[512,256]{1,0:T(8,128)S(1)}, f32[512,256]{1,0:T(8,128)S(1)}, f32[256,512]{1,0:T(8,128)S(1)}, f32[256,512]{1,0:T(8,128)S(1)}, bf16[512,512]{1...) custom-call(f32[512,256]{1,0:T(8,128)S(1)} %get-tuple-element.56.u_re, ...), custom_call_target="tpu_custom_call" | custom-call | flops 1 | bytes 1 | tf_op jit(solution)/shard_map/round_late/pallas_call | solution.py:261
  26.8 0.1 collective-permute-start.5
  26.9 0.5 collective-permute-start.6
  27.4 0.8 users_update.3
  28.2 2.1 %counts_23.1 = (bf16[2,512,512]{2,1,0:T(8,128)(2,1)S(1)}, f32[2,512,128]{2,1,0:T(8,128)S(1)}, f32[2,8,512]{2,1,0:T(8,128)S(1)}, bf16[2,512,512]{2,1,0:T(8,128)(2...) custom-call(f32[512,256]{1,0:T(8,128)S(1)} %get-tuple-element.74.after_ref.ume_ref, ...), custom_call_target="tpu_custom_call" | custom-call | flops 1 | bytes 1 | tf_op jit(solution)/shard_map/counts_23/pallas_call | solution.py:261
  30.4 0.0 collective-permute-done.5.ato_ref
  30.4 0.0 collective-permute-done.6.amto_ref
  30.4 5.3 %collective-permute-done.4.ads_ref = f32[2,256,512]{2,1,0:T(8,128)S(1)} collective-permute-done((f32[2,256,512]{2,1,0:T(8,128)S(1)}, f32[2,256,512]{2,1,0:T(8,128)S(1)}, u32[]{:S(2)}, u32[]{:S(2)}) %collective-permute-start.4) | collective-permute-done | bytes 1048608 | tf_op jit(solution)/shard_map/ppermute | solution.py:307
  35.7 0.0 collective-permute-done.3.users_ref
  35.7 3.3 %round_pick.1 = (f32[512,256]{1,0:T(8,128)S(1)}, f32[512,256]{1,0:T(8,128)S(1)}, f32[256,512]{1,0:T(8,128)S(1)}, f32[256,512]{1,0:T(8,128)S(1)}) custom-call(f32[512,256]{1,0:T(8,128)S(1)} %get-tuple-element.73.ue_ref, f32[512,256]{1,0:T(8,128)S(1)} %get-tuple-element.74.after_ref.ume_ref, f32[2,512,256]{2,1,0:T(8,128)S(1)} %collective-permute-done.3.users_ref, ...), custom_call_target="tpu_custom_call" | custom-call | flops 1 | bytes 1 | tf_op jit(solution)/shard_map/round_pick/pallas_call | solution.py:261
  39.0 3.5 %collective-permute-start.7 = (f32[512,256]{1,0:T(8,128)S(1)}, f32[512,256]{1,0:T(8,128)S(1)}, u32[]{:S(2)}, u32[]{:S(2)}) collective-permute-start(f32[512,256]{1,0:T(8,128)S(1)} %get-tuple-element.81), channel_id=1, source_target_pairs={{0,192},{1,193},{2,194},{3,195},{4,196},{5,197},{6,198},{7,199},{8... | collective-permute-start | bytes 1572872 | tf_op jit(solution)/shard_map/ppermute | solution.py:307
  42.5 0.1 collective-permute-start.8
  42.6 0.1 collective-permute-start.9
  42.6 3.0 %collective-permute-start.10 = (f32[512,256]{1,0:T(8,128)S(1)}, f32[512,256]{1,0:T(8,128)S(1)}, u32[]{:S(2)}, u32[]{:S(2)}) collective-permute-start(f32[512,256]{1,0:T(8,128)S(1)} %get-tuple-element.84), channel_id=1, source_target_pairs={{0,192},{1,193},{2,194},{3,195},{4,196},{5,197},{6,198},{7,199},{8... | collective-permute-start | bytes 1572872 | tf_op jit(solution)/shard_map/ppermute | solution.py:307
  45.6 4.4 %collective-permute-done.7.u_ref = f32[512,256]{1,0:T(8,128)S(1)} collective-permute-done((f32[512,256]{1,0:T(8,128)S(1)}, f32[512,256]{1,0:T(8,128)S(1)}, u32[]{:S(2)}, u32[]{:S(2)}) %collective-permute-start.7) | collective-permute-done | bytes 524320 | tf_op jit(solution)/shard_map/ppermute | solution.py:307
  50.1 2.3 %collective-permute-done.8.at_ref = f32[256,512]{1,0:T(8,128)S(1)} collective-permute-done((f32[256,512]{1,0:T(8,128)S(1)}, f32[256,512]{1,0:T(8,128)S(1)}, u32[]{:S(2)}, u32[]{:S(2)}) %collective-permute-start.8) | collective-permute-done | bytes 524320 | tf_op jit(solution)/shard_map/ppermute | solution.py:307
  52.4 1.5 %round_last_gradients.1 = (f32[512,256]{1,0:T(8,128)S(1)}, f32[256,512]{1,0:T(8,128)S(1)}) custom-call(f32[512,256]{1,0:T(8,128)S(1)} %collective-permute-done.7.u_ref, f32[256,512]{1,0:T(8,128)S(1)} %collective-permute-done.8.at_ref, bf16[2,512,512]{2,1,0:T(8,128)(2,1)S(1)} %get-tuple-element.85.mh, f32[2,512,128]{2,1,0:T(8,128)S(1)} %get-tuple-element.86.cu, ...), custom_call_target="tpu_custom_call" | custom-call | flops 1 | bytes 1 | tf_op jit(solution)/shard_map/round_last_gradients/pallas_call | solution.py:261
  53.9 4.1 %collective-permute-done.9.amt_ref = f32[256,512]{1,0:T(8,128)S(1)} collective-permute-done((f32[256,512]{1,0:T(8,128)S(1)}, f32[256,512]{1,0:T(8,128)S(1)}, u32[]{:S(2)}, u32[]{:S(2)}) %collective-permute-start.9) | collective-permute-done | bytes 524320 | tf_op jit(solution)/shard_map/ppermute | solution.py:307
  58.0 0.0 collective-permute-done.10.um_ref
  58.0 2.0 %round_last_end.1 = (f32[2,256,512]{2,1,0:T(8,128)S(1)}, f32[2,512,256]{2,1,0:T(8,128)S(1)}) custom-call(f32[512,256]{1,0:T(8,128)S(1)} %collective-permute-done.7.u_ref, f32[256,512]{1,0:T(8,128)S(1)} %collective-permute-done.8.at_ref, f32[256,512]{1,0:T(8,128)S(1)} %collective-permute-done.9.amt_ref, f32[512,256]{1,0:T(8,128)S(1)} %collective-permute-done.10.um_ref, ...), custom_call_target="tpu_custom_call" | custom-call | flops 1 | bytes 1 | tf_op jit(solution)/shard_map/round_last_end/pallas_call | solution.py:261
  60.0 0.1 collective-permute-start.12
  60.1 2.4 %collective-permute-start.11 = (f32[2,512,256]{2,1,0:T(8,128)S(1)}, f32[2,512,256]{2,1,0:T(8,128)S(1)}, u32[]{:S(2)}, u32[]{:S(2)}) collective-permute-start(f32[2,512,256]{2,1,0:T(8,128)S(1)} %get-tuple-element.90), channel_id=1, source_target_pairs={{0,64},{1,65},{2,66},{3,67},{4,68},{5,69},{6,70},{7,71},{8,72},{9,... | collective-permute-start | bytes 3145736 | tf_op jit(solution)/shard_map/ppermute | solution.py:307
  62.4 13.0 %collective-permute-done.12.ads_ref = f32[2,256,512]{2,1,0:T(8,128)S(1)} collective-permute-done((f32[2,256,512]{2,1,0:T(8,128)S(1)}, f32[2,256,512]{2,1,0:T(8,128)S(1)}, u32[]{:S(2)}, u32[]{:S(2)}) %collective-permute-start.12) | collective-permute-done | bytes 1048608 | tf_op jit(solution)/shard_map/ppermute | solution.py:307
  75.5 1.1 %ads_out.1 = (f32[512,256]{1,0:T(8,128)}, f32[512,256]{1,0:T(8,128)}) custom-call(f32[2,256,512]{2,1,0:T(8,128)S(1)} %collective-permute-done.12.ads_ref), custom_call_target="tpu_custom_call" | custom-call | flops 1 | bytes 1 | tf_op jit(solution)/shard_map/ads_out/pallas_call | solution.py:261
  76.6 1.3 %collective-permute-done.11.users_ref = f32[2,512,256]{2,1,0:T(8,128)S(1)} collective-permute-done((f32[2,512,256]{2,1,0:T(8,128)S(1)}, f32[2,512,256]{2,1,0:T(8,128)S(1)}, u32[]{:S(2)}, u32[]{:S(2)}) %collective-permute-start.11) | collective-permute-done | bytes 1048608 | tf_op jit(solution)/shard_map/ppermute | solution.py:307
  78.0 1.0 %users_out.1 = (f32[512,256]{1,0:T(8,128)}, f32[512,256]{1,0:T(8,128)}) custom-call(f32[2,512,256]{2,1,0:T(8,128)S(1)} %collective-permute-done.11.users_ref, f32[512,256]{1,0:T(8,128)} %get-tuple-element.49.after_hbm), custom_call_target="tpu_custom_call" | custom-call | flops 1 | bytes 1 | tf_op jit(solution)/shard_map/users_out/pallas_call | solution.py:261
Async XLA Ops:
  5.7 2.7 %collective-permute-start.1 = (f32[2,256,512]{2,1,0:T(8,128)S(1)}, f32[2,256,512]{2,1,0:T(8,128)S(1)}, u32[]{:S(2)}, u32[]{:S(2)}) collective-permute-start(f32[2,256,512]{2,1,0:T(8,128)S(1)} %get-tuple-element.58), channel_id=1, source_target_pairs={{0,16},{1,17},{2,18},{3,19},{4,20},{5,21},{6,22},{7,23},{8,24},{9,... | collective-permute-start | bytes 3145736 | tf_op jit(solution)/shard_map/ppermute | solution.py:307
  5.8 18.1 %collective-permute-start = (f32[2,256,512]{2,1,0:T(8,128)S(1)}, f32[2,256,512]{2,1,0:T(8,128)S(1)}, u32[]{:S(2)}, u32[]{:S(2)}) collective-permute-start(f32[2,256,512]{2,1,0:T(8,128)S(1)} %get-tuple-element.58), channel_id=1, source_target_pairs={{0,16},{1,17},{2,18},{3,19},{4,20},{5,21},{6,22},{7,23},{8,24},{9,... | collective-permute-start | bytes 3145736 | tf_op jit(solution)/shard_map/ppermute | solution.py:307
  11.6 24.1 %collective-permute-start.4 = (f32[2,256,512]{2,1,0:T(8,128)S(1)}, f32[2,256,512]{2,1,0:T(8,128)S(1)}, u32[]{:S(2)}, u32[]{:S(2)}) collective-permute-start(f32[2,256,512]{2,1,0:T(8,128)S(1)} %get-tuple-element.75), channel_id=1, source_target_pairs={{0,16},{1,17},{2,18},{3,19},{4,20},{5,21},{6,22},{7,23},{8,24},{9,... | collective-permute-start | bytes 3145736 | tf_op jit(solution)/shard_map/ppermute | solution.py:307
  14.0 21.7 %collective-permute-start.3 = (f32[2,512,256]{2,1,0:T(8,128)S(1)}, f32[2,512,256]{2,1,0:T(8,128)S(1)}, u32[]{:S(2)}, u32[]{:S(2)}) collective-permute-start(f32[2,512,256]{2,1,0:T(8,128)S(1)} %get-tuple-element.65.after_ref), channel_id=1, source_target_pairs={{0,0},{1,1},{2,2},{3,3},{4,4},{5,5},{6,6},{7,7},{8,8},{9,9},{10,10... | collective-permute-start | bytes 3145736 | tf_op jit(solution)/shard_map/ppermute | solution.py:307
  14.7 6.1 %collective-permute-start.2 = (s32[8,512]{1,0:T(8,128)S(1)}, s32[8,512]{1,0:T(8,128)S(1)}, u32[]{:S(2)}, u32[]{:S(2)}) collective-permute-start(s32[8,512]{1,0:T(8,128)S(1)} %get-tuple-element.66), channel_id=1, source_target_pairs={{0,192},{1,193},{2,194},{3,195},{4,196},{5,197},{6,198},{7,199},{8... | collective-permute-start | bytes 49160 | tf_op jit(solution)/shard_map/ppermute | solution.py:307
  26.8 3.5 %collective-permute-start.5 = (f32[256,512]{1,0:T(8,128)S(1)}, f32[256,512]{1,0:T(8,128)S(1)}, u32[]{:S(2)}, u32[]{:S(2)}) collective-permute-start(f32[256,512]{1,0:T(8,128)S(1)} %get-tuple-element.76), channel_id=1, source_target_pairs={{0,16},{1,17},{2,18},{3,19},{4,20},{5,21},{6,22},{7,23},{8,24},{9,... | collective-permute-start | bytes 1572872 | tf_op jit(solution)/shard_map/ppermute | solution.py:307
  26.9 3.5 %collective-permute-start.6 = (f32[256,512]{1,0:T(8,128)S(1)}, f32[256,512]{1,0:T(8,128)S(1)}, u32[]{:S(2)}, u32[]{:S(2)}) collective-permute-start(f32[256,512]{1,0:T(8,128)S(1)} %get-tuple-element.77), channel_id=1, source_target_pairs={{0,16},{1,17},{2,18},{3,19},{4,20},{5,21},{6,22},{7,23},{8,24},{9,... | collective-permute-start | bytes 1572872 | tf_op jit(solution)/shard_map/ppermute | solution.py:307
  39.0 11.1 %collective-permute-start.7 = (f32[512,256]{1,0:T(8,128)S(1)}, f32[512,256]{1,0:T(8,128)S(1)}, u32[]{:S(2)}, u32[]{:S(2)}) collective-permute-start(f32[512,256]{1,0:T(8,128)S(1)} %get-tuple-element.81), channel_id=1, source_target_pairs={{0,192},{1,193},{2,194},{3,195},{4,196},{5,197},{6,198},{7,199},{8... | collective-permute-start | bytes 1572872 | tf_op jit(solution)/shard_map/ppermute | solution.py:307
  42.5 9.9 %collective-permute-start.8 = (f32[256,512]{1,0:T(8,128)S(1)}, f32[256,512]{1,0:T(8,128)S(1)}, u32[]{:S(2)}, u32[]{:S(2)}) collective-permute-start(f32[256,512]{1,0:T(8,128)S(1)} %get-tuple-element.82), channel_id=1, source_target_pairs={{0,16},{1,17},{2,18},{3,19},{4,20},{5,21},{6,22},{7,23},{8,24},{9,... | collective-permute-start | bytes 1572872 | tf_op jit(solution)/shard_map/ppermute | solution.py:307
  42.6 15.4 %collective-permute-start.9 = (f32[256,512]{1,0:T(8,128)S(1)}, f32[256,512]{1,0:T(8,128)S(1)}, u32[]{:S(2)}, u32[]{:S(2)}) collective-permute-start(f32[256,512]{1,0:T(8,128)S(1)} %get-tuple-element.83), channel_id=1, source_target_pairs={{0,16},{1,17},{2,18},{3,19},{4,20},{5,21},{6,22},{7,23},{8,24},{9,... | collective-permute-start | bytes 1572872 | tf_op jit(solution)/shard_map/ppermute | solution.py:307
  42.6 15.3 %collective-permute-start.10 = (f32[512,256]{1,0:T(8,128)S(1)}, f32[512,256]{1,0:T(8,128)S(1)}, u32[]{:S(2)}, u32[]{:S(2)}) collective-permute-start(f32[512,256]{1,0:T(8,128)S(1)} %get-tuple-element.84), channel_id=1, source_target_pairs={{0,192},{1,193},{2,194},{3,195},{4,196},{5,197},{6,198},{7,199},{8... | collective-permute-start | bytes 1572872 | tf_op jit(solution)/shard_map/ppermute | solution.py:307
  60.0 15.5 %collective-permute-start.12 = (f32[2,256,512]{2,1,0:T(8,128)S(1)}, f32[2,256,512]{2,1,0:T(8,128)S(1)}, u32[]{:S(2)}, u32[]{:S(2)}) collective-permute-start(f32[2,256,512]{2,1,0:T(8,128)S(1)} %get-tuple-element.91), channel_id=1, source_target_pairs={{0,24},{1,25},{2,26},{3,27},{4,28},{5,29},{6,30},{7,31},{8,16},{9,... | collective-permute-start | bytes 3145736 | tf_op jit(solution)/shard_map/ppermute | solution.py:307
  60.1 17.9 %collective-permute-start.11 = (f32[2,512,256]{2,1,0:T(8,128)S(1)}, f32[2,512,256]{2,1,0:T(8,128)S(1)}, u32[]{:S(2)}, u32[]{:S(2)}) collective-permute-start(f32[2,512,256]{2,1,0:T(8,128)S(1)} %get-tuple-element.90), channel_id=1, source_target_pairs={{0,64},{1,65},{2,66},{3,67},{4,68},{5,69},{6,70},{7,71},{8,72},{9,... | collective-permute-start | bytes 3145736 | tf_op jit(solution)/shard_map/ppermute | solution.py:307

commit v10 on v9

--- a/solution.py
+++ b/solution.py
@@ -216,11 +216,11 @@
 
 
 def last_end_kernel(
-    u_ref, at_ref, amt_ref, um_ref, gu_ref, ga_ref, mh, cu, cn, ads_ref, users_ref, u1_ref, um1_ref,
+    u_ref, um_ref, at_ref, amt_ref, gu_ref, ga_ref, mh, cu, cn, ads_ref, uo_ref, umo_ref, u1_ref, um1_ref,
 ):
     u1_ref[...], um1_ref[...] = adagrad(u_ref[...], um_ref[...], gu_ref[...])
     at1, amt1 = adagrad(at_ref[...], amt_ref[...], ga_ref[...])
-    put = update_users(reader(u1_ref), reader(um1_ref), users_ref.at[0], users_ref.at[1])
+    put = update_users(reader(u1_ref), reader(um1_ref), uo_ref, umo_ref)
     ga = group_pass(1, reader(u1_ref), u1_ref.shape[0], split(at1), (mh, cu, cn), put)
     ads_ref[0], ads_ref[1] = adagrad(at1, amt1, ga)
 
@@ -270,15 +270,13 @@
     )(*ins[:split_at], *far)
 
 
-def users_out_kernel(users_ref, after_hbm, u_hbm, um_hbm, sems):
-    size = users_ref.shape[1] // PARTS_OUT
+def users_out_kernel(u_ref, after_hbm, u_hbm, sems):
+    size = u_ref.shape[0] // PARTS_OUT
     copies = []
-    for t, out_hbm in enumerate((u_hbm, um_hbm)):
-        for k in range(PARTS_OUT):
-            rows = pl.ds(k * size, size)
-            copies.append(pltpu.make_async_copy(users_ref.at[t, rows, :], out_hbm.at[rows, :], sems.at[t * PARTS_OUT + k]))
-    for c in copies:
-        c.start()
+    for k in range(PARTS_OUT):
+        rows = pl.ds(k * size, size)
+        copies.append(pltpu.make_async_copy(u_ref.at[rows, :], u_hbm.at[rows, :], sems.at[k]))
+        copies[-1].start()
     for c in copies:
         c.wait()
 
@@ -374,19 +372,24 @@
     u, um = move((u, um), (-4, False), away, stay, away)
     at, amt = move((at, amt), (1, False), (1, True), (1, False), (-3, True))
     gu, ga = call(gradient_kernel, (u, at, *prep_last), [table_u, table_a], name="round_last_gradients")
-    ads_now, users_now = call(
-        last_end_kernel, (u, at, amt, um, gu, ga, *prep_last), [both_a, both_u], users_scratch, name="round_last_end",
+    ads_now, u, um = call(
+        last_end_kernel, (u, um, at, amt, gu, ga, *prep_last), [both_a, table_u, table_u], users_scratch, name="round_last_end",
     )
     (ads_now,) = move((ads_now,), (1, True), (-3, True), (-3, True), (-3, True))
-    (users_now,) = move((users_now,), (4, False), stay, stay, stay)
+    u, um = move((u, um), (4, False), stay, stay, stay)
     out_sems = pltpu.SemaphoreType.DMA((2 * PARTS_OUT,))
     a, am = call(
         ads_out_kernel, (ads_now,), [pltpu.HBM((na, d), F32)] * 2, [pltpu.VMEM((2, na, d), F32), out_sems],
         name="ads_out", out_place=pltpu.HBM,
     )
-    u, um = call(
-        users_out_kernel, (users_now, am), [pltpu.HBM((nu, d), F32)] * 2, [out_sems], hbm=1, name="users_out", out_place=pltpu.HBM,
-    )
+    def users_out(x, after):
+        return call(
+            users_out_kernel, (x, after), [pltpu.HBM((nu, d), F32)], [pltpu.SemaphoreType.DMA((PARTS_OUT,))], hbm=1,
+            name="users_out", out_place=pltpu.HBM,
+        )[0]
+
+    u = users_out(u, am)
+    um = users_out(um, u)
     return u, um, a, am
 
 

time: 79.5 us -> 79.3 us (level)
  waiting for transfers between devices: 35.5 us -> 32.5 us
  starting transfers between devices: 18.1 us -> 20.3 us
    ppermute x13 -> x14, waiting for transfers between devices: 35.5 us -> 32.5 us  [move(): return tuple((lax.ppermute(x, AXES, route) for x in arrays))]
    ppermute x13 -> x14, starting transfers between devices: 18.1 us -> 20.3 us  [move(): return tuple((lax.ppermute(x, AXES, route) for x in arrays))]
    pallas_call x12 -> x13, Pallas kernels: 24.5 us -> 25.2 us  [call(): pl.pallas_call(kernel, out_shape=outs, in_specs=[vmem] * split_at + [pl.B...]
  transfers between devices with their start and end apart: 13 -> 14, of which waited for: 9 -> 10; matrix products, arithmetic and copies ran while one was open for 0% -> 0% of each run, Pallas kernels for 17% -> 18%
where the time goes in v10:
time: 79.3 us; the launch traced here: 79 us
  waiting for transfers between devices  32.5 us (41%)
  Pallas kernels  25.2 us (32%)
  starting transfers between devices  20.3 us (26%)
  between operations  1.01 us (1%)
    ppermute x14, waiting for transfers between devices, move(): return tuple((lax.ppermute(x, AXES, route) for x in arrays))  32.5 us
    pallas_call x13, Pallas kernels, call(): pl.pallas_call(kernel, out_shape=outs, in_specs=[vmem] * split_at + [pl.B...  25.2 us
    ppermute x14, starting transfers between devices, move(): return tuple((lax.ppermute(x, AXES, route) for x in arrays))  20.3 us
  transfers between devices with their start and end apart: 14, of which 10 were waited for; matrix products, arithmetic and copies ran while one was open for 0% of the time, Pallas kernels for 18%

profile of v10, /device:TPU:192, one launch (start us, length us, event | category | flops | bytes accessed | tf_op | source)
XLA Modules:
  0.0 79.0 jit_solution(11966117721324017464)
XLA Ops:
  0.6 5.1 %round_first.1 = (f32[512,256]{1,0:T(8,128)S(1)}, f32[512,256]{1,0:T(8,128)S(1)}, f32[2,256,512]{2,1,0:T(8,128)S(1)}, bf16[512,512]{1,0:T(8,128)(2,1)S(1)}, bf16...) custom-call(s32[1,16,4,512]{3,2,1,0:T(4,128)} %pu_hbm.3, ...), custom_call_target="tpu_custom_call" | custom-call | flops 1 | bytes 1 | tf_op jit(solution)/shard_map/round_first/pallas_call | solution.py:261
  5.7 0.1 collective-permute-start.1
  5.8 0.5 collective-permute-start
  6.3 0.8 users_update.2
  7.1 0.7 counts_1.1
  7.8 0.6 collective-permute-done.1.near_ref
  8.4 3.2 %round_early.1 = (f32[2,256,512]{2,1,0:T(8,128)S(1)}, f32[2,512,256]{2,1,0:T(8,128)S(1)}) custom-call(f32[512,256]{1,0:T(8,128)S(1)} %get-tuple-element.55.u_ref, f32[512,256]{1,0:T(8,128)S(1)} %get-tuple-element.56.after_ref.um_ref, f32[2,256,512]{2,1,0:T(8,128)S(1)} %collective-permute-done.1.near_ref, bf16[2,512,512]{2,1,0:T(8,128)(2,1)S(1)} %get-tuple-element.61.mh, ...), custom_call_target="tpu_custom_call" | custom-call | flops 1 | bytes 1 | tf_op jit(solution)/shard_map/round_early/pallas_call | solution.py:261
  11.6 2.3 %collective-permute-start.4 = (f32[2,256,512]{2,1,0:T(8,128)S(1)}, f32[2,256,512]{2,1,0:T(8,128)S(1)}, u32[]{:S(2)}, u32[]{:S(2)}) collective-permute-start(f32[2,256,512]{2,1,0:T(8,128)S(1)} %get-tuple-element.74), channel_id=1, source_target_pairs={{0,16},{1,17},{2,18},{3,19},{4,20},{5,21},{6,22},{7,23},{8,24},{9,... | collective-permute-start | bytes 3145736 | tf_op jit(solution)/shard_map/ppermute | solution.py:305
  14.0 0.7 collective-permute-start.3
  14.7 4.8 %collective-permute-start.2 = (s32[8,512]{1,0:T(8,128)S(1)}, s32[8,512]{1,0:T(8,128)S(1)}, u32[]{:S(2)}, u32[]{:S(2)}) collective-permute-start(s32[8,512]{1,0:T(8,128)S(1)} %get-tuple-element.65), channel_id=1, source_target_pairs={{0,192},{1,193},{2,194},{3,195},{4,196},{5,197},{6,198},{7,199},{8... | collective-permute-start | bytes 49160 | tf_op jit(solution)/shard_map/ppermute | solution.py:305
  19.6 1.2 %collective-permute-done.2.lists_ref = s32[8,512]{1,0:T(8,128)S(1)} collective-permute-done((s32[8,512]{1,0:T(8,128)S(1)}, s32[8,512]{1,0:T(8,128)S(1)}, u32[]{:S(2)}, u32[]{:S(2)}) %collective-permute-start.2) | collective-permute-done | bytes 16416 | tf_op jit(solution)/shard_map/ppermute | solution.py:305
  20.8 3.1 %collective-permute-done.far_ref = f32[2,256,512]{2,1,0:T(8,128)S(1)} collective-permute-done((f32[2,256,512]{2,1,0:T(8,128)S(1)}, f32[2,256,512]{2,1,0:T(8,128)S(1)}, u32[]{:S(2)}, u32[]{:S(2)}) %collective-permute-start) | collective-permute-done | bytes 1048608 | tf_op jit(solution)/shard_map/ppermute | solution.py:305
  23.9 3.0 %round_late.1 = (f32[512,256]{1,0:T(8,128)S(1)}, f32[512,256]{1,0:T(8,128)S(1)}, f32[256,512]{1,0:T(8,128)S(1)}, f32[256,512]{1,0:T(8,128)S(1)}, bf16[512,512]{1...) custom-call(f32[512,256]{1,0:T(8,128)S(1)} %get-tuple-element.55.u_re, ...), custom_call_target="tpu_custom_call" | custom-call | flops 1 | bytes 1 | tf_op jit(solution)/shard_map/round_late/pallas_call | solution.py:261
  26.8 0.1 collective-permute-start.5
  26.9 0.5 collective-permute-start.6
  27.4 0.8 users_update.3
  28.2 2.1 %counts_23.1 = (bf16[2,512,512]{2,1,0:T(8,128)(2,1)S(1)}, f32[2,512,128]{2,1,0:T(8,128)S(1)}, f32[2,8,512]{2,1,0:T(8,128)S(1)}, bf16[2,512,512]{2,1,0:T(8,128)(2...) custom-call(f32[512,256]{1,0:T(8,128)S(1)} %get-tuple-element.73.after_ref.ume_ref, ...), custom_call_target="tpu_custom_call" | custom-call | flops 1 | bytes 1 | tf_op jit(solution)/shard_map/counts_23/pallas_call | solution.py:261
  30.4 0.0 collective-permute-done.5.ato_ref
  30.4 0.0 collective-permute-done.6.amto_ref
  30.4 5.3 %collective-permute-done.4.ads_ref = f32[2,256,512]{2,1,0:T(8,128)S(1)} collective-permute-done((f32[2,256,512]{2,1,0:T(8,128)S(1)}, f32[2,256,512]{2,1,0:T(8,128)S(1)}, u32[]{:S(2)}, u32[]{:S(2)}) %collective-permute-start.4) | collective-permute-done | bytes 1048608 | tf_op jit(solution)/shard_map/ppermute | solution.py:305
  35.7 0.0 collective-permute-done.3.users_ref
  35.7 3.3 %round_pick.1 = (f32[512,256]{1,0:T(8,128)S(1)}, f32[512,256]{1,0:T(8,128)S(1)}, f32[256,512]{1,0:T(8,128)S(1)}, f32[256,512]{1,0:T(8,128)S(1)}) custom-call(f32[512,256]{1,0:T(8,128)S(1)} %get-tuple-element.72.ue_ref, f32[512,256]{1,0:T(8,128)S(1)} %get-tuple-element.73.after_ref.ume_ref, f32[2,512,256]{2,1,0:T(8,128)S(1)} %collective-permute-done.3.users_ref, ...), custom_call_target="tpu_custom_call" | custom-call | flops 1 | bytes 1 | tf_op jit(solution)/shard_map/round_pick/pallas_call | solution.py:261
  39.0 3.5 %collective-permute-start.7 = (f32[512,256]{1,0:T(8,128)S(1)}, f32[512,256]{1,0:T(8,128)S(1)}, u32[]{:S(2)}, u32[]{:S(2)}) collective-permute-start(f32[512,256]{1,0:T(8,128)S(1)} %get-tuple-element.80), channel_id=1, source_target_pairs={{0,192},{1,193},{2,194},{3,195},{4,196},{5,197},{6,198},{7,199},{8... | collective-permute-start | bytes 1572872 | tf_op jit(solution)/shard_map/ppermute | solution.py:305
  42.5 0.1 collective-permute-start.9
  42.5 2.7 %collective-permute-start.8 = (f32[512,256]{1,0:T(8,128)S(1)}, f32[512,256]{1,0:T(8,128)S(1)}, u32[]{:S(2)}, u32[]{:S(2)}) collective-permute-start(f32[512,256]{1,0:T(8,128)S(1)} %get-tuple-element.81), channel_id=1, source_target_pairs={{0,192},{1,193},{2,194},{3,195},{4,196},{5,197},{6,198},{7,199},{8... | collective-permute-start | bytes 1572872 | tf_op jit(solution)/shard_map/ppermute | solution.py:305
  45.3 0.3 collective-permute-start.10
  45.6 4.5 %collective-permute-done.7.u_ref = f32[512,256]{1,0:T(8,128)S(1)} collective-permute-done((f32[512,256]{1,0:T(8,128)S(1)}, f32[512,256]{1,0:T(8,128)S(1)}, u32[]{:S(2)}, u32[]{:S(2)}) %collective-permute-start.7) | collective-permute-done | bytes 524320 | tf_op jit(solution)/shard_map/ppermute | solution.py:305
  50.1 2.3 %collective-permute-done.9.at_ref = f32[256,512]{1,0:T(8,128)S(1)} collective-permute-done((f32[256,512]{1,0:T(8,128)S(1)}, f32[256,512]{1,0:T(8,128)S(1)}, u32[]{:S(2)}, u32[]{:S(2)}) %collective-permute-start.9) | collective-permute-done | bytes 524320 | tf_op jit(solution)/shard_map/ppermute | solution.py:305
  52.4 1.5 %round_last_gradients.1 = (f32[512,256]{1,0:T(8,128)S(1)}, f32[256,512]{1,0:T(8,128)S(1)}) custom-call(f32[512,256]{1,0:T(8,128)S(1)} %collective-permute-done.7.u_ref, f32[256,512]{1,0:T(8,128)S(1)} %collective-permute-done.9.at_ref, bf16[2,512,512]{2,1,0:T(8,128)(2,1)S(1)} %get-tuple-element.84.mh, f32[2,512,128]{2,1,0:T(8,128)S(1)} %get-tuple-element.85.cu, ...), custom_call_target="tpu_custom_call" | custom-call | flops 1 | bytes 1 | tf_op jit(solution)/shard_map/round_last_gradients/pallas_call | solution.py:261
  53.9 1.8 %collective-permute-done.8.um_ref = f32[512,256]{1,0:T(8,128)S(1)} collective-permute-done((f32[512,256]{1,0:T(8,128)S(1)}, f32[512,256]{1,0:T(8,128)S(1)}, u32[]{:S(2)}, u32[]{:S(2)}) %collective-permute-start.8) | collective-permute-done | bytes 524320 | tf_op jit(solution)/shard_map/ppermute | solution.py:305
  55.7 2.3 %collective-permute-done.10.amt_ref = f32[256,512]{1,0:T(8,128)S(1)} collective-permute-done((f32[256,512]{1,0:T(8,128)S(1)}, f32[256,512]{1,0:T(8,128)S(1)}, u32[]{:S(2)}, u32[]{:S(2)}) %collective-permute-start.10) | collective-permute-done | bytes 524320 | tf_op jit(solution)/shard_map/ppermute | solution.py:305
  58.0 2.0 %round_last_end.1 = (f32[2,256,512]{2,1,0:T(8,128)S(1)}, f32[512,256]{1,0:T(8,128)S(1)}, f32[512,256]{1,0:T(8,128)S(1)}) custom-call(f32[512,256]{1,0:T(8,128)S(1)} %collective-permute-done.7.u_ref, f32[512,256]{1,0:T(8,128)S(1)} %collective-permute-done.8.um_ref, f32[256,512]{1,0:T(8,128)S(1)} %collective-permute-done.9.at_ref, ...), custom_call_target="tpu_custom_call" | custom-call | flops 1 | bytes 1 | tf_op jit(solution)/shard_map/round_last_end/pallas_call | solution.py:261
  60.0 0.1 collective-permute-start.12
  60.1 2.4 %collective-permute-start.11 = (f32[512,256]{1,0:T(8,128)S(1)}, f32[512,256]{1,0:T(8,128)S(1)}, u32[]{:S(2)}, u32[]{:S(2)}) collective-permute-start(f32[512,256]{1,0:T(8,128)S(1)} %get-tuple-element.89), channel_id=1, source_target_pairs={{0,64},{1,65},{2,66},{3,67},{4,68},{5,69},{6,70},{7,71},{8,72},{9,... | collective-permute-start | bytes 1572872 | tf_op jit(solution)/shard_map/ppermute | solution.py:305
  62.4 2.2 %collective-permute-start.13 = (f32[512,256]{1,0:T(8,128)S(1)}, f32[512,256]{1,0:T(8,128)S(1)}, u32[]{:S(2)}, u32[]{:S(2)}) collective-permute-start(f32[512,256]{1,0:T(8,128)S(1)} %get-tuple-element.92), channel_id=1, source_target_pairs={{0,64},{1,65},{2,66},{3,67},{4,68},{5,69},{6,70},{7,71},{8,72},{9,... | collective-permute-start | bytes 1572872 | tf_op jit(solution)/shard_map/ppermute | solution.py:305
  64.6 10.8 %collective-permute-done.12.ads_ref = f32[2,256,512]{2,1,0:T(8,128)S(1)} collective-permute-done((f32[2,256,512]{2,1,0:T(8,128)S(1)}, f32[2,256,512]{2,1,0:T(8,128)S(1)}, u32[]{:S(2)}, u32[]{:S(2)}) %collective-permute-start.12) | collective-permute-done | bytes 1048608 | tf_op jit(solution)/shard_map/ppermute | solution.py:305
  75.5 1.1 %ads_out.1 = (f32[512,256]{1,0:T(8,128)}, f32[512,256]{1,0:T(8,128)}) custom-call(f32[2,256,512]{2,1,0:T(8,128)S(1)} %collective-permute-done.12.ads_ref), custom_call_target="tpu_custom_call" | custom-call | flops 1 | bytes 1 | tf_op jit(solution)/shard_map/ads_out/pallas_call | solution.py:261
  76.6 0.0 collective-permute-done.11.u_ref
  76.6 0.8 %users_out.2.after_hbm = f32[512,256]{1,0:T(8,128)} custom-call(f32[512,256]{1,0:T(8,128)S(1)} %collective-permute-done.11.u_ref, f32[512,256]{1,0:T(8,128)} %get-tuple-element.48.after_hbm), custom_call_target="tpu_custom_call" | custom-call | flops 1 | bytes 1 | tf_op jit(solution)/shard_map/users_out/pallas_call | solution.py:261
  77.4 0.5 collective-permute-done.13.u_ref
  78.0 0.8 %users_out.3 = f32[512,256]{1,0:T(8,128)} custom-call(f32[512,256]{1,0:T(8,128)S(1)} %collective-permute-done.13.u_ref, f32[512,256]{1,0:T(8,128)} %users_out.2.after_hbm), custom_call_target="tpu_custom_call" | custom-call | flops 1 | bytes 1 | tf_op jit(solution)/shard_map/users_out/pallas_call | solution.py:261
Async XLA Ops:
  5.7 2.7 %collective-permute-start.1 = (f32[2,256,512]{2,1,0:T(8,128)S(1)}, f32[2,256,512]{2,1,0:T(8,128)S(1)}, u32[]{:S(2)}, u32[]{:S(2)}) collective-permute-start(f32[2,256,512]{2,1,0:T(8,128)S(1)} %get-tuple-element.57), channel_id=1, source_target_pairs={{0,16},{1,17},{2,18},{3,19},{4,20},{5,21},{6,22},{7,23},{8,24},{9,... | collective-permute-start | bytes 3145736 | tf_op jit(solution)/shard_map/ppermute | solution.py:305
  5.8 18.1 %collective-permute-start = (f32[2,256,512]{2,1,0:T(8,128)S(1)}, f32[2,256,512]{2,1,0:T(8,128)S(1)}, u32[]{:S(2)}, u32[]{:S(2)}) collective-permute-start(f32[2,256,512]{2,1,0:T(8,128)S(1)} %get-tuple-element.57), channel_id=1, source_target_pairs={{0,16},{1,17},{2,18},{3,19},{4,20},{5,21},{6,22},{7,23},{8,24},{9,... | collective-permute-start | bytes 3145736 | tf_op jit(solution)/shard_map/ppermute | solution.py:305
  11.6 24.1 %collective-permute-start.4 = (f32[2,256,512]{2,1,0:T(8,128)S(1)}, f32[2,256,512]{2,1,0:T(8,128)S(1)}, u32[]{:S(2)}, u32[]{:S(2)}) collective-permute-start(f32[2,256,512]{2,1,0:T(8,128)S(1)} %get-tuple-element.74), channel_id=1, source_target_pairs={{0,16},{1,17},{2,18},{3,19},{4,20},{5,21},{6,22},{7,23},{8,24},{9,... | collective-permute-start | bytes 3145736 | tf_op jit(solution)/shard_map/ppermute | solution.py:305
  14.0 21.7 %collective-permute-start.3 = (f32[2,512,256]{2,1,0:T(8,128)S(1)}, f32[2,512,256]{2,1,0:T(8,128)S(1)}, u32[]{:S(2)}, u32[]{:S(2)}) collective-permute-start(f32[2,512,256]{2,1,0:T(8,128)S(1)} %get-tuple-element.64.after_ref), channel_id=1, source_target_pairs={{0,0},{1,1},{2,2},{3,3},{4,4},{5,5},{6,6},{7,7},{8,8},{9,9},{10,10... | collective-permute-start | bytes 3145736 | tf_op jit(solution)/shard_map/ppermute | solution.py:305
  14.7 6.1 %collective-permute-start.2 = (s32[8,512]{1,0:T(8,128)S(1)}, s32[8,512]{1,0:T(8,128)S(1)}, u32[]{:S(2)}, u32[]{:S(2)}) collective-permute-start(s32[8,512]{1,0:T(8,128)S(1)} %get-tuple-element.65), channel_id=1, source_target_pairs={{0,192},{1,193},{2,194},{3,195},{4,196},{5,197},{6,198},{7,199},{8... | collective-permute-start | bytes 49160 | tf_op jit(solution)/shard_map/ppermute | solution.py:305
  26.8 3.5 %collective-permute-start.5 = (f32[256,512]{1,0:T(8,128)S(1)}, f32[256,512]{1,0:T(8,128)S(1)}, u32[]{:S(2)}, u32[]{:S(2)}) collective-permute-start(f32[256,512]{1,0:T(8,128)S(1)} %get-tuple-element.75), channel_id=1, source_target_pairs={{0,16},{1,17},{2,18},{3,19},{4,20},{5,21},{6,22},{7,23},{8,24},{9,... | collective-permute-start | bytes 1572872 | tf_op jit(solution)/shard_map/ppermute | solution.py:305
  26.9 3.4 %collective-permute-start.6 = (f32[256,512]{1,0:T(8,128)S(1)}, f32[256,512]{1,0:T(8,128)S(1)}, u32[]{:S(2)}, u32[]{:S(2)}) collective-permute-start(f32[256,512]{1,0:T(8,128)S(1)} %get-tuple-element.76), channel_id=1, source_target_pairs={{0,16},{1,17},{2,18},{3,19},{4,20},{5,21},{6,22},{7,23},{8,24},{9,... | collective-permute-start | bytes 1572872 | tf_op jit(solution)/shard_map/ppermute | solution.py:305
  39.0 11.1 %collective-permute-start.7 = (f32[512,256]{1,0:T(8,128)S(1)}, f32[512,256]{1,0:T(8,128)S(1)}, u32[]{:S(2)}, u32[]{:S(2)}) collective-permute-start(f32[512,256]{1,0:T(8,128)S(1)} %get-tuple-element.80), channel_id=1, source_target_pairs={{0,192},{1,193},{2,194},{3,195},{4,196},{5,197},{6,198},{7,199},{8... | collective-permute-start | bytes 1572872 | tf_op jit(solution)/shard_map/ppermute | solution.py:305
  42.5 9.9 %collective-permute-start.9 = (f32[256,512]{1,0:T(8,128)S(1)}, f32[256,512]{1,0:T(8,128)S(1)}, u32[]{:S(2)}, u32[]{:S(2)}) collective-permute-start(f32[256,512]{1,0:T(8,128)S(1)} %get-tuple-element.82), channel_id=1, source_target_pairs={{0,16},{1,17},{2,18},{3,19},{4,20},{5,21},{6,22},{7,23},{8,24},{9,... | collective-permute-start | bytes 1572872 | tf_op jit(solution)/shard_map/ppermute | solution.py:305
  42.5 13.1 %collective-permute-start.8 = (f32[512,256]{1,0:T(8,128)S(1)}, f32[512,256]{1,0:T(8,128)S(1)}, u32[]{:S(2)}, u32[]{:S(2)}) collective-permute-start(f32[512,256]{1,0:T(8,128)S(1)} %get-tuple-element.81), channel_id=1, source_target_pairs={{0,192},{1,193},{2,194},{3,195},{4,196},{5,197},{6,198},{7,199},{8... | collective-permute-start | bytes 1572872 | tf_op jit(solution)/shard_map/ppermute | solution.py:305
  45.3 12.7 %collective-permute-start.10 = (f32[256,512]{1,0:T(8,128)S(1)}, f32[256,512]{1,0:T(8,128)S(1)}, u32[]{:S(2)}, u32[]{:S(2)}) collective-permute-start(f32[256,512]{1,0:T(8,128)S(1)} %get-tuple-element.83), channel_id=1, source_target_pairs={{0,16},{1,17},{2,18},{3,19},{4,20},{5,21},{6,22},{7,23},{8,24},{9,... | collective-permute-start | bytes 1572872 | tf_op jit(solution)/shard_map/ppermute | solution.py:305
  60.0 15.5 %collective-permute-start.12 = (f32[2,256,512]{2,1,0:T(8,128)S(1)}, f32[2,256,512]{2,1,0:T(8,128)S(1)}, u32[]{:S(2)}, u32[]{:S(2)}) collective-permute-start(f32[2,256,512]{2,1,0:T(8,128)S(1)} %get-tuple-element.90), channel_id=1, source_target_pairs={{0,24},{1,25},{2,26},{3,27},{4,28},{5,29},{6,30},{7,31},{8,16},{9,... | collective-permute-start | bytes 3145736 | tf_op jit(solution)/shard_map/ppermute | solution.py:305
  60.1 16.6 %collective-permute-start.11 = (f32[512,256]{1,0:T(8,128)S(1)}, f32[512,256]{1,0:T(8,128)S(1)}, u32[]{:S(2)}, u32[]{:S(2)}) collective-permute-start(f32[512,256]{1,0:T(8,128)S(1)} %get-tuple-element.89), channel_id=1, source_target_pairs={{0,64},{1,65},{2,66},{3,67},{4,68},{5,69},{6,70},{7,71},{8,72},{9,... | collective-permute-start | bytes 1572872 | tf_op jit(solution)/shard_map/ppermute | solution.py:305
  62.4 15.5 %collective-permute-start.13 = (f32[512,256]{1,0:T(8,128)S(1)}, f32[512,256]{1,0:T(8,128)S(1)}, u32[]{:S(2)}, u32[]{:S(2)}) collective-permute-start(f32[512,256]{1,0:T(8,128)S(1)} %get-tuple-element.92), channel_id=1, source_target_pairs={{0,64},{1,65},{2,66},{3,67},{4,68},{5,69},{6,70},{7,71},{8,72},{9,... | collective-permute-start | bytes 1572872 | tf_op jit(solution)/shard_map/ppermute | solution.py:305
